TPU v7x, 256 devices: a whole 4x4x8 slice. The times are simulated.
256 devices in a mesh: dp: 8 (over z), expert: 32 (over x, y, core).
Axes of the slice: x: 4, y: 4, z: 8, core: 2. Of those that a mesh axis runs over, the one named last changes fastest.
Arguments:
- tokens: bfloat16 [32768, 2048], P(('dp', 'expert')), may hold values from -6 to 6
- grad_out: bfloat16 [32768, 2048], P(('dp', 'expert')), may hold values from -24 to 24
- gates: float32 [32768, 8], P(('dp', 'expert')), may hold values from 0.05 to 0.5
- expert_ids: int32 [32768, 8], P(('dp', 'expert')), may hold values from 0 to 31, all different within a row; in each aligned block of 128 rows (0 to 127, 128 to 255, ...) at most 36 rows name the same one
- w_gate: bfloat16 [32, 2048, 384], P('expert'), may hold values from -0.125 to 0.125
- w_up: bfloat16 [32, 2048, 384], P('expert'), may hold values from -0.125 to 0.125
- w_down: bfloat16 [32, 384, 2048], P('expert'), may hold values from -0.3125 to 0.3125
Outputs:
- grad_tokens: bfloat16 [32768, 2048], P(('dp', 'expert'))
- grad_gate: bfloat16 [32, 2048, 384], P('expert', 'dp')
- grad_up: bfloat16 [32, 2048, 384], P('expert', 'dp')
- grad_down: bfloat16 [32, 384, 2048], P('expert', 'dp')
Inputs may be any that keep to these rules, and one draw needn't show every extreme that they name: `expert_ids`: each row names 8 different experts. In the rows of one device no expert is named more than 36 times, a bound that some block reaches.
All inputs are finite; a program needn't handle non-finite values.
Results may differ from a plain program's by a relative error of at most 0.019.
Values may be sent and summed in bfloat16 or wider, within the bound.
No kernel may reach another device: no remote copies, remote signals or barrier semaphores. Data moves between devices by JAX's collectives and lax.ppermute only.
A program may use at most 128 MiB of HBM per device.

v0:
```python
import jax
import jax.numpy as jnp
from jax import lax
from jax.sharding import PartitionSpec as P


def shards(tokens, grad_out, gates, expert_ids, w_gate, w_up, w_down):
    tok_rows, width = tokens.shape
    top_count = expert_ids.shape[1]
    peers = lax.axis_size("expert")
    exp_local = w_gate.shape[0]
    experts_all = peers * exp_local
    most_rows = min(tok_rows, tok_rows * top_count * 9 // (8 * experts_all))
    flat_ids = expert_ids.reshape(-1)
    onehot = (flat_ids[:, None] == jnp.arange(experts_all, dtype=jnp.int32)[None, :]).astype(
        jnp.int32
    )
    position = jnp.sum((jnp.cumsum(onehot, axis=0) - onehot) * onehot, axis=1)
    slots = flat_ids * most_rows + position
    routed_rows = (
        (gates[:, :, None] * grad_out[:, None, :].astype(jnp.float32))
        .astype(jnp.bfloat16)
        .reshape(-1, width)
    )
    input_rows = jnp.repeat(tokens, top_count, axis=0)
    send_x = jnp.zeros((experts_all * most_rows, width), jnp.bfloat16).at[slots].set(input_rows)
    send_g = jnp.zeros((experts_all * most_rows, width), jnp.bfloat16).at[slots].set(routed_rows)
    send_x = send_x.reshape(peers, exp_local * most_rows, width)
    send_g = send_g.reshape(peers, exp_local * most_rows, width)
    recv_x, recv_g = (
        lax.all_to_all(send_x, "expert", split_axis=0, concat_axis=0, tiled=True),
        lax.all_to_all(send_g, "expert", split_axis=0, concat_axis=0, tiled=True),
    )
    rows_x = (
        recv_x.reshape(peers, exp_local, most_rows, width)
        .transpose(1, 0, 2, 3)
        .reshape(exp_local, peers * most_rows, width)
    )
    routed = (
        recv_g.reshape(peers, exp_local, most_rows, width)
        .transpose(1, 0, 2, 3)
        .reshape(exp_local, peers * most_rows, width)
    )
    pre_gate = jnp.einsum("erd,edf->erf", rows_x, w_gate, preferred_element_type=jnp.float32)
    pre_up = jnp.einsum("erd,edf->erf", rows_x, w_up, preferred_element_type=jnp.float32)
    sigma = jax.nn.sigmoid(pre_gate)
    silu_part = pre_gate * sigma
    act = (silu_part * pre_up).astype(jnp.bfloat16)
    d_act = jnp.einsum("erd,efd->erf", routed, w_down, preferred_element_type=jnp.float32)
    d_gate = (d_act * pre_up * sigma * (1.0 + pre_gate * (1.0 - sigma))).astype(jnp.bfloat16)
    d_up = (d_act * silu_part).astype(jnp.bfloat16)
    term_gate = jnp.einsum("erd,erf->def", rows_x, d_gate, preferred_element_type=jnp.float32)
    term_up = jnp.einsum("erd,erf->def", rows_x, d_up, preferred_element_type=jnp.float32)
    term_down = jnp.einsum("erf,erd->fed", act, routed, preferred_element_type=jnp.float32)
    sum_gate = lax.psum_scatter(
        term_gate.astype(jnp.bfloat16), "dp", scatter_dimension=0, tiled=True
    ).astype(jnp.float32)
    sum_up = lax.psum_scatter(
        term_up.astype(jnp.bfloat16), "dp", scatter_dimension=0, tiled=True
    ).astype(jnp.float32)
    sum_down = lax.psum_scatter(
        term_down.astype(jnp.bfloat16), "dp", scatter_dimension=0, tiled=True
    ).astype(jnp.float32)
    grad_g = sum_gate.transpose(1, 0, 2).astype(jnp.bfloat16)
    grad_u = sum_up.transpose(1, 0, 2).astype(jnp.bfloat16)
    grad_d = sum_down.transpose(1, 0, 2).astype(jnp.bfloat16)
    grad_g, grad_u, grad_d = (grad_g, grad_u, grad_d)
    summed = jnp.einsum("erf,edf->erd", d_gate, w_gate, preferred_element_type=jnp.float32)
    summed = summed + jnp.einsum("erf,edf->erd", d_up, w_up, preferred_element_type=jnp.float32)
    pair_grad = summed.astype(jnp.bfloat16)
    outgoing = (
        pair_grad.reshape(exp_local, peers, most_rows, width)
        .transpose(1, 0, 2, 3)
        .reshape(peers, exp_local * most_rows, width)
    )
    returned = lax.all_to_all(outgoing, "expert", split_axis=0, concat_axis=0, tiled=True)
    mine = returned.reshape(experts_all * most_rows, width)[slots]
    grad_tokens = jnp.sum(
        mine.reshape(tok_rows, top_count, width).astype(jnp.float32), axis=1
    ).astype(jnp.bfloat16)
    return (grad_tokens, grad_g, grad_u, grad_d)


def solution(mesh):
    in_specs = (
        P(("dp", "expert"), None),
        P(("dp", "expert"), None),
        P(("dp", "expert"), None),
        P(("dp", "expert"), None),
        P("expert", None, None),
        P("expert", None, None),
        P("expert", None, None),
    )
    out_specs = (
        P(("dp", "expert"), None),
        P("expert", "dp", None),
        P("expert", "dp", None),
        P("expert", "dp", None),
    )
    return jax.shard_map(shards, mesh=mesh, in_specs=in_specs, out_specs=out_specs, check_vma=False)
```

profile of v0, /device:TPU:1, one launch (start us, length us, event | category | flops | bytes accessed | tf_op | source)
XLA Modules:
  0.0 410.4 jit_solution(9929717262446031485)
XLA Ops:
  7.2 0.8 broadcast_multiply_fusion
  8.0 0.8 copy.33
  8.8 0.1 eq.29
  8.9 0.1 eq.25
  9.0 0.1 copy.32
  9.1 0.1 mul.67
  9.2 9.0 %reduce-window.6 = s32[32,8,128]{2,1,0:T(8,128)S(1)} reduce-window(s32[32,8,128]{2,1,0:T(8,128)S(1)} %fusion.28, s32[]{:T(128)} %constant.7.clone.1), window={size=1x1x128 pad=0_0x0_0x127_0}, to_apply=%region_0.0 | reduce-window | flops 4161536 | bytes 262148 | tf_op jit(solution)/shard_map/reduce-window
  18.2 0.1 slice.10
  18.3 0.1 copy.35
  18.5 0.1 copy.36
  18.5 0.1 broadcast_add_fusion
  18.7 9.8 %scatter_custom_fusion.1 = bf16[1152,2048]{1,0:T(8,128)(2,1)} fusion(s32[1024]{0:T(1024)S(1)} %bitcast.81, bf16[]{:T(256)} %constant.5.clone.1, bf16[128,2048]{1,0:T(8,128)(2,1)} %param.7), kind=kCustom, calls=%fused_computation.9 | custom fusion | bytes 5242882 | tf_op jit(solution)/shard_map/scatter | solution.py:26
  28.5 7.2 %reshape.187 = bf16[32,36,2048]{2,1,0:T(8,128)(2,1)} reshape(bf16[1152,2048]{1,0:T(8,128)(2,1)} %scatter_custom_fusion.1) | data formatting | bytes 9437184 | tf_op jit(solution)/shard_map/reshape | solution.py:28
  35.7 8.8 %all-to-all-start.1 = ((bf16[32,36,2048]{2,1,0:T(8,128)(2,1)}), bf16[32,36,2048]{2,1,0:T(8,128)(2,1)}, u32[]{:S(2)}, u32[]{:S(2)}) async-start(bf16[32,36,2048]{2,1,0:T(8,128)(2,1)} %reshape.187), calls=%async_computation.1 | async-start | bytes 10485760 | tf_op jit(solution)/shard_map/all_to_all | solution.py:31
  44.5 0.1 copy.37
  44.6 0.1 mul.69
  44.7 0.1 convert_element_type.101
  44.8 9.7 %scatter_custom_fusion = bf16[1152,2048]{1,0:T(8,128)(2,1)} fusion(s32[1024]{0:T(1024)S(1)} %bitcast.82, f32[128,2048]{1,0:T(8,128)S(1)} %convert_element_type.101, f32[1024]{0:T(1024)S(1)} %mul.69, bf16[]{:T(256)} %constant.5.clone.1), kind=kCustom, calls=%fused_computation.7 | custom fusion | flops 4194304 | bytes 5771266 | tf_op jit(solution)/shard_map/scatter | solution.py:27
  54.5 7.2 %reshape.183 = bf16[32,36,2048]{2,1,0:T(8,128)(2,1)} reshape(bf16[1152,2048]{1,0:T(8,128)(2,1)} %scatter_custom_fusion) | data formatting | bytes 9437184 | tf_op jit(solution)/shard_map/reshape | solution.py:29
  61.7 47.4 %all-to-all-done.1 = bf16[32,36,2048]{2,1,0:T(8,128)(2,1)} async-done(((bf16[32,36,2048]{2,1,0:T(8,128)(2,1)}), bf16[32,36,2048]{2,1,0:T(8,128)(2,1)}, u32[]{:S(2)}, u32[]{:S(2)}) %all-to-all-start.1) | async-done | bytes 4718624 | tf_op jit(solution)/shard_map/all_to_all | solution.py:31
  109.1 9.8 %all-to-all-start = ((bf16[32,36,2048]{2,1,0:T(8,128)(2,1)}), bf16[32,36,2048]{2,1,0:T(8,128)(2,1)}, u32[]{:S(2)}, u32[]{:S(2)}) async-start(bf16[32,36,2048]{2,1,0:T(8,128)(2,1)} %reshape.183), calls=%async_computation | async-start | bytes 10485760 | tf_op jit(solution)/shard_map/all_to_all | solution.py:32
  119.0 7.2 %reshape.188 = bf16[1152,2048]{1,0:T(8,128)(2,1)} reshape(bf16[32,36,2048]{2,1,0:T(8,128)(2,1)} %all-to-all-done.1) | data formatting | bytes 9437184 | tf_op jit(solution)/shard_map/reshape.6
  126.2 6.3 %fusion.17 = f32[1152,384]{1,0:T(8,128)} fusion(bf16[1152,2048]{1,0:T(8,128)(2,1)} %reshape.188, bf16[1,2048,384]{2,1,0:T(8,128)(2,1)S(1)} %copy-done), kind=kOutput, calls=%fused_computation.29 | convolution fusion | flops 1811939328 | bytes 8060928 | tf_op jit(solution)/shard_map/erd,edf->erf/dot_general | solution.py:44
  132.5 3.8 fusion.20
  136.4 47.1 %all-to-all-done = bf16[32,36,2048]{2,1,0:T(8,128)(2,1)} async-done(((bf16[32,36,2048]{2,1,0:T(8,128)(2,1)}), bf16[32,36,2048]{2,1,0:T(8,128)(2,1)}, u32[]{:S(2)}, u32[]{:S(2)}) %all-to-all-start) | async-done | bytes 4718624 | tf_op jit(solution)/shard_map/all_to_all | solution.py:32
  183.5 7.2 %reshape.184 = bf16[1152,2048]{1,0:T(8,128)(2,1)} reshape(bf16[32,36,2048]{2,1,0:T(8,128)(2,1)} %all-to-all-done) | data formatting | bytes 9437184 | tf_op jit(solution)/shard_map/reshape.3
  190.7 6.2 %fusion.10 = bf16[384,1,2048]{0,2,1:T(8,128)(2,1)S(1)} fusion(bf16[1152,2048]{1,0:T(8,128)(2,1)} %reshape.184, f32[1152,384]{1,0:T(8,128)} %fusion.20, f32[1152,384]{1,0:T(8,128)} %fusion.17), kind=kOutput, calls=%fused_computation.18 | convolution fusion | flops 1815379968 | bytes 9830400 | tf_op jit(solution)/shard_map/erf,erd->fed/dot_general | solution.py:54
  197.0 5.9 %copy.38 = bf16[384,1,2048]{2,1,0:T(2,128)(2,1)} copy(bf16[384,1,2048]{0,2,1:T(8,128)(2,1)S(1)} %fusion.10) | data formatting | bytes 3145728 | tf_op jit(solution)/shard_map/convert_element_type | solution.py:62
  202.9 0.3 reduce-scatter.3.cloned.1.call-start
  203.1 7.1 %multiply_convert_fusion.1 = (bf16[1152,384]{1,0:T(8,128)(2,1)S(1)}, bf16[1152,384]{1,0:T(8,128)(2,1)S(1)}) fusion(f32[1152,384]{1,0:T(8,128)} %fusion.17, f32[1152,384]{1,0:T(8,128)} %fusion.20, bf16[1152,2048]{1,0:T(8,128)(2,1)} %reshape.184, bf16[1,384,2048]{2,1,0:T(8,128)(2,1)} %param.13), kind=kOutput, calls=%fused_computation.23 | convolution fusion | flops 1817690112 | bytes 11599872 | tf_op jit(solution)/shard_map/erd,efd->erf/dot_general | solution.py:49
  210.2 5.7 %fusion.8 = bf16[2048,1,384]{0,2,1:T(8,128)(2,1)} fusion(bf16[1152,384]{1,0:T(8,128)(2,1)S(1)} %get-tuple-element.21, bf16[1152,2048]{1,0:T(8,128)(2,1)} %reshape.188), kind=kOutput, calls=%fused_computation.16 | convolution fusion | flops 1812725760 | bytes 7176192 | tf_op jit(solution)/shard_map/erd,erf->def/dot_general | solution.py:52
  216.0 2.6 fusion.15
  218.6 4.3 %fusion.1 = bf16[1152,2048]{1,0:T(8,128)(2,1)} fusion(f32[1152,2048]{1,0:T(8,128)S(1)} %fusion.15, bf16[1152,384]{1,0:T(8,128)(2,1)S(1)} %get-tuple-element.20, bf16[1,2048,384]{2,1,0:T(8,128)(2,1)S(1)} %copy-done.3), kind=kOutput, calls=%fused_computation.6 | convolution fusion | flops 1816657920 | bytes 16613376 | tf_op jit(solution)/shard_map/erf,edf->erd/dot_general | solution.py:69
  223.0 7.2 %reshape_transpose_reshape.2 = bf16[32,36,2048]{2,1,0:T(8,128)(2,1)} reshape(bf16[1152,2048]{1,0:T(8,128)(2,1)} %fusion.1) | data formatting | bytes 9437184 | tf_op jit(solution)/shard_map/reshape;transpose;reshape | solution.py:74
  230.2 8.3 %all-to-all-start.2 = ((bf16[32,36,2048]{2,1,0:T(8,128)(2,1)}), bf16[32,36,2048]{2,1,0:T(8,128)(2,1)}, u32[]{:S(2)}, u32[]{:S(2)}) async-start(bf16[32,36,2048]{2,1,0:T(8,128)(2,1)} %reshape_transpose_reshape.2), calls=%async_computation.2 | async-start | bytes 10485760 | tf_op jit(solution)/shard_map/all_to_all | solution.py:76
  238.4 0.3 reduce-scatter.5.cloned.1.call-start
  238.7 5.8 %fusion.9 = bf16[2048,1,384]{0,2,1:T(8,128)(2,1)} fusion(bf16[1152,384]{1,0:T(8,128)(2,1)S(1)} %get-tuple-element.20, bf16[1152,2048]{1,0:T(8,128)(2,1)} %reshape.188), kind=kOutput, calls=%fused_computation.17 | convolution fusion | flops 1812725760 | bytes 7176192 | tf_op jit(solution)/shard_map/erd,erf->def/dot_general | solution.py:53
  244.6 0.6 dynamic-slice
  245.8 51.5 %all-reduce.3.cloned.1.call-done = bf16[384,1,2048]{2,1,0:T(2,128)(2,1)} async-done(((bf16[384,1,2048]{2,1,0:T(2,128)(2,1)}), bf16[384,1,2048]{2,1,0:T(2,128)(2,1)}) %all-reduce.3.cloned.1.call-update) | async-done | bytes 1572880
  297.3 1.4 constant_dynamic-slice_fusion
  298.7 0.8 copy.45
  299.5 36.1 %reduce-scatter.3.cloned.1.call-done = bf16[256,1,384]{0,2,1:T(8,128)(2,1)} async-done(((bf16[2048,1,384]{0,2,1:T(8,128)(2,1)}), bf16[256,1,384]{0,2,1:T(8,128)(2,1)}) %reduce-scatter.3.cloned.1.call-update) | async-done | bytes 196624 | tf_op jit(solution)/shard_map/reduce_scatter | solution.py:55
  335.6 1.7 copy.39
  337.3 39.8 %reduce-scatter.5.cloned.1.call-done = bf16[256,1,384]{0,2,1:T(8,128)(2,1)} async-done(((bf16[2048,1,384]{0,2,1:T(8,128)(2,1)}), bf16[256,1,384]{0,2,1:T(8,128)(2,1)}) %reduce-scatter.5.cloned.1.call-update) | async-done | bytes 196624 | tf_op jit(solution)/shard_map/reduce_scatter | solution.py:58
  377.2 1.7 copy.40
  378.9 7.2 %reshape.191 = bf16[1152,2048]{1,0:T(8,128)(2,1)} reshape(bf16[32,36,2048]{2,1,0:T(8,128)(2,1)} %all-to-all-done.2) | data formatting | bytes 9437184 | tf_op jit(solution)/shard_map/reshape | solution.py:77
  386.2 11.8 %gather_fusion = bf16[1024,2048]{1,0:T(8,128)(2,1)} fusion(bf16[1152,2048]{1,0:T(8,128)(2,1)} %reshape.191, s32[1024]{0:T(1024)S(1)} %broadcast_clamp_fusion), kind=kCustom, calls=%fused_computation | custom fusion | bytes 8392704 | tf_op jit(solution)/shard_map/gather | solution.py:77
  398.0 5.9 %bitcast_reduce_fusion = bf16[128,2048]{1,0:T(8,128)(2,1)} fusion(bf16[1024,2048]{1,0:T(8,128)(2,1)} %gather_fusion), kind=kLoop, calls=%fused_computation.8 | loop fusion | flops 1835008 | bytes 4718592 | tf_op jit(solution)/shard_map/reduce_sum | solution.py:78
  (25 shorter events, 0.2 us)
Async XLA Ops:
  7.2 119.0 %copy-start = (bf16[1,2048,384]{2,1,0:T(8,128)(2,1)S(1)}, bf16[1,2048,384]{2,1,0:T(8,128)(2,1)}, u32[]{:S(2)}) copy-start(bf16[1,2048,384]{2,1,0:T(8,128)(2,1)} %param.11) | copy-start | bytes 4718596
  35.7 8.8 %copy-start.5 = (f32[128,8]{0,1:T(8,128)S(1)}, f32[128,8]{0,1:T(8,128)}, u32[]{:S(2)}) copy-start(f32[128,8]{0,1:T(8,128)} %param.9) | copy-start | bytes 12292
  35.7 9.0 %copy-start.4 = (bf16[128,2048]{1,0:T(8,128)(2,1)S(1)}, bf16[128,2048]{1,0:T(8,128)(2,1)}, u32[]{:S(2)}) copy-start(bf16[128,2048]{1,0:T(8,128)(2,1)} %param.8) | copy-start | bytes 1572868
  35.7 73.3 %all-to-all-start.1 = ((bf16[32,36,2048]{2,1,0:T(8,128)(2,1)}), bf16[32,36,2048]{2,1,0:T(8,128)(2,1)}, u32[]{:S(2)}, u32[]{:S(2)}) async-start(bf16[32,36,2048]{2,1,0:T(8,128)(2,1)} %reshape.187), calls=%async_computation.1 | async-start | bytes 10485760 | tf_op jit(solution)/shard_map/all_to_all | solution.py:31
  109.1 74.4 %all-to-all-start = ((bf16[32,36,2048]{2,1,0:T(8,128)(2,1)}), bf16[32,36,2048]{2,1,0:T(8,128)(2,1)}, u32[]{:S(2)}, u32[]{:S(2)}) async-start(bf16[32,36,2048]{2,1,0:T(8,128)(2,1)} %reshape.183), calls=%async_computation | async-start | bytes 10485760 | tf_op jit(solution)/shard_map/all_to_all | solution.py:32
  118.9 178.4 %all-reduce.3.cloned.1.call-start = ((), (), s32[]{:S(2)}) async-start(), calls=%async_computation.7 | async-start | bytes 6291456
  126.2 6.3 %copy-start.1 = (bf16[1152,2048]{1,0:T(8,128)(2,1)S(1)}, bf16[1152,2048]{1,0:T(8,128)(2,1)}, u32[]{:S(2)}) copy-start(bf16[1152,2048]{1,0:T(8,128)(2,1)} %reshape.188) | copy-start | bytes 14155780
  126.2 6.3 %copy-start.2 = (bf16[1,2048,384]{2,1,0:T(8,128)(2,1)S(1)}, bf16[1,2048,384]{2,1,0:T(8,128)(2,1)}, u32[]{:S(2)}) copy-start(bf16[1,2048,384]{2,1,0:T(8,128)(2,1)} %param.12) | copy-start | bytes 4718596
  202.9 132.7 %reduce-scatter.3.cloned.1.call-start = ((), (), s32[]{:S(2)}) async-start(), calls=%async_computation.5 | async-start | bytes 1769472 | tf_op jit(solution)/shard_map/reduce_scatter | solution.py:55
  216.0 2.7 copy-start.3
  230.2 148.8 %all-to-all-start.2 = ((bf16[32,36,2048]{2,1,0:T(8,128)(2,1)}), bf16[32,36,2048]{2,1,0:T(8,128)(2,1)}, u32[]{:S(2)}, u32[]{:S(2)}) async-start(bf16[32,36,2048]{2,1,0:T(8,128)(2,1)} %reshape_transpose_reshape.2), calls=%async_computation.2 | async-start | bytes 10485760 | tf_op jit(solution)/shard_map/all_to_all | solution.py:76
  238.4 6.1 %copy-start.6 = (u32[256]{0:T(256)S(1)}, u32[256]{0:T(256)}, u32[]{:S(2)}) copy-start(u32[256]{0:T(256)} %constant.26) | copy-start | bytes 3076
  238.4 138.7 %reduce-scatter.5.cloned.1.call-start = ((), (), s32[]{:S(2)}) async-start(), calls=%async_computation.6 | async-start | bytes 1769472 | tf_op jit(solution)/shard_map/reduce_scatter | solution.py:58
Sparse Core Ops, SparseCore 0:
  203.0 94.2 all-reduce.2
  299.9 35.6 reduce-scatter.2
  338.2 38.9 reduce-scatter.4
where the time goes:
time: 415 us; the launch traced here: 410 us
  waiting for transfers between devices  222 us (53%)
  local copies, waits for them, and re-layouts  78.7 us (19%)
  matrix products  41.9 us (10%)
  starting transfers between devices  27.5 us (7%)
  other arithmetic  25.7 us (6%)
  between operations  14.6 us (4%)
    unnamed x4, waiting for transfers between devices  51.5 us
    all_to_all x1, waiting for transfers between devices, shards(): lax.all_to_all(send_x, 'expert', split_axis=0, concat_axis=0, tiled=True)  47.4 us
    all_to_all x1, waiting for transfers between devices, shards(): lax.all_to_all(send_g, 'expert', split_axis=0, concat_axis=0, tiled=True)  47.1 us
    reduce_scatter x1, waiting for transfers between devices, shards(): lax.psum_scatter(term_up.astype(jnp.bfloat16), 'dp', scatter_dimension=0,...  39.8 us
    reduce_scatter x1, waiting for transfers between devices, shards(): lax.psum_scatter(term_gate.astype(jnp.bfloat16), 'dp', scatter_dimension=...  36.1 us
    another operation x4, local copies, waits for them, and re-layouts  14.6 us
    gather x1, local copies, waits for them, and re-layouts, shards(): mine = returned.reshape(experts_all * most_rows, width)[slots]  11.8 us
    all_to_all x1, starting transfers between devices, shards(): lax.all_to_all(send_g, 'expert', split_axis=0, concat_axis=0, tiled=True)  9.83 us
  transfers between devices with their start and end apart: 6, of which 5 were waited for; matrix products, arithmetic and copies ran while one was open for 18% of the time, Pallas kernels for 0%

commit v1 on v0

v1 whole, which is shorter than its diff:
```python
import functools

import jax
import jax.numpy as jnp
from jax import lax
from jax.experimental import pallas as pl
from jax.experimental.pallas import tpu as pltpu
from jax.sharding import PartitionSpec as P

BF = jnp.bfloat16
F32 = jnp.float32
MIB = 1 << 20

MAIN = 32
REM = 4
PACK = 2 * (MAIN + REM)


def dot(a, b, ca=1, cb=0):
    return lax.dot_general(a, b, (((ca,), (cb,)), ((), ())), preferred_element_type=F32)


def iota(shape, dim):
    return lax.broadcasted_iota(jnp.int32, shape, dim)


def positions(ids, experts):
    toks, top = ids.shape
    ids_t = ids.astype(F32).T
    ident = iota((experts, toks), 0).astype(F32)
    member = jnp.zeros((experts, toks), F32)
    for k in range(top):
        member = member + jnp.where(ids_t[k : k + 1, :] == ident, 1.0, 0.0)
    before = (iota((toks, toks), 0) < iota((toks, toks), 1)).astype(F32).astype(BF)
    pos = dot(member.astype(BF), before)
    return jnp.where(member > 0.5, pos, -1.0), ids_t, ident


def select(pos):
    experts, toks = pos.shape
    wide = pos[:, None, :]
    main = (wide == iota((experts, MAIN, toks), 1).astype(F32)).astype(F32)
    rest = (wide == (MAIN + iota((experts, 2 * REM, toks), 1) % REM).astype(F32)).astype(F32)
    return main.reshape(experts * MAIN, toks), rest.reshape(experts * 2 * REM, toks)


def is_left(rows, cols):
    return iota((rows, cols), 0) % (2 * REM) < REM


def dispatch_kernel(scaled, *refs):
    if scaled:
        ids_ref, gates_ref, left_ref, right_ref, out_ref, main_ref, rest_ref, gmain_ref, grest_ref = refs
    else:
        ids_ref, left_ref, right_ref, out_ref, main_ref, rest_ref = refs
    experts, _, width = out_ref.shape

    @pl.when(pl.program_id(0) == 0)
    def _():
        pos, ids_t, ident = positions(ids_ref[...], experts)
        main, rest = select(pos)
        main_ref[...] = main.astype(BF)
        rest_ref[...] = rest.astype(BF)
        if scaled:
            gates_t = gates_ref[...].T
            weight = jnp.zeros(pos.shape, F32)
            for k in range(gates_t.shape[0]):
                weight = weight + jnp.where(ids_t[k : k + 1, :] == ident, gates_t[k : k + 1, :], 0.0)
            toks = pos.shape[1]
            for rows, sel, ref in ((MAIN, main, gmain_ref), (2 * REM, rest, grest_ref)):
                wide = jnp.broadcast_to(weight[:, None, :], (experts, rows, toks)).reshape(experts * rows, toks)
                ref[...] = jnp.broadcast_to(jnp.sum(sel * wide, axis=1, keepdims=True), ref.shape)

    left, right = left_ref[...], right_ref[...]

    def rows_of(sel_ref, g_ref, data):
        got = dot(sel_ref[...], data)
        if scaled:
            got = got * jnp.concatenate([g_ref[...]] * (width // 128), axis=1)
        return got

    gm = gmain_ref if scaled else None
    gr = grest_ref if scaled else None
    out_ref[:, 0:MAIN, :] = rows_of(main_ref, gm, left).astype(BF).reshape(experts, MAIN, width)
    out_ref[:, MAIN : 2 * MAIN, :] = rows_of(main_ref, gm, right).astype(BF).reshape(experts, MAIN, width)
    rest_l = rows_of(rest_ref, gr, left)
    rest_r = rows_of(rest_ref, gr, right)
    both = jnp.where(is_left(*rest_l.shape), rest_l, rest_r)
    out_ref[:, 2 * MAIN : PACK, :] = both.astype(BF).reshape(experts, 2 * REM, width)


def dispatch(ids, data, experts, gates=None):
    toks, width = data.shape
    half, steps = width // 2, 4
    cols = half // steps
    full = lambda a: pl.BlockSpec(a.shape, lambda c: (0,) * a.ndim)
    small = [ids] if gates is None else [ids, gates]
    scratch = [pltpu.VMEM((experts * MAIN, toks), BF), pltpu.VMEM((experts * 2 * REM, toks), BF)]
    if gates is not None:
        scratch += [pltpu.VMEM((experts * MAIN, 128), F32), pltpu.VMEM((experts * 2 * REM, 128), F32)]
    return pl.pallas_call(
        functools.partial(dispatch_kernel, gates is not None),
        out_shape=jax.ShapeDtypeStruct((experts, PACK, half), BF),
        grid=(steps,),
        in_specs=[full(a) for a in small]
        + [pl.BlockSpec((toks, cols), lambda c: (0, c)), pl.BlockSpec((toks, cols), lambda c: (0, c + steps))],
        out_specs=pl.BlockSpec((experts, PACK, cols), lambda c: (0, 0, c)),
        scratch_shapes=scratch,
        compiler_params=pltpu.CompilerParams(vmem_limit_bytes=28 * MIB),
        cost_estimate=pl.CostEstimate(flops=2 * 1280 * toks * width, bytes_accessed=6 * MIB, transcendentals=0),
        name="dispatch",
    )(*small, data, data)


def halves(ref):
    n, _, half = ref.shape
    rest = ref[:, 2 * MAIN : PACK, :].reshape(n * 2 * REM, half)
    left = ref[:, 0:MAIN, :].reshape(n * MAIN, half)
    right = ref[:, MAIN : 2 * MAIN, :].reshape(n * MAIN, half)
    return jnp.concatenate([left, rest], axis=0), jnp.concatenate([right, rest], axis=0)


def joined(p_left, p_right, mains):
    main = p_left[:mains] + p_right[:mains]
    tail = p_right[mains:]
    rest = p_left[mains:] + pltpu.roll(tail, tail.shape[0] - REM, 0)
    return main, jnp.where(is_left(*rest.shape), rest, 0.0)


def forward_kernel(x_ref, wg_ref, wu_ref, csm_ref, csr_ref, actm_ref, actr_ref, wcat_ref):
    hidden = wg_ref.shape[1]
    half = x_ref.shape[2]

    @pl.when(pl.program_id(0) == 0)
    def _():
        wcat_ref[:, :hidden] = wg_ref[...]
        wcat_ref[:, hidden:] = wu_ref[...]

    mains = x_ref.shape[0] * MAIN
    a_left, a_right = halves(x_ref)
    pre = joined(dot(a_left, wcat_ref[:half, :]), dot(a_right, wcat_ref[half:, :]), mains)
    for p, cs_ref, act_ref in zip(pre, (csm_ref, csr_ref), (actm_ref, actr_ref)):
        gate, up = p[:, :hidden], p[:, hidden:]
        sigma = jax.nn.sigmoid(gate)
        silu = gate * sigma
        cs_ref[:, :hidden] = up * sigma * (1.0 + gate * (1.0 - sigma))
        cs_ref[:, hidden:] = silu
        act_ref[...] = (silu * up).astype(BF)


def forward(rx, wg, wu):
    n, _, half = rx.shape
    width, hidden = wg.shape
    steps = 4
    step = n // steps
    rows = lambda per, cols: pl.BlockSpec((step * per, cols), lambda i: (i, 0))
    full = lambda shape: pl.BlockSpec(shape, lambda i: (0, 0))
    mains, rests = n * MAIN, n * 2 * REM
    return pl.pallas_call(
        forward_kernel,
        out_shape=(
            jax.ShapeDtypeStruct((mains, 2 * hidden), F32),
            jax.ShapeDtypeStruct((rests, 2 * hidden), F32),
            jax.ShapeDtypeStruct((mains, hidden), BF),
            jax.ShapeDtypeStruct((rests, hidden), BF),
            jax.ShapeDtypeStruct((width, 2 * hidden), BF),
        ),
        grid=(steps,),
        in_specs=[
            pl.BlockSpec((step, PACK, half), lambda i: (i, 0, 0)),
            full((width, hidden)),
            full((width, hidden)),
        ],
        out_specs=(
            rows(MAIN, 2 * hidden),
            rows(2 * REM, 2 * hidden),
            rows(MAIN, hidden),
            rows(2 * REM, hidden),
            full((width, 2 * hidden)),
        ),
        compiler_params=pltpu.CompilerParams(vmem_limit_bytes=40 * MIB),
        cost_estimate=pl.CostEstimate(
            flops=2 * (mains + rests) * width * 2 * hidden, bytes_accessed=16 * MIB, transcendentals=mains * hidden
        ),
        name="forward",
    )(rx, wg, wu)


def hidden_grad_kernel(g_ref, wd_ref, csm_ref, csr_ref, dm_ref, dr_ref):
    half = g_ref.shape[2]
    mains = g_ref.shape[0] * MAIN
    a_left, a_right = halves(g_ref)
    d_act = joined(dot(a_left, wd_ref[:, :half], 1, 1), dot(a_right, wd_ref[:, half:], 1, 1), mains)
    for d, cs_ref, out_ref in zip(d_act, (csm_ref, csr_ref), (dm_ref, dr_ref)):
        out_ref[...] = (jnp.concatenate([d, d], axis=1) * cs_ref[...]).astype(BF)


def hidden_grad(rg, wd, csm, csr):
    n, _, half = rg.shape
    hidden = wd.shape[0]
    steps = 4
    step = n // steps
    rows = lambda per, cols: pl.BlockSpec((step * per, cols), lambda i: (i, 0))
    mains, rests = n * MAIN, n * 2 * REM
    return pl.pallas_call(
        hidden_grad_kernel,
        out_shape=(
            jax.ShapeDtypeStruct((mains, 2 * hidden), BF),
            jax.ShapeDtypeStruct((rests, 2 * hidden), BF),
        ),
        grid=(steps,),
        in_specs=[
            pl.BlockSpec((step, PACK, half), lambda i: (i, 0, 0)),
            pl.BlockSpec(wd.shape, lambda i: (0, 0)),
            rows(MAIN, 2 * hidden),
            rows(2 * REM, 2 * hidden),
        ],
        out_specs=(rows(MAIN, 2 * hidden), rows(2 * REM, 2 * hidden)),
        compiler_params=pltpu.CompilerParams(vmem_limit_bytes=32 * MIB),
        cost_estimate=pl.CostEstimate(
            flops=2 * (mains + rests) * 2 * half * hidden, bytes_accessed=12 * MIB, transcendentals=0
        ),
        name="hidden_grad",
    )(rg, wd, csm, csr)


def shifted(rest):
    return pltpu.roll(rest.astype(F32), REM, 0)


def weight_grad_kernel(x_ref, g_ref, dm_ref, dr_ref, actm_ref, actr_ref, out_ref, dt_ref, at_ref):
    copies = out_ref.shape[0]
    n, _, half = x_ref.shape
    mains = n * MAIN
    both, hidden = dm_ref.shape[1], actm_ref.shape[1]

    for src_m, src_r, dst in ((dm_ref, dr_ref, dt_ref), (actm_ref, actr_ref, at_ref)):
        main_t = src_m[...].T
        rest = src_r[...]
        dst[0, :, :mains] = main_t
        dst[1, :, :mains] = main_t
        dst[0, :, mains:] = rest.T
        dst[1, :, mains:] = shifted(rest).astype(BF).T

    tile = 256
    per = 2 * half // copies
    slab = hidden // copies
    base = both * per // 128
    for side in range(2):
        for j in range(half // tile):
            cols = pl.ds(j * tile, tile)

            def rows_of(ref):
                main = ref[:, side * MAIN : (side + 1) * MAIN, cols].reshape(mains, tile)
                rest = ref[:, 2 * MAIN : PACK, cols].reshape(n * 2 * REM, tile)
                return jnp.concatenate([main, rest], axis=0)

            into = dot(dt_ref[side], rows_of(x_ref)).astype(BF)
            down = dot(at_ref[side], rows_of(g_ref)).astype(BF)
            for q in range(tile // 128):
                at = (side * half + j * tile) // 128 + q
                owner, piece = at * 128 // per, at % (per // 128)
                part = into[:, q * 128 : (q + 1) * 128]
                out_ref[owner, piece * both : (piece + 1) * both, :] = part
                part = down[:, q * 128 : (q + 1) * 128].reshape(copies, slab, 128)
                out_ref[:, base + at * slab : base + (at + 1) * slab, :] = part


def weight_grad(rx, rg, dm, dr, actm, actr, copies):
    n, _, half = rx.shape
    both, hidden = dm.shape[1], actm.shape[1]
    rows = dm.shape[0] + dr.shape[0]
    length = 3 * hidden * 2 * half // copies // 128
    return pl.pallas_call(
        weight_grad_kernel,
        out_shape=jax.ShapeDtypeStruct((copies, length, 128), BF),
        in_specs=[pl.BlockSpec(memory_space=pltpu.VMEM)] * 6,
        out_specs=pl.BlockSpec(memory_space=pltpu.VMEM),
        scratch_shapes=[pltpu.VMEM((2, both, rows), BF), pltpu.VMEM((2, hidden, rows), BF)],
        compiler_params=pltpu.CompilerParams(vmem_limit_bytes=40 * MIB),
        cost_estimate=pl.CostEstimate(
            flops=2 * rows * 2 * half * 3 * hidden, bytes_accessed=18 * MIB, transcendentals=0
        ),
        name="weight_grad",
    )(rx, rg, dm, dr, actm, actr)


def unpack_kernel(in_ref, gate_ref, up_ref, down_ref):
    per, hidden = gate_ref.shape
    slab = down_ref.shape[0]
    base = 2 * hidden * per // 128
    for q in range(per // 128):
        both = in_ref[q * 2 * hidden : (q + 1) * 2 * hidden, :].T
        gate_ref[q * 128 : (q + 1) * 128, :] = both[:, :hidden]
        up_ref[q * 128 : (q + 1) * 128, :] = both[:, hidden:]
    for q in range(down_ref.shape[1] // 128):
        down_ref[:, q * 128 : (q + 1) * 128] = in_ref[base + q * slab : base + (q + 1) * slab, :]


def unpack(summed, per, hidden, width, slab):
    vmem = pl.BlockSpec(memory_space=pltpu.VMEM)
    return pl.pallas_call(
        unpack_kernel,
        out_shape=(
            jax.ShapeDtypeStruct((per, hidden), BF),
            jax.ShapeDtypeStruct((per, hidden), BF),
            jax.ShapeDtypeStruct((slab, width), BF),
        ),
        in_specs=[vmem],
        out_specs=(vmem, vmem, vmem),
        cost_estimate=pl.CostEstimate(flops=0, bytes_accessed=2 * MIB, transcendentals=0),
        name="unpack",
    )(summed)


def pair_grad_kernel(dm_ref, dr_ref, wcat_ref, out_ref):
    n, _, half = out_ref.shape
    mains = n * MAIN
    main, rest = dm_ref[...], dr_ref[...]
    d_left = jnp.concatenate([main, rest], axis=0)
    d_right = jnp.concatenate([main, shifted(rest).astype(BF)], axis=0)
    y_left = dot(d_left, wcat_ref[:half, :], 1, 1)
    y_right = dot(d_right, wcat_ref[half:, :], 1, 1)
    out_ref[:, 0:MAIN, :] = y_left[:mains].astype(BF).reshape(n, MAIN, half)
    out_ref[:, MAIN : 2 * MAIN, :] = y_right[:mains].astype(BF).reshape(n, MAIN, half)
    out_ref[:, 2 * MAIN : PACK, :] = (y_left[mains:] + y_right[mains:]).astype(BF).reshape(n, 2 * REM, half)


def pair_grad(dm, dr, wcat):
    width, both = wcat.shape
    n, half = dm.shape[0] // MAIN, width // 2
    steps = 4
    step = n // steps
    return pl.pallas_call(
        pair_grad_kernel,
        out_shape=jax.ShapeDtypeStruct((n, PACK, half), BF),
        grid=(steps,),
        in_specs=[
            pl.BlockSpec((step * MAIN, both), lambda i: (i, 0)),
            pl.BlockSpec((step * 2 * REM, both), lambda i: (i, 0)),
            pl.BlockSpec(wcat.shape, lambda i: (0, 0)),
        ],
        out_specs=pl.BlockSpec((step, PACK, half), lambda i: (i, 0, 0)),
        compiler_params=pltpu.CompilerParams(vmem_limit_bytes=32 * MIB),
        cost_estimate=pl.CostEstimate(flops=2 * 1280 * width * both, bytes_accessed=10 * MIB, transcendentals=0),
        name="pair_grad",
    )(dm, dr, wcat)


def combine_kernel(ids_ref, ret_ref, out_ref, main_ref, rest_ref):
    experts, _, cols = ret_ref.shape
    toks = out_ref.shape[0]
    half = out_ref.shape[1] // 2
    c = pl.program_id(0)

    @pl.when(c == 0)
    def _():
        pos, _, _ = positions(ids_ref[...], experts)
        main, rest = select(pos)
        left = is_left(*rest.shape)
        main_ref[...] = main.T.astype(BF)
        rest_ref[0] = jnp.where(left, rest, 0.0).T.astype(BF)
        rest_ref[1] = jnp.where(left, 0.0, rest).T.astype(BF)

    tail = ret_ref[:, 2 * MAIN : PACK, :].reshape(experts * 2 * REM, cols)
    for side in range(2):
        body = ret_ref[:, side * MAIN : (side + 1) * MAIN, :].reshape(experts * MAIN, cols)
        total = dot(main_ref[...], body) + dot(rest_ref[side], tail)
        out_ref[:, pl.ds(pl.multiple_of(side * half + c * cols, 128), cols)] = total.astype(BF)


def combine(ids, ret):
    experts, _, half = ret.shape
    toks = ids.shape[0]
    steps = 4
    cols = half // steps
    return pl.pallas_call(
        combine_kernel,
        out_shape=jax.ShapeDtypeStruct((toks, 2 * half), BF),
        grid=(steps,),
        in_specs=[
            pl.BlockSpec(ids.shape, lambda c: (0, 0)),
            pl.BlockSpec((experts, PACK, cols), lambda c: (0, 0, c)),
        ],
        out_specs=pl.BlockSpec((toks, 2 * half), lambda c: (0, 0)),
        scratch_shapes=[
            pltpu.VMEM((toks, experts * MAIN), BF),
            pltpu.VMEM((2, toks, experts * 2 * REM), BF),
        ],
        compiler_params=pltpu.CompilerParams(vmem_limit_bytes=24 * MIB),
        cost_estimate=pl.CostEstimate(flops=2 * 1280 * toks * 2 * half, bytes_accessed=6 * MIB, transcendentals=0),
        name="combine",
    )(ids, ret)


def exchange(block):
    return lax.all_to_all(block, "expert", split_axis=0, concat_axis=0, tiled=True)


def shards(tokens, grad_out, gates, expert_ids, w_gate, w_up, w_down):
    experts = lax.axis_size("expert")
    copies = lax.axis_size("dp")
    wg, wu, wd = w_gate[0], w_up[0], w_down[0]
    width, hidden = wg.shape
    send_x, grad_out = lax.optimization_barrier((dispatch(expert_ids, tokens, experts), grad_out))
    rx = exchange(send_x)
    rg = exchange(dispatch(expert_ids, grad_out, experts, gates))
    csm, csr, actm, actr, wcat = forward(rx, wg, wu)
    dm, dr = hidden_grad(rg, wd, csm, csr)
    packed = weight_grad(rx, rg, dm, dr, actm, actr, copies)
    summed = lax.psum_scatter(packed, "dp", scatter_dimension=0, tiled=True)[0]
    ret = exchange(pair_grad(dm, dr, wcat))
    grad_tokens = combine(expert_ids, ret)
    grad_g, grad_u, grad_d = unpack(summed, width // copies, hidden, width, hidden // copies)
    return (grad_tokens, grad_g[None], grad_u[None], grad_d[None])


def solution(mesh):
    rows = P(("dp", "expert"), None)
    weights = P("expert", None, None)
    cut = P("expert", "dp", None)
    return jax.shard_map(
        shards,
        mesh=mesh,
        in_specs=(rows, rows, rows, rows, weights, weights, weights),
        out_specs=(rows, cut, cut, cut),
        check_vma=False,
    )
```

time: 415 us -> 255 us (0.61)
  waiting for transfers between devices: 222 us -> 98.6 us
  blocking collectives: 0 us -> 63.7 us
  local copies, waits for them, and re-layouts: 78.7 us -> 22.5 us
  matrix products: 41.9 us -> 0 us
  Pallas kernels: 0 us -> 38.3 us
  other arithmetic: 25.7 us -> 0 us
  starting transfers between devices: 27.5 us -> 16.6 us
    reduce_scatter x2 -> x1, waiting for transfers between devices: 75.9 us -> 0.01 us  [shards(): summed = lax.psum_scatter(packed, 'dp', scatter_dimension=0, tiled=True)[0]]
    all_to_all x0 -> x1, blocking collectives: none -> 63.7 us  [exchange(): lax.all_to_all(block, 'expert', split_axis=0, concat_axis=0, tiled=True)]
    unnamed x4 -> x1, waiting for transfers between devices: 51.5 us -> 0.02 us
    dot_general x8 -> x0, matrix products: 41.9 us -> none  [the longest x1 7.06 us: shards(): jnp.einsum('erd,efd->erf', routed, w_down, preferred_element_type=jnp.flo...]
    pallas_call x0 -> x8, Pallas kernels: none -> 38.3 us  [the longest x1 10.1 us: weight_grad(): pl.pallas_call(weight_grad_kernel, out_shape=jax.ShapeDtypeStruct((copies...]
    another operation x5 -> x0, local copies, waits for them, and re-layouts: 21.8 us -> none
    reshape x3 -> x0, local copies, waits for them, and re-layouts: 21.6 us -> none  [the longest x1 7.24 us: shards(): mine = returned.reshape(experts_all * most_rows, width)[slots]]
    unnamed x21 -> x40, local copies, waits for them, and re-layouts: 7.19 us -> 22.5 us
  transfers between devices with their start and end apart: 6 -> 3, of which waited for: 5 -> 2; matrix products, arithmetic and copies ran while one was open for 18% -> 0% of each run, Pallas kernels for 0% -> 7%
where the time goes in v1:
time: 255 us; the launch traced here: 254 us
  waiting for transfers between devices  98.6 us (39%)
  blocking collectives  63.7 us (25%)
  Pallas kernels  38.3 us (15%)
  local copies, waits for them, and re-layouts  22.5 us (9%)
  starting transfers between devices  16.6 us (7%)
  between operations  14.2 us (6%)
    all_to_all x2, waiting for transfers between devices, exchange(): lax.all_to_all(block, 'expert', split_axis=0, concat_axis=0, tiled=True)  98.6 us
    all_to_all x1, blocking collectives, exchange(): lax.all_to_all(block, 'expert', split_axis=0, concat_axis=0, tiled=True)  63.7 us
    unnamed x40, local copies, waits for them, and re-layouts  22.5 us
    all_to_all x2, starting transfers between devices, exchange(): lax.all_to_all(block, 'expert', split_axis=0, concat_axis=0, tiled=True)  16.6 us
    pallas_call x1, Pallas kernels, weight_grad(): pl.pallas_call(weight_grad_kernel, out_shape=jax.ShapeDtypeStruct((copies...  10.1 us
    pallas_call x1, Pallas kernels, forward(): pl.pallas_call(forward_kernel, out_shape=(jax.ShapeDtypeStruct((mains, 2...  6.56 us
    pallas_call x2, Pallas kernels, dispatch(): pl.pallas_call(functools.partial(dispatch_kernel, gates is not None), out...  6.08 us
    pallas_call x1, Pallas kernels, hidden_grad(): pl.pallas_call(hidden_grad_kernel, out_shape=(jax.ShapeDtypeStruct((mains...  5.37 us
  transfers between devices with their start and end apart: 3, of which 2 were waited for; matrix products, arithmetic and copies ran while one was open for 0% of the time, Pallas kernels for 7%

profile of v1, /device:TPU:1, one launch (start us, length us, event | category | flops | bytes accessed | tf_op | source)
XLA Modules:
  0.0 253.9 jit_solution(14799922380098989099)
XLA Ops:
  7.2 0.8 copy.14.refs_0_.ids_ref
  8.0 0.0 copy-start.3
  8.0 1.0 copy-done.3
  9.0 2.9 %dispatch.2 = bf16[32,72,1024]{2,1,0:T(8,128)(2,1)S(1)} custom-call(s32[128,8]{1,0:T(8,128)S(1)} %copy.14.refs_0_.ids_ref, bf16[128,2048]{1,0:T(8,128)(2,1)S(1)} %copy-done.3, bf16[128,2048]{1,0:T(8,128)(2,1)S(1)} %copy-done.3), custom_call_target="tpu_custom_call" | custom-call | flops 671088640 | bytes 6291456 | tf_op jit(solution)/shard_map/dispatch/pallas_call | solution.py:101
  11.9 0.0 copy-start.1
  11.9 2.2 copy-done.1
  14.1 0.0 copy-start.18
  14.1 0.0 copy-start.4
  14.1 8.8 %all-to-all-start.1 = ((bf16[32,72,1024]{2,1,0:T(8,128)(2,1)}), bf16[32,72,1024]{2,1,0:T(8,128)(2,1)}, u32[]{:S(2)}, u32[]{:S(2)}) async-start(bf16[32,72,1024]{2,1,0:T(8,128)(2,1)} %copy-done.1), calls=%async_computation.1 | async-start | bytes 9437184 | tf_op jit(solution)/shard_map/all_to_all | solution.py:397
  22.9 0.0 copy-done.18
  22.9 0.1 copy.13.refs_1_
  23.0 0.0 copy-done.4
  23.0 3.2 %dispatch.3 = bf16[32,72,1024]{2,1,0:T(8,128)(2,1)S(1)} custom-call(s32[128,8]{1,0:T(8,128)S(1)} %copy.14.refs_0_.ids_ref, f32[128,8]{1,0:T(8,128)S(1)} %copy.13.refs_1_, bf16[128,2048]{1,0:T(8,128)(2,1)S(1)} %copy-done.4, bf16[128,2048]{1,0:T(8,128)(2,1)S(1)} %copy-done.4), custom_call_target="tpu_custom_call" | custom-call | flops 671088640 | bytes 6291456 | tf_op jit(solution)/shard_map/dispatch/pallas_call | solution.py:101
  26.2 0.0 copy-start
  26.2 2.2 copy-done
  28.4 52.9 %all-to-all-done.1.x_ref = bf16[32,72,1024]{2,1,0:T(8,128)(2,1)} async-done(((bf16[32,72,1024]{2,1,0:T(8,128)(2,1)}), bf16[32,72,1024]{2,1,0:T(8,128)(2,1)}, u32[]{:S(2)}, u32[]{:S(2)}) %all-to-all-start.1) | async-done | bytes 4718624 | tf_op jit(solution)/shard_map/all_to_all | solution.py:397
  81.3 7.8 %all-to-all-start = ((bf16[32,72,1024]{2,1,0:T(8,128)(2,1)}), bf16[32,72,1024]{2,1,0:T(8,128)(2,1)}, u32[]{:S(2)}, u32[]{:S(2)}) async-start(bf16[32,72,1024]{2,1,0:T(8,128)(2,1)} %copy-done), calls=%async_computation | async-start | bytes 9437184 | tf_op jit(solution)/shard_map/all_to_all | solution.py:397
  89.1 0.0 reduce-scatter.2.cloned.1.call-start
  89.2 0.0 copy-start.8
  89.2 1.4 copy-done.8
  90.6 0.0 copy-start.9
  90.6 1.4 copy-done.9
  92.0 6.6 %forward.1 = (f32[1024,768]{1,0:T(8,128)S(1)}, f32[256,768]{1,0:T(8,128)S(1)}, bf16[1024,384]{1,0:T(8,128)(2,1)S(1)}, bf16[256,384]{1,0:T(8,128)(2,1)S(1)}, bf16[2048,768]{1,0:T(8,128)(2,1)S(1)}) custom-call(bf16[32,72,1024]{2,1,0:T(8,128)(2,1)} %all-to-all-done.1.x_ref, bf16[2048,384]{1,0:T(8,128)(2,1)S(1)} %bitcast.8, bf16[2048,384]{1,0:T(8,128)(2,1)S(1)} %bitcast.9), custom_call_target="tpu_custom_call" | custom-call | flops 4026531840 | bytes 16777216 | tf_op jit(solution)/shard_map/forward/pallas_call | solution.py:159
  98.6 0.0 copy-start.6
  98.6 0.9 copy-done.6
  99.5 0.0 copy-start.14
  99.5 1.6 copy-done.14
  101.1 0.0 copy-start.16
  101.1 0.9 copy-done.16
  102.0 45.7 %all-to-all-done.g_ref = bf16[32,72,1024]{2,1,0:T(8,128)(2,1)} async-done(((bf16[32,72,1024]{2,1,0:T(8,128)(2,1)}), bf16[32,72,1024]{2,1,0:T(8,128)(2,1)}, u32[]{:S(2)}, u32[]{:S(2)}) %all-to-all-start) | async-done | bytes 4718624 | tf_op jit(solution)/shard_map/all_to_all | solution.py:397
  147.7 0.0 copy-start.5
  147.7 1.4 copy-done.5
  149.1 1.1 copy-done.7
  150.2 5.4 %hidden_grad.1 = (bf16[1024,768]{1,0:T(8,128)(2,1)S(1)}, bf16[256,768]{1,0:T(8,128)(2,1)S(1)}) custom-call(bf16[32,72,1024]{2,1,0:T(8,128)(2,1)} %all-to-all-done.g_ref, bf16[384,2048]{1,0:T(8,128)(2,1)S(1)} %bitcast.7, f32[1024,768]{1,0:T(8,128)S(1)} %get-tuple-element.18.csm_ref, f32[256,768]{1,0:T(8,128)S(1)} %copy-done.7), custom_call_target="tpu_custom_call" | custom-call | flops 2013265920 | bytes 12582912 | tf_op jit(solution)/shard_map/hidden_grad/pallas_call | solution.py:205
  155.6 0.0 copy-done.17
  155.6 10.1 %weight_grad.1 = bf16[8,2304,128]{2,1,0:T(8,128)(2,1)S(1)} custom-call(bf16[32,72,1024]{2,1,0:T(8,128)(2,1)} %all-to-all-done.1.x_ref, bf16[32,72,1024]{2,1,0:T(8,128)(2,1)} %all-to-all-done.g_ref, bf16[1024,768]{1,0:T(8,128)(2,1)S(1)} %get-tuple-element.20.dm_ref, bf16[256,768]{1,0:T(8,128)(2,1)S(1)} %get-tuple-element.21.dr_ref, ...), custom_call_target="tpu_custom_call" | custom-call | flops 6039797760 | bytes 18874368 | tf_op jit(solution)/shard_map/weight_grad/pallas_call | solution.py:274
  165.7 0.0 copy-start.2
  165.7 2.1 copy-done.2
  167.8 1.2 copy-done.10
  169.0 0.7 copy-done.12
  169.8 0.0 reduce-scatter.2.cloned.1.call-update
  169.8 1.4 copy-done.11
  171.2 0.1 copy-done.13
  171.3 1.9 copy-done.15
  173.1 4.9 %pair_grad.1 = bf16[32,72,1024]{2,1,0:T(8,128)(2,1)S(1)} custom-call(bf16[1024,768]{1,0:T(8,128)(2,1)S(1)} %copy-done.11, bf16[256,768]{1,0:T(8,128)(2,1)S(1)} %copy-done.13, bf16[2048,768]{1,0:T(8,128)(2,1)S(1)} %copy-done.15), custom_call_target="tpu_custom_call" | custom-call | flops 4026531840 | bytes 10485760 | tf_op jit(solution)/shard_map/pair_grad/pallas_call | solution.py:334
  178.0 63.7 %all_to_all.15.ret_ref = bf16[32,72,1024]{2,1,0:T(8,128)(2,1)S(1)} all-to-all(bf16[32,72,1024]{2,1,0:T(8,128)(2,1)S(1)} %pair_grad.1), channel_id=1, replica_groups=mesh['dp'=8,'expert'=32] {'expert'}, dimensions={0} | all-to-all | bytes 9437184 | tf_op jit(solution)/shard_map/all_to_all | solution.py:397
  241.7 3.3 %combine.1 = bf16[128,2048]{1,0:T(8,128)(2,1)} custom-call(s32[128,8]{1,0:T(8,128)S(1)} %copy.14.refs_0_.ids_ref, bf16[32,72,1024]{2,1,0:T(8,128)(2,1)S(1)} %all_to_all.15.ret_ref), custom_call_target="tpu_custom_call" | custom-call | flops 671088640 | bytes 6291456 | tf_op jit(solution)/shard_map/combine/pallas_call | solution.py:377
  245.0 2.0 unpack.1
  (8 shorter events, 0.0 us)
Async XLA Ops:
  8.0 1.0 copy-start.3
  11.9 2.2 copy-start.1
  14.1 8.8 %copy-start.18 = (f32[128,8]{0,1:T(8,128)S(1)}, f32[128,8]{0,1:T(8,128)}, u32[]{:S(2)}) copy-start(f32[128,8]{0,1:T(8,128)} %param.9) | copy-start | bytes 12292
  14.1 8.9 %copy-start.4 = (bf16[128,2048]{1,0:T(8,128)(2,1)S(1)}, bf16[128,2048]{1,0:T(8,128)(2,1)}, u32[]{:S(2)}) copy-start(bf16[128,2048]{1,0:T(8,128)(2,1)} %refs_3_) | copy-start | bytes 1572868
  14.1 67.2 %all-to-all-start.1 = ((bf16[32,72,1024]{2,1,0:T(8,128)(2,1)}), bf16[32,72,1024]{2,1,0:T(8,128)(2,1)}, u32[]{:S(2)}, u32[]{:S(2)}) async-start(bf16[32,72,1024]{2,1,0:T(8,128)(2,1)} %copy-done.1), calls=%async_computation.1 | async-start | bytes 9437184 | tf_op jit(solution)/shard_map/all_to_all | solution.py:397
  26.2 2.2 copy-start
  81.3 66.4 %all-to-all-start = ((bf16[32,72,1024]{2,1,0:T(8,128)(2,1)}), bf16[32,72,1024]{2,1,0:T(8,128)(2,1)}, u32[]{:S(2)}, u32[]{:S(2)}) async-start(bf16[32,72,1024]{2,1,0:T(8,128)(2,1)} %copy-done), calls=%async_computation | async-start | bytes 9437184 | tf_op jit(solution)/shard_map/all_to_all | solution.py:397
  89.1 155.9 %reduce-scatter.2.cloned.1.call-start = ((), (), s32[]{:S(2)}) async-start(), calls=%async_computation.4 | async-start | bytes 5308416 | tf_op jit(solution)/shard_map/reduce_scatter | solution.py:411
  89.2 1.4 copy-start.8
  90.6 1.4 copy-start.9
  98.6 0.9 copy-start.6
  99.5 1.6 copy-start.14
  101.1 0.9 copy-start.16
  147.7 1.4 copy-start.5
  149.1 1.1 copy-start.7
  150.2 5.4 %copy-start.17 = (bf16[1024,384]{1,0:T(8,128)(2,1)S(1)}, bf16[1024,384]{1,0:T(8,128)(2,1)}, u32[]{:S(2)}) copy-start(bf16[1024,384]{1,0:T(8,128)(2,1)} %copy-done.16) | copy-start | bytes 2359300
  165.7 2.1 copy-start.2
  167.8 1.2 copy-start.10
  169.0 0.7 copy-start.12
  169.8 1.4 copy-start.11
  169.8 1.5 copy-start.13
  171.3 1.9 copy-start.15
Sparse Core Ops, SparseCore 0:
  169.9 62.8 reduce-scatter.1

commit v2 on v1

--- a/solution.py
+++ b/solution.py
@@ -100,7 +100,7 @@
         scratch += [pltpu.VMEM((experts * MAIN, 128), F32), pltpu.VMEM((experts * 2 * REM, 128), F32)]
     return pl.pallas_call(
         functools.partial(dispatch_kernel, gates is not None),
-        out_shape=jax.ShapeDtypeStruct((experts, PACK, half), BF),
+        out_shape=pltpu.HBM((experts, PACK, half), BF),
         grid=(steps,),
         in_specs=[full(a) for a in small]
         + [pl.BlockSpec((toks, cols), lambda c: (0, c)), pl.BlockSpec((toks, cols), lambda c: (0, c + steps))],
@@ -178,7 +178,7 @@
             rows(2 * REM, hidden),
             full((width, 2 * hidden)),
         ),
-        compiler_params=pltpu.CompilerParams(vmem_limit_bytes=40 * MIB),
+        compiler_params=pltpu.CompilerParams(vmem_limit_bytes=28 * MIB),
         cost_estimate=pl.CostEstimate(
             flops=2 * (mains + rests) * width * 2 * hidden, bytes_accessed=16 * MIB, transcendentals=mains * hidden
         ),
@@ -186,61 +186,44 @@
     )(rx, wg, wu)
 
 
-def hidden_grad_kernel(g_ref, wd_ref, csm_ref, csr_ref, dm_ref, dr_ref):
-    half = g_ref.shape[2]
-    mains = g_ref.shape[0] * MAIN
-    a_left, a_right = halves(g_ref)
-    d_act = joined(dot(a_left, wd_ref[:, :half], 1, 1), dot(a_right, wd_ref[:, half:], 1, 1), mains)
-    for d, cs_ref, out_ref in zip(d_act, (csm_ref, csr_ref), (dm_ref, dr_ref)):
-        out_ref[...] = (jnp.concatenate([d, d], axis=1) * cs_ref[...]).astype(BF)
-
-
-def hidden_grad(rg, wd, csm, csr):
-    n, _, half = rg.shape
-    hidden = wd.shape[0]
-    steps = 4
-    step = n // steps
-    rows = lambda per, cols: pl.BlockSpec((step * per, cols), lambda i: (i, 0))
-    mains, rests = n * MAIN, n * 2 * REM
-    return pl.pallas_call(
-        hidden_grad_kernel,
-        out_shape=(
-            jax.ShapeDtypeStruct((mains, 2 * hidden), BF),
-            jax.ShapeDtypeStruct((rests, 2 * hidden), BF),
-        ),
-        grid=(steps,),
-        in_specs=[
-            pl.BlockSpec((step, PACK, half), lambda i: (i, 0, 0)),
-            pl.BlockSpec(wd.shape, lambda i: (0, 0)),
-            rows(MAIN, 2 * hidden),
-            rows(2 * REM, 2 * hidden),
-        ],
-        out_specs=(rows(MAIN, 2 * hidden), rows(2 * REM, 2 * hidden)),
-        compiler_params=pltpu.CompilerParams(vmem_limit_bytes=32 * MIB),
-        cost_estimate=pl.CostEstimate(
-            flops=2 * (mains + rests) * 2 * half * hidden, bytes_accessed=12 * MIB, transcendentals=0
-        ),
-        name="hidden_grad",
-    )(rg, wd, csm, csr)
-
-
 def shifted(rest):
     return pltpu.roll(rest.astype(F32), REM, 0)
 
 
-def weight_grad_kernel(x_ref, g_ref, dm_ref, dr_ref, actm_ref, actr_ref, out_ref, dt_ref, at_ref):
-    copies = out_ref.shape[0]
+def middle_kernel(
+    g_ref, x_ref, wd_ref, wcat_ref, csm_ref, csr_ref, actm_ref, actr_ref,
+    packed_hbm, pair_ref,
+    dm_ref, dr_ref, dt_ref, at_ref, packed_ref, sem,
+):
+    copies = packed_ref.shape[0]
     n, _, half = x_ref.shape
     mains = n * MAIN
-    both, hidden = dm_ref.shape[1], actm_ref.shape[1]
-
-    for src_m, src_r, dst in ((dm_ref, dr_ref, dt_ref), (actm_ref, actr_ref, at_ref)):
-        main_t = src_m[...].T
-        rest = src_r[...]
-        dst[0, :, :mains] = main_t
-        dst[1, :, :mains] = main_t
-        dst[0, :, mains:] = rest.T
-        dst[1, :, mains:] = shifted(rest).astype(BF).T
+    both, hidden = dm_ref.shape[1], wd_ref.shape[0]
+    parts = 4
+    step = n // parts
+    most, few = step * MAIN, step * 2 * REM
+
+    main = actm_ref[...].T
+    at_ref[0, :, :mains] = main
+    at_ref[1, :, :mains] = main
+    rest = actr_ref[...]
+    at_ref[0, :, mains:] = rest.T
+    at_ref[1, :, mains:] = shifted(rest).astype(BF).T
+
+    for i in range(parts):
+        a_left, a_right = halves(g_ref.at[i * step : (i + 1) * step])
+        d_act = joined(dot(a_left, wd_ref[:, :half], 1, 1), dot(a_right, wd_ref[:, half:], 1, 1), most)
+        for d, cs_ref, d_ref, per, base in zip(
+            d_act, (csm_ref, csr_ref), (dm_ref, dr_ref), (most, few), (0, mains)
+        ):
+            rows = slice(i * per, (i + 1) * per)
+            cols = slice(base + i * per, base + (i + 1) * per)
+            grad = jnp.concatenate([d, d], axis=1) * cs_ref[rows, :]
+            low = grad.astype(BF)
+            d_ref[rows, :] = low
+            turned = low.T
+            dt_ref[0, :, cols] = turned
+            dt_ref[1, :, cols] = turned if base == 0 else pltpu.roll(grad, REM, 0).astype(BF).T
 
     tile = 256
     per = 2 * half // copies
@@ -248,12 +231,12 @@
     base = both * per // 128
     for side in range(2):
         for j in range(half // tile):
-            cols = pl.ds(j * tile, tile)
+            cols = slice(j * tile, (j + 1) * tile)
 
             def rows_of(ref):
-                main = ref[:, side * MAIN : (side + 1) * MAIN, cols].reshape(mains, tile)
-                rest = ref[:, 2 * MAIN : PACK, cols].reshape(n * 2 * REM, tile)
-                return jnp.concatenate([main, rest], axis=0)
+                body = ref[:, side * MAIN : (side + 1) * MAIN, cols].reshape(mains, tile)
+                tail = ref[:, 2 * MAIN : PACK, cols].reshape(n * 2 * REM, tile)
+                return jnp.concatenate([body, tail], axis=0)
 
             into = dot(dt_ref[side], rows_of(x_ref)).astype(BF)
             down = dot(at_ref[side], rows_of(g_ref)).astype(BF)
@@ -261,28 +244,54 @@
                 at = (side * half + j * tile) // 128 + q
                 owner, piece = at * 128 // per, at % (per // 128)
                 part = into[:, q * 128 : (q + 1) * 128]
-                out_ref[owner, piece * both : (piece + 1) * both, :] = part
+                packed_ref[owner, piece * both : (piece + 1) * both, :] = part
                 part = down[:, q * 128 : (q + 1) * 128].reshape(copies, slab, 128)
-                out_ref[:, base + at * slab : base + (at + 1) * slab, :] = part
-
-
-def weight_grad(rx, rg, dm, dr, actm, actr, copies):
+                packed_ref[:, base + at * slab : base + (at + 1) * slab, :] = part
+    packed_out = pltpu.make_async_copy(packed_ref, packed_hbm, sem)
+    packed_out.start()
+
+    for i in range(parts):
+        main = dm_ref[i * most : (i + 1) * most, :]
+        rest = dr_ref[i * few : (i + 1) * few, :]
+        d_left = jnp.concatenate([main, rest], axis=0)
+        d_right = jnp.concatenate([main, shifted(rest).astype(BF)], axis=0)
+        y_left = dot(d_left, wcat_ref[:half, :], 1, 1)
+        y_right = dot(d_right, wcat_ref[half:, :], 1, 1)
+        some = slice(i * step, (i + 1) * step)
+        pair_ref[some, 0:MAIN, :] = y_left[:most].astype(BF).reshape(step, MAIN, half)
+        pair_ref[some, MAIN : 2 * MAIN, :] = y_right[:most].astype(BF).reshape(step, MAIN, half)
+        tail = (y_left[most:] + y_right[most:]).astype(BF)
+        pair_ref[some, 2 * MAIN : PACK, :] = tail.reshape(step, 2 * REM, half)
+    packed_out.wait()
+
+
+def middle(rg, rx, wd, wcat, csm, csr, actm, actr, copies):
     n, _, half = rx.shape
-    both, hidden = dm.shape[1], actm.shape[1]
-    rows = dm.shape[0] + dr.shape[0]
+    both, hidden = csm.shape[1], wd.shape[0]
+    mains, rests = csm.shape[0], csr.shape[0]
+    rows = mains + rests
     length = 3 * hidden * 2 * half // copies // 128
+    vmem = pl.BlockSpec(memory_space=pltpu.VMEM)
+    hbm = pl.BlockSpec(memory_space=pltpu.HBM)
     return pl.pallas_call(
-        weight_grad_kernel,
-        out_shape=jax.ShapeDtypeStruct((copies, length, 128), BF),
-        in_specs=[pl.BlockSpec(memory_space=pltpu.VMEM)] * 6,
-        out_specs=pl.BlockSpec(memory_space=pltpu.VMEM),
-        scratch_shapes=[pltpu.VMEM((2, both, rows), BF), pltpu.VMEM((2, hidden, rows), BF)],
-        compiler_params=pltpu.CompilerParams(vmem_limit_bytes=40 * MIB),
+        middle_kernel,
+        out_shape=(pltpu.HBM((copies, length, 128), BF), jax.ShapeDtypeStruct((n, PACK, half), BF)),
+        in_specs=[vmem] * 8,
+        out_specs=(hbm, vmem),
+        scratch_shapes=[
+            pltpu.VMEM((mains, both), BF),
+            pltpu.VMEM((rests, both), BF),
+            pltpu.VMEM((2, both, rows), BF),
+            pltpu.VMEM((2, hidden, rows), BF),
+            pltpu.VMEM((copies, length, 128), BF),
+            pltpu.SemaphoreType.DMA,
+        ],
+        compiler_params=pltpu.CompilerParams(vmem_limit_bytes=32 * MIB),
         cost_estimate=pl.CostEstimate(
-            flops=2 * rows * 2 * half * 3 * hidden, bytes_accessed=18 * MIB, transcendentals=0
+            flops=2 * rows * 2 * half * 6 * hidden, bytes_accessed=28 * MIB, transcendentals=0
         ),
-        name="weight_grad",
-    )(rx, rg, dm, dr, actm, actr)
+        name="middle",
+    )(rg, rx, wd, wcat, csm, csr, actm, actr)
 
 
 def unpack_kernel(in_ref, gate_ref, up_ref, down_ref):
@@ -311,40 +320,6 @@
         cost_estimate=pl.CostEstimate(flops=0, bytes_accessed=2 * MIB, transcendentals=0),
         name="unpack",
     )(summed)
-
-
-def pair_grad_kernel(dm_ref, dr_ref, wcat_ref, out_ref):
-    n, _, half = out_ref.shape
-    mains = n * MAIN
-    main, rest = dm_ref[...], dr_ref[...]
-    d_left = jnp.concatenate([main, rest], axis=0)
-    d_right = jnp.concatenate([main, shifted(rest).astype(BF)], axis=0)
-    y_left = dot(d_left, wcat_ref[:half, :], 1, 1)
-    y_right = dot(d_right, wcat_ref[half:, :], 1, 1)
-    out_ref[:, 0:MAIN, :] = y_left[:mains].astype(BF).reshape(n, MAIN, half)
-    out_ref[:, MAIN : 2 * MAIN, :] = y_right[:mains].astype(BF).reshape(n, MAIN, half)
-    out_ref[:, 2 * MAIN : PACK, :] = (y_left[mains:] + y_right[mains:]).astype(BF).reshape(n, 2 * REM, half)
-
-
-def pair_grad(dm, dr, wcat):
-    width, both = wcat.shape
-    n, half = dm.shape[0] // MAIN, width // 2
-    steps = 4
-    step = n // steps
-    return pl.pallas_call(
-        pair_grad_kernel,
-        out_shape=jax.ShapeDtypeStruct((n, PACK, half), BF),
-        grid=(steps,),
-        in_specs=[
-            pl.BlockSpec((step * MAIN, both), lambda i: (i, 0)),
-            pl.BlockSpec((step * 2 * REM, both), lambda i: (i, 0)),
-            pl.BlockSpec(wcat.shape, lambda i: (0, 0)),
-        ],
-        out_specs=pl.BlockSpec((step, PACK, half), lambda i: (i, 0, 0)),
-        compiler_params=pltpu.CompilerParams(vmem_limit_bytes=32 * MIB),
-        cost_estimate=pl.CostEstimate(flops=2 * 1280 * width * both, bytes_accessed=10 * MIB, transcendentals=0),
-        name="pair_grad",
-    )(dm, dr, wcat)
 
 
 def combine_kernel(ids_ref, ret_ref, out_ref, main_ref, rest_ref):
@@ -406,10 +381,9 @@
     rx = exchange(send_x)
     rg = exchange(dispatch(expert_ids, grad_out, experts, gates))
     csm, csr, actm, actr, wcat = forward(rx, wg, wu)
-    dm, dr = hidden_grad(rg, wd, csm, csr)
-    packed = weight_grad(rx, rg, dm, dr, actm, actr, copies)
+    packed, outgoing = middle(rg, rx, wd, wcat, csm, csr, actm, actr, copies)
     summed = lax.psum_scatter(packed, "dp", scatter_dimension=0, tiled=True)[0]
-    ret = exchange(pair_grad(dm, dr, wcat))
+    ret = exchange(outgoing)
     grad_tokens = combine(expert_ids, ret)
     grad_g, grad_u, grad_d = unpack(summed, width // copies, hidden, width, hidden // copies)
     return (grad_tokens, grad_g[None], grad_u[None], grad_d[None])

time: 255 us -> 249 us (0.976)
  local copies, waits for them, and re-layouts: 22.5 us -> 15.9 us
    unnamed x40 -> x28, local copies, waits for them, and re-layouts: 22.5 us -> 15.9 us
    pallas_call x3 -> x1, Pallas kernels: 20.3 us -> 16.9 us  [middle(): pl.pallas_call(middle_kernel, out_shape=(pltpu.HBM((copies, length, 128),...]
  transfers between devices with their start and end apart: 3 -> 3, of which waited for: 2 -> 2; matrix products, arithmetic and copies ran while one was open for 0% -> 0% of each run, Pallas kernels for 7% -> 6%
where the time goes in v2:
time: 249 us; the launch traced here: 248 us
  waiting for transfers between devices  100 us (40%)
  blocking collectives  63.9 us (26%)
  Pallas kernels  37.1 us (15%)
  starting transfers between devices  16.8 us (7%)
  local copies, waits for them, and re-layouts  15.9 us (6%)
  between operations  14.1 us (6%)
    all_to_all x2, waiting for transfers between devices, exchange(): lax.all_to_all(block, 'expert', split_axis=0, concat_axis=0, tiled=True)  100 us
    all_to_all x1, blocking collectives, exchange(): lax.all_to_all(block, 'expert', split_axis=0, concat_axis=0, tiled=True)  63.9 us
    pallas_call x1, Pallas kernels, middle(): pl.pallas_call(middle_kernel, out_shape=(pltpu.HBM((copies, length, 128),...  16.9 us
    all_to_all x2, starting transfers between devices, exchange(): lax.all_to_all(block, 'expert', split_axis=0, concat_axis=0, tiled=True)  16.6 us
    unnamed x28, local copies, waits for them, and re-layouts  15.9 us
    pallas_call x2, Pallas kernels, dispatch(): pl.pallas_call(functools.partial(dispatch_kernel, gates is not None), out...  8.3 us
    pallas_call x1, Pallas kernels, forward(): pl.pallas_call(forward_kernel, out_shape=(jax.ShapeDtypeStruct((mains, 2...  6.56 us
  transfers between devices with their start and end apart: 3, of which 2 were waited for; matrix products, arithmetic and copies ran while one was open for 0% of the time, Pallas kernels for 6%

profile of v2, /device:TPU:1, one launch (start us, length us, event | category | flops | bytes accessed | tf_op | source)
XLA Modules:
  0.0 248.1 jit_solution(44467310232790489)
XLA Ops:
  7.2 0.8 copy.14.refs_0_.ids_ref
  8.0 0.0 copy-start.1
  8.0 1.0 copy-done.1
  9.0 4.1 %dispatch.2 = bf16[32,72,1024]{2,1,0:T(8,128)(2,1)} custom-call(s32[128,8]{1,0:T(8,128)S(1)} %copy.14.refs_0_.ids_ref, bf16[128,2048]{1,0:T(8,128)(2,1)S(1)} %copy-done.1, bf16[128,2048]{1,0:T(8,128)(2,1)S(1)} %copy-done.1), custom_call_target="tpu_custom_call" | custom-call | flops 671088640 | bytes 6291456 | tf_op jit(solution)/shard_map/dispatch/pallas_call | solution.py:101
  13.1 0.0 copy-start.12
  13.1 0.0 copy-start.2
  13.1 8.8 %all-to-all-start.1 = ((bf16[32,72,1024]{2,1,0:T(8,128)(2,1)}), bf16[32,72,1024]{2,1,0:T(8,128)(2,1)}, u32[]{:S(2)}, u32[]{:S(2)}) async-start(bf16[32,72,1024]{2,1,0:T(8,128)(2,1)} %dispatch.2), calls=%async_computation.1 | async-start | bytes 9437184 | tf_op jit(solution)/shard_map/all_to_all | solution.py:372
  21.9 0.0 copy-done.12
  21.9 0.1 copy.13.refs_1_
  22.0 0.0 copy-done.2
  22.0 4.2 %dispatch.3 = bf16[32,72,1024]{2,1,0:T(8,128)(2,1)} custom-call(s32[128,8]{1,0:T(8,128)S(1)} %copy.14.refs_0_.ids_ref, f32[128,8]{1,0:T(8,128)S(1)} %copy.13.refs_1_, bf16[128,2048]{1,0:T(8,128)(2,1)S(1)} %copy-done.2, bf16[128,2048]{1,0:T(8,128)(2,1)S(1)} %copy-done.2), custom_call_target="tpu_custom_call" | custom-call | flops 671088640 | bytes 6291456 | tf_op jit(solution)/shard_map/dispatch/pallas_call | solution.py:101
  26.2 0.0 copy-start.3
  26.2 54.1 %all-to-all-done.1.x_ref = bf16[32,72,1024]{2,1,0:T(8,128)(2,1)} async-done(((bf16[32,72,1024]{2,1,0:T(8,128)(2,1)}), bf16[32,72,1024]{2,1,0:T(8,128)(2,1)}, u32[]{:S(2)}, u32[]{:S(2)}) %all-to-all-start.1) | async-done | bytes 4718624 | tf_op jit(solution)/shard_map/all_to_all | solution.py:372
  80.3 7.8 %all-to-all-start = ((bf16[32,72,1024]{2,1,0:T(8,128)(2,1)}), bf16[32,72,1024]{2,1,0:T(8,128)(2,1)}, u32[]{:S(2)}, u32[]{:S(2)}) async-start(bf16[32,72,1024]{2,1,0:T(8,128)(2,1)} %dispatch.3), calls=%async_computation | async-start | bytes 9437184 | tf_op jit(solution)/shard_map/all_to_all | solution.py:372
  88.1 0.2 reduce-scatter.2.cloned.1.call-start
  88.3 0.0 copy-done.3
  88.3 0.0 copy-start.4
  88.3 1.4 copy-done.4
  89.7 6.6 %forward.1 = (f32[1024,768]{1,0:T(8,128)S(1)}, f32[256,768]{1,0:T(8,128)S(1)}, bf16[1024,384]{1,0:T(8,128)(2,1)S(1)}, bf16[256,384]{1,0:T(8,128)(2,1)S(1)}, bf16[2048,768]{1,0:T(8,128)(2,1)S(1)}) custom-call(bf16[32,72,1024]{2,1,0:T(8,128)(2,1)} %all-to-all-done.1.x_ref, bf16[2048,384]{1,0:T(8,128)(2,1)S(1)} %bitcast.7, bf16[2048,384]{1,0:T(8,128)(2,1)S(1)} %bitcast.8), custom_call_target="tpu_custom_call" | custom-call | flops 4026531840 | bytes 16777216 | tf_op jit(solution)/shard_map/forward/pallas_call | solution.py:159
  96.3 0.0 copy-start.6
  96.3 1.6 copy-done.6
  97.9 0.0 copy-start.8
  97.9 1.6 copy-done.8
  99.5 0.0 copy-start.10
  99.5 0.9 copy-done.10
  100.4 46.2 %all-to-all-done.g_ref = bf16[32,72,1024]{2,1,0:T(8,128)(2,1)} async-done(((bf16[32,72,1024]{2,1,0:T(8,128)(2,1)}), bf16[32,72,1024]{2,1,0:T(8,128)(2,1)}, u32[]{:S(2)}, u32[]{:S(2)}) %all-to-all-start) | async-done | bytes 4718624 | tf_op jit(solution)/shard_map/all_to_all | solution.py:372
  146.6 0.0 copy-start.5
  146.6 1.4 copy-done.5
  148.0 0.0 copy-start.7
  148.0 1.9 copy-done.7
  149.9 0.0 copy-start.9
  149.9 1.9 copy-done.9
  151.8 0.0 copy-start.11
  151.8 1.1 copy-done.11
  152.9 16.9 %middle.1 = (bf16[8,2304,128]{2,1,0:T(8,128)(2,1)}, bf16[32,72,1024]{2,1,0:T(8,128)(2,1)S(1)}) custom-call(bf16[32,72,1024]{2,1,0:T(8,128)(2,1)} %all-to-all-done.g_ref, bf16[32,72,1024]{2,1,0:T(8,128)(2,1)} %all-to-all-done.1.x_ref, bf16[384,2048]{1,0:T(8,128)(2,1)S(1)} %bitcast.9, bf16[2048,768]{1,0:T(8,128)(2,1)S(1)} %copy-done.9, ...), custom_call_target="tpu_custom_call" | custom-call | flops 12079595520 | bytes 29360128 | tf_op jit(solution)/shard_map/middle/pallas_call | solution.py:276
  169.9 0.0 copy-start
  169.9 2.1 copy-done
  172.0 0.0 reduce-scatter.2.cloned.1.call-update
  172.0 63.9 %all_to_all.15.ret_ref = bf16[32,72,1024]{2,1,0:T(8,128)(2,1)S(1)} all-to-all(bf16[32,72,1024]{2,1,0:T(8,128)(2,1)} %copy-done), channel_id=1, replica_groups=mesh['dp'=8,'expert'=32] {'expert'}, dimensions={0} | all-to-all | bytes 9437184 | tf_op jit(solution)/shard_map/all_to_all | solution.py:372
  236.0 3.3 %combine.1 = bf16[128,2048]{1,0:T(8,128)(2,1)} custom-call(s32[128,8]{1,0:T(8,128)S(1)} %copy.14.refs_0_.ids_ref, bf16[32,72,1024]{2,1,0:T(8,128)(2,1)S(1)} %all_to_all.15.ret_ref), custom_call_target="tpu_custom_call" | custom-call | flops 671088640 | bytes 6291456 | tf_op jit(solution)/shard_map/combine/pallas_call | solution.py:352
  239.2 0.0 reduce-scatter.2.cloned.1.call-done
  239.2 2.0 unpack.1
Async XLA Ops:
  8.0 1.0 copy-start.1
  13.1 8.8 %copy-start.12 = (f32[128,8]{0,1:T(8,128)S(1)}, f32[128,8]{0,1:T(8,128)}, u32[]{:S(2)}) copy-start(f32[128,8]{0,1:T(8,128)} %param.9) | copy-start | bytes 12292
  13.1 8.9 %copy-start.2 = (bf16[128,2048]{1,0:T(8,128)(2,1)S(1)}, bf16[128,2048]{1,0:T(8,128)(2,1)}, u32[]{:S(2)}) copy-start(bf16[128,2048]{1,0:T(8,128)(2,1)} %refs_3_) | copy-start | bytes 1572868
  13.1 67.2 %all-to-all-start.1 = ((bf16[32,72,1024]{2,1,0:T(8,128)(2,1)}), bf16[32,72,1024]{2,1,0:T(8,128)(2,1)}, u32[]{:S(2)}, u32[]{:S(2)}) async-start(bf16[32,72,1024]{2,1,0:T(8,128)(2,1)} %dispatch.2), calls=%async_computation.1 | async-start | bytes 9437184 | tf_op jit(solution)/shard_map/all_to_all | solution.py:372
  26.2 62.1 %copy-start.3 = (bf16[1,2048,384]{2,1,0:T(8,128)(2,1)S(1)}, bf16[1,2048,384]{2,1,0:T(8,128)(2,1)}, u32[]{:S(2)}) copy-start(bf16[1,2048,384]{2,1,0:T(8,128)(2,1)} %param.11) | copy-start | bytes 4718596
  80.3 66.3 %all-to-all-start = ((bf16[32,72,1024]{2,1,0:T(8,128)(2,1)}), bf16[32,72,1024]{2,1,0:T(8,128)(2,1)}, u32[]{:S(2)}, u32[]{:S(2)}) async-start(bf16[32,72,1024]{2,1,0:T(8,128)(2,1)} %dispatch.3), calls=%async_computation | async-start | bytes 9437184 | tf_op jit(solution)/shard_map/all_to_all | solution.py:372
  88.1 151.2 %reduce-scatter.2.cloned.1.call-start = ((), (), s32[]{:S(2)}) async-start(), calls=%async_computation.4 | async-start | bytes 5308416 | tf_op jit(solution)/shard_map/reduce_scatter | solution.py:385
  88.3 1.4 copy-start.4
  96.3 1.6 copy-start.6
  97.9 1.6 copy-start.8
  99.5 0.9 copy-start.10
  146.6 1.4 copy-start.5
  148.0 1.9 copy-start.7
  149.9 1.9 copy-start.9
  151.8 1.1 copy-start.11
  169.9 2.1 copy-start
Sparse Core Ops, SparseCore 0:
  172.2 62.8 reduce-scatter.1

commit v3 on v2

v3 whole, which is shorter than its diff:
```python
import functools

import jax
import jax.numpy as jnp
from jax import lax
from jax.experimental import pallas as pl
from jax.experimental.pallas import tpu as pltpu
from jax.sharding import PartitionSpec as P

BF = jnp.bfloat16
F32 = jnp.float32
MIB = 1 << 20

MAIN = 32
REM = 4
PACK = 2 * (MAIN + REM)


def dot(a, b, ca=1, cb=0):
    return lax.dot_general(a, b, (((ca,), (cb,)), ((), ())), preferred_element_type=F32)


def iota(shape, dim):
    return lax.broadcasted_iota(jnp.int32, shape, dim)


def positions(ids, experts):
    top, toks = ids.shape
    ids_t = ids.astype(F32)
    ident = iota((experts, toks), 0).astype(F32)
    member = jnp.zeros((experts, toks), F32)
    for k in range(top):
        member = member + jnp.where(ids_t[k : k + 1, :] == ident, 1.0, 0.0)
    before = (iota((toks, toks), 0) < iota((toks, toks), 1)).astype(F32).astype(BF)
    pos = dot(member.astype(BF), before)
    return jnp.where(member > 0.5, pos, -1.0), ids_t, ident


def select(pos):
    experts, toks = pos.shape
    wide = pos[:, None, :]
    main = (wide == iota((experts, MAIN, toks), 1).astype(F32)).astype(F32)
    rest = (wide == (MAIN + iota((experts, 2 * REM, toks), 1) % REM).astype(F32)).astype(F32)
    return main.reshape(experts * MAIN, toks), rest.reshape(experts * 2 * REM, toks)


def is_left(rows, cols):
    return iota((rows, cols), 0) % (2 * REM) < REM


def prepare_kernel(ids_ref, gates_ref, tokens_hbm, grads_hbm, tokens_out, grads_out, extra_ref, sems):
    width = tokens_hbm.shape[1]
    copies = [
        pltpu.make_async_copy(tokens_hbm, tokens_out.at[:, :width], sems.at[0]),
        pltpu.make_async_copy(grads_hbm, grads_out.at[:, :width], sems.at[1]),
    ]
    for copy in copies:
        copy.start()
    pos, ids_t, ident = positions(ids_ref[...], 32)
    gates_t = gates_ref[...]
    weight = jnp.zeros(pos.shape, F32)
    for k in range(gates_t.shape[0]):
        weight = weight + jnp.where(ids_t[k : k + 1, :] == ident, gates_t[k : k + 1, :], 0.0)
    high = weight.astype(BF).astype(F32)
    mid = (weight - high).astype(BF).astype(F32)
    low = weight - high - mid
    extra_ref[...] = jnp.concatenate([pos, high, mid, low], axis=0).T.astype(BF)
    for n, dst in enumerate((tokens_out, grads_out)):
        copies.append(pltpu.make_async_copy(extra_ref, dst.at[:, width:], sems.at[2 + n]))
        copies[-1].start()
    for copy in copies:
        copy.wait()


HBM = pl.BlockSpec(memory_space=pltpu.HBM)
VMEM = pl.BlockSpec(memory_space=pltpu.VMEM)


def prepare(ids, gates, tokens, grads):
    toks, width = tokens.shape
    shape = pltpu.HBM((toks, width + 128), BF)
    return pl.pallas_call(
        prepare_kernel,
        out_shape=(shape, shape),
        in_specs=[VMEM, VMEM, HBM, HBM],
        out_specs=(HBM, HBM),
        scratch_shapes=[pltpu.VMEM((toks, 128), BF), pltpu.SemaphoreType.DMA((4,))],
        compiler_params=pltpu.CompilerParams(vmem_limit_bytes=16 * MIB),
        cost_estimate=pl.CostEstimate(flops=1 << 20, bytes_accessed=2 * MIB, transcendentals=0),
        name="prepare",
    )(ids, gates, tokens, grads)


def dispatch_kernel(scaled, per, wanted_ref, slot_ref, *refs):
    lines = 4
    sources = refs[:lines]
    count = 8 if scaled else 1
    outs = refs[lines : lines + count]
    data_ref, s_ref, out_ref, scale_ref, in_sems, out_sems = refs[lines + count :]
    experts, rows, width = out_ref.shape
    toks = sources[0].shape[0]

    loads = [
        pltpu.make_async_copy(src, data_ref.at[k * toks : (k + 1) * toks, :], in_sems.at[k])
        for k, src in enumerate(sources)
    ]
    for load in loads:
        load.start()
    for load in loads:
        load.wait()

    extra = data_ref[:, width:]
    wanted = wanted_ref[...]
    lane = iota(wanted.shape, 1)

    def column(piece):
        pick = (lane == wanted + piece * 32).astype(F32).astype(BF)
        return dot(pick, extra, 1, 1)

    pos = column(0)
    target = jnp.where(pos >= 0.0, pos + slot_ref[0:1, :].astype(F32) * float(per), -1.0)
    chosen = target[:, None, :] == iota((experts, rows, lines * toks), 1).astype(F32)
    chosen = chosen.astype(F32)
    s_ref[...] = chosen.reshape(experts * rows, lines * toks).astype(BF)
    if scaled:
        weight = column(1) + (column(2) + column(3))
        total = jnp.sum(chosen * weight[:, None, :], axis=2, keepdims=True)
        scale_ref[...] = jnp.broadcast_to(total, (experts, rows, 128)).reshape(experts * rows, 128)

    stores = []
    parts = 4
    columns = width // parts
    for c in range(parts):
        cols = slice(c * columns, (c + 1) * columns)
        got = dot(s_ref[...], data_ref[:, cols])
        if scaled:
            got = got * jnp.concatenate([scale_ref[...]] * (columns // 128), axis=1)
        out_ref[:, :, cols] = got.astype(BF).reshape(experts, rows, columns)
        for k, out in enumerate(outs):
            here, there = (out_ref.at[k], out) if scaled else (out_ref, out)
            at = (slice(None),) * (len(there.shape) - 1) + (cols,)
            stores.append(pltpu.make_async_copy(here.at[at], there.at[at], out_sems.at[c * count + k]))
            stores[-1].start()
    for store in stores:
        store.wait()


def dispatch(wanted, slots, lines, scaled):
    toks, width = lines[0].shape[0], lines[0].shape[1] - 128
    per, experts = MAIN + REM, 8
    rows, all_toks = len(lines) * per, len(lines) * toks
    shapes = (pltpu.HBM((rows, width), BF),) * experts if scaled else (pltpu.HBM((experts, rows, width), BF),)
    return pl.pallas_call(
        functools.partial(dispatch_kernel, scaled, per),
        out_shape=shapes,
        in_specs=[VMEM, VMEM] + [HBM] * len(lines),
        out_specs=(HBM,) * len(shapes),
        scratch_shapes=[
            pltpu.VMEM((all_toks, width + 128), BF),
            pltpu.VMEM((experts * rows, all_toks), BF),
            pltpu.VMEM((experts, rows, width), BF),
            pltpu.VMEM((experts * rows, 128), F32),
            pltpu.SemaphoreType.DMA((len(lines),)),
            pltpu.SemaphoreType.DMA((4 * len(shapes),)),
        ],
        compiler_params=pltpu.CompilerParams(vmem_limit_bytes=32 * MIB),
        cost_estimate=pl.CostEstimate(
            flops=2 * experts * rows * all_toks * width, bytes_accessed=7 * MIB, transcendentals=0
        ),
        name="dispatch",
    )(wanted, slots, *lines)


def regrouped(block):
    return block % 4 * 8 + block // 4 % 2 * 4 + block // 8


def forward_kernel(*refs):
    blocks, wg_hbm, wu_hbm = refs[:3]
    cs_hbm, act_hbm, wcat_hbm = refs[3:6]
    x_ref, wcat_ref, cs_ref, act_ref, turn_ref, at_ref, sems = refs[6:]
    rows = blocks.shape[1]
    hidden = wg_hbm.shape[1]
    loads = [
        pltpu.make_async_copy(wg_hbm, wcat_ref.at[:, :hidden], sems.at[8]),
        pltpu.make_async_copy(wu_hbm, wcat_ref.at[:, hidden:], sems.at[9]),
    ]
    loads += [
        pltpu.make_async_copy(blocks.at[k], x_ref.at[k * rows : (k + 1) * rows, :], sems.at[k]) for k in range(8)
    ]
    for load in loads:
        load.start()
    loads[0].wait()
    loads[1].wait()
    stores = [pltpu.make_async_copy(wcat_ref, wcat_hbm, sems.at[10])]
    stores[0].start()
    parts = 2
    most = 8 // parts * rows
    for i in range(parts):
        for load in loads[2 + i * 8 // parts : 2 + (i + 1) * 8 // parts]:
            load.wait()
        some = slice(i * most, (i + 1) * most)
        pre = dot(x_ref[some, :], wcat_ref[...])
        gate, up = pre[:, :hidden], pre[:, hidden:]
        sigma = jax.nn.sigmoid(gate)
        silu = gate * sigma
        cs_ref[some, :hidden] = up * sigma * (1.0 + gate * (1.0 - sigma))
        cs_ref[some, hidden:] = silu
        act_ref[some, :] = silu * up
        store = pltpu.make_async_copy(cs_ref.at[some, :], cs_hbm.at[some, :], sems.at[11 + i])
        store.start()
        stores.append(store)
    per = MAIN + REM
    for b in range(32):
        to = regrouped(b)
        turn_ref[to * per : (to + 1) * per, :] = act_ref[b * per : (b + 1) * per, :]
    at_ref[...] = turn_ref[...].astype(BF).T
    stores.append(pltpu.make_async_copy(at_ref, act_hbm, sems.at[13]))
    stores[-1].start()
    for store in stores:
        store.wait()


def forward(blocks, wg, wu):
    width, hidden = wg.shape
    rows = 8 * blocks.shape[1]
    return pl.pallas_call(
        forward_kernel,
        out_shape=(
            pltpu.HBM((rows, 2 * hidden), F32),
            pltpu.HBM((hidden, rows), BF),
            pltpu.HBM((width, 2 * hidden), BF),
        ),
        in_specs=[HBM] * 3,
        out_specs=(HBM,) * 3,
        scratch_shapes=[
            pltpu.VMEM((rows, width), BF),
            pltpu.VMEM((width, 2 * hidden), BF),
            pltpu.VMEM((rows, 2 * hidden), F32),
            pltpu.VMEM((rows, hidden), F32),
            pltpu.VMEM((rows, hidden), F32),
            pltpu.VMEM((hidden, rows), BF),
            pltpu.SemaphoreType.DMA((14,)),
        ],
        compiler_params=pltpu.CompilerParams(vmem_limit_bytes=36 * MIB),
        cost_estimate=pl.CostEstimate(
            flops=2 * rows * width * 2 * hidden, bytes_accessed=16 * MIB, transcendentals=rows * hidden
        ),
        name="forward",
    )(blocks, wg, wu)


def middle_kernel(*refs):
    to_ref, at_row_ref, gs, xs = refs[0], refs[1], refs[2:10], refs[10]
    wd_hbm, wcat_hbm, cs_hbm, act_hbm = refs[11:15]
    packed_hbm, pair_hbm = refs[15:17]
    (g_ref, x_ref, wd_ref, wcat_ref, cs_ref, at_ref, raw_ref, turn_ref, d_ref, dt_ref, dm_ref, dr_ref, packed_ref,
     pair_ref, sems, out_sems) = refs[17:]
    rows = gs[0].shape[0]
    copies = packed_ref.shape[0]
    n, _, half = pair_ref.shape
    hidden, both = at_ref.shape[0], wcat_ref.shape[1]
    per_block = MAIN + REM

    def load(src, dst, sem):
        copy = pltpu.make_async_copy(src, dst, sems.at[sem])
        copy.start()
        return copy

    wd_in = load(wd_hbm, wd_ref, 16)
    g_in = [
        load(b, g_ref.at[pl.ds(pl.multiple_of(at_row_ref[k], 16), rows), :], k) for k, b in enumerate(gs)
    ]
    cs_in = load(cs_hbm, cs_ref, 17)
    x_in = [load(xs.at[k], x_ref.at[k * rows : (k + 1) * rows, :], 8 + k) for k in range(8)]
    act_in = load(act_hbm, at_ref, 18)
    wcat_in = load(wcat_hbm, wcat_ref, 19)

    wd_in.wait()
    parts = 4
    most = 8 // parts * rows
    for i in range(parts):
        for copy in g_in[i * 8 // parts : (i + 1) * 8 // parts]:
            copy.wait()
        some = slice(i * most, (i + 1) * most)
        raw_ref[some, :] = dot(g_ref[some, :], wd_ref[...], 1, 1)
    for b in range(n):
        to = regrouped(b)
        turn_ref[to * per_block : (to + 1) * per_block, :] = raw_ref[b * per_block : (b + 1) * per_block, :]
    cs_in.wait()
    for i in range(parts):
        some = slice(i * most, (i + 1) * most)
        d_act = turn_ref[some, :]
        grad = jnp.concatenate([d_act, d_act], axis=1) * cs_ref[some, :]
        d_ref[some, :] = grad
    dt_ref[...] = d_ref[...].astype(BF).T
    dr_ref[...] = jnp.zeros_like(dr_ref)
    for b in range(n):
        dm_ref[b * MAIN : (b + 1) * MAIN, :] = d_ref[b * per_block : b * per_block + MAIN, :].astype(BF)
        dr_ref[b * 2 * REM : b * 2 * REM + REM, :] = d_ref[b * per_block + MAIN : (b + 1) * per_block, :]

    for copy in x_in:
        copy.wait()
    act_in.wait()
    tile = 256
    per = 2 * half // copies
    slab = hidden // copies
    base = both * per // 128
    for j in range(2 * half // tile):
        cols = slice(j * tile, (j + 1) * tile)
        into = dot(dt_ref[...], x_ref[:, cols]).astype(BF)
        down = dot(at_ref[...], g_ref[:, cols]).astype(BF)
        for q in range(tile // 128):
            at = j * tile // 128 + q
            owner, piece = at * 128 // per, at % (per // 128)
            part = into[:, q * 128 : (q + 1) * 128]
            packed_ref[owner, piece * both : (piece + 1) * both, :] = part
            part = down[:, q * 128 : (q + 1) * 128].reshape(copies, slab, 128)
            packed_ref[:, base + at * slab : base + (at + 1) * slab, :] = part
    packed_out = pltpu.make_async_copy(packed_ref, packed_hbm, out_sems.at[n])
    packed_out.start()

    wcat_in.wait()
    sent = []
    step = n // parts
    most, few = step * MAIN, step * 2 * REM
    for i in range(parts):
        main = dm_ref[i * most : (i + 1) * most, :]
        rest = dr_ref[i * few : (i + 1) * few, :]
        d_left = jnp.concatenate([main, rest.astype(BF)], axis=0)
        d_right = jnp.concatenate([main, pltpu.roll(rest, REM, 0).astype(BF)], axis=0)
        y_left = dot(d_left, wcat_ref[:half, :], 1, 1)
        y_right = dot(d_right, wcat_ref[half:, :], 1, 1)
        some = slice(i * step, (i + 1) * step)
        pair_ref[some, 0:MAIN, :] = y_left[:most].astype(BF).reshape(step, MAIN, half)
        pair_ref[some, MAIN : 2 * MAIN, :] = y_right[:most].astype(BF).reshape(step, MAIN, half)
        tail = (y_left[most:] + y_right[most:]).astype(BF)
        pair_ref[some, 2 * MAIN : PACK, :] = tail.reshape(step, 2 * REM, half)
        for b in range(i * step, (i + 1) * step):
            copy = pltpu.make_async_copy(pair_ref.at[b], pair_hbm.at[to_ref[b]], out_sems.at[b])
            copy.start()
            sent.append(copy)
    for copy in sent:
        copy.wait()
    packed_out.wait()


def middle(to, at_row, gs, xs, wd, wcat, cs, act, copies):
    hidden, width = wd.shape
    both, rows = cs.shape[1], cs.shape[0]
    n, half = to.shape[0], width // 2
    length = 3 * hidden * width // copies // 128
    smem = pl.BlockSpec(memory_space=pltpu.SMEM)
    return pl.pallas_call(
        middle_kernel,
        out_shape=(pltpu.HBM((copies, length, 128), BF), pltpu.HBM((n, PACK, half), BF)),
        in_specs=[smem] * 2 + [HBM] * 13,
        out_specs=(HBM,) * 2,
        scratch_shapes=[
            pltpu.VMEM((rows, width), BF),
            pltpu.VMEM((rows, width), BF),
            pltpu.VMEM((hidden, width), BF),
            pltpu.VMEM((width, both), BF),
            pltpu.VMEM((rows, both), F32),
            pltpu.VMEM((hidden, rows), BF),
            pltpu.VMEM((rows, hidden), F32),
            pltpu.VMEM((rows, hidden), F32),
            pltpu.VMEM((rows, both), F32),
            pltpu.VMEM((both, rows), BF),
            pltpu.VMEM((n * MAIN, both), BF),
            pltpu.VMEM((n * 2 * REM, both), F32),
            pltpu.VMEM((copies, length, 128), BF),
            pltpu.VMEM((n, PACK, half), BF),
            pltpu.SemaphoreType.DMA((20,)),
            pltpu.SemaphoreType.DMA((n + 1,)),
        ],
        compiler_params=pltpu.CompilerParams(vmem_limit_bytes=50 * MIB),
        cost_estimate=pl.CostEstimate(flops=2 * rows * width * 6 * hidden, bytes_accessed=28 * MIB, transcendentals=0),
        name="middle",
    )(to, at_row, *gs, xs, wd, wcat, cs, act)


def unpack_kernel(in_ref, gate_ref, up_ref, down_ref):
    per, hidden = gate_ref.shape
    slab = down_ref.shape[0]
    base = 2 * hidden * per // 128
    for q in range(per // 128):
        both = in_ref[q * 2 * hidden : (q + 1) * 2 * hidden, :].T
        gate_ref[q * 128 : (q + 1) * 128, :] = both[:, :hidden]
        up_ref[q * 128 : (q + 1) * 128, :] = both[:, hidden:]
    for q in range(down_ref.shape[1] // 128):
        down_ref[:, q * 128 : (q + 1) * 128] = in_ref[base + q * slab : base + (q + 1) * slab, :]


def unpack(summed, per, hidden, width, slab):
    vmem = pl.BlockSpec(memory_space=pltpu.VMEM)
    return pl.pallas_call(
        unpack_kernel,
        out_shape=(
            jax.ShapeDtypeStruct((per, hidden), BF),
            jax.ShapeDtypeStruct((per, hidden), BF),
            jax.ShapeDtypeStruct((slab, width), BF),
        ),
        in_specs=[vmem],
        out_specs=(vmem, vmem, vmem),
        cost_estimate=pl.CostEstimate(flops=0, bytes_accessed=2 * MIB, transcendentals=0),
        name="unpack",
    )(summed)


def combine_kernel(ids_ref, ret_ref, out_ref, main_ref, rest_ref):
    experts, _, cols = ret_ref.shape
    toks = out_ref.shape[0]
    half = out_ref.shape[1] // 2
    c = pl.program_id(0)

    @pl.when(c == 0)
    def _():
        pos, _, _ = positions(ids_ref[...], experts)
        main, rest = select(pos)
        left = is_left(*rest.shape)
        main_ref[...] = main.T.astype(BF)
        rest_ref[0] = jnp.where(left, rest, 0.0).T.astype(BF)
        rest_ref[1] = jnp.where(left, 0.0, rest).T.astype(BF)

    tail = ret_ref[:, 2 * MAIN : PACK, :].reshape(experts * 2 * REM, cols)
    for side in range(2):
        body = ret_ref[:, side * MAIN : (side + 1) * MAIN, :].reshape(experts * MAIN, cols)
        total = dot(main_ref[...], body) + dot(rest_ref[side], tail)
        out_ref[:, pl.ds(pl.multiple_of(side * half + c * cols, 128), cols)] = total.astype(BF)


def combine(ids, ret):
    experts, _, half = ret.shape
    toks = ids.shape[1]
    steps = 4
    cols = half // steps
    return pl.pallas_call(
        combine_kernel,
        out_shape=jax.ShapeDtypeStruct((toks, 2 * half), BF),
        grid=(steps,),
        in_specs=[
            pl.BlockSpec(ids.shape, lambda c: (0, 0)),
            pl.BlockSpec((experts, PACK, cols), lambda c: (0, 0, c)),
        ],
        out_specs=pl.BlockSpec((toks, 2 * half), lambda c: (0, 0)),
        scratch_shapes=[
            pltpu.VMEM((toks, experts * MAIN), BF),
            pltpu.VMEM((2, toks, experts * 2 * REM), BF),
        ],
        compiler_params=pltpu.CompilerParams(vmem_limit_bytes=24 * MIB),
        cost_estimate=pl.CostEstimate(flops=2 * 1280 * toks * 2 * half, bytes_accessed=6 * MIB, transcendentals=0),
        name="combine",
    )(ids, ret)


SIDE = 4
CORES = 2
SHIFTS = [(d, f) for d in range(SIDE) for f in range(CORES)]


def place(x, y, core):
    return (x % SIDE * SIDE + y % SIDE) * CORES + core


def moved(value, dx, dy, flip):
    if dx == dy == flip == 0:
        return value
    pairs = []
    for x in range(SIDE):
        for y in range(SIDE):
            for core in range(CORES):
                pairs.append((place(x, y, core), place(x + dx, y + dy, core ^ flip)))
    return lax.ppermute(value, "expert", pairs)


def shards(tokens, grad_out, gates, expert_ids, w_gate, w_up, w_down):
    copies = lax.axis_size("dp")
    wg, wu, wd = w_gate[0], w_up[0], w_down[0]
    width, hidden = wg.shape
    me = lax.axis_index("expert")
    x, y, core = me // (SIDE * CORES), me // CORES % SIDE, me % CORES
    wide = lambda values: jnp.broadcast_to(jnp.stack(values).astype(jnp.int32)[:, None], (len(values), 128))
    along_y = wide([place(x, d, f) for d, f in SHIFTS])
    along_x = wide([place(x + d, y, core ^ f) for d, f in SHIFTS])
    toks = tokens.shape[0]
    near = jnp.arange(SIDE, dtype=jnp.int32)
    slots_x = jnp.broadcast_to(jnp.repeat(near, toks)[None, :], (8, SIDE * toks))
    slots_g = jnp.broadcast_to(jnp.repeat((y - near + SIDE) % SIDE, toks)[None, :], (8, SIDE * toks))
    origin = jnp.stack([place(x - d + SIDE, b, f) for b, f in SHIFTS for d in range(SIDE)]).astype(jnp.int32)
    at_row = jnp.stack([(d * CORES + (core ^ f)) * SIDE * (MAIN + REM) for d, f in SHIFTS]).astype(jnp.int32)

    ids_t = expert_ids.T
    tokens, grad_out = prepare(ids_t, gates.T, tokens, grad_out)
    lines_x = [moved(tokens, d, 0, 0) for d in range(SIDE)]
    lines_g = [moved(grad_out, 0, d, 0) for d in range(SIDE)]
    lines_x, lines_g = lax.optimization_barrier((lines_x, lines_g))
    (out_x,) = dispatch(along_y, slots_x, lines_x, False)
    columns = [[place(a, b, f) for b in range(SIDE) for f in range(CORES)] for a in range(SIDE)]
    xs = lax.all_to_all(out_x, "expert", split_axis=0, concat_axis=0, axis_index_groups=columns, tiled=True)
    along_x, _ = lax.optimization_barrier((along_x, out_x))
    out_g = dispatch(along_x, slots_g, lines_g, True)
    gs = [moved(v, d, 0, f) for v, (d, f) in zip(out_g, SHIFTS)]
    cs, act, wcat = forward(xs, wg, wu)
    packed, outgoing = middle(origin, at_row, gs, xs, wd, wcat, cs, act, copies)
    summed = lax.psum_scatter(packed, "dp", scatter_dimension=0, tiled=True)[0]
    ret = lax.all_to_all(outgoing, "expert", split_axis=0, concat_axis=0, tiled=True)
    grad_tokens = combine(ids_t, ret)
    grad_g, grad_u, grad_d = unpack(summed, width // copies, hidden, width, hidden // copies)
    return (grad_tokens, grad_g[None], grad_u[None], grad_d[None])


def solution(mesh):
    rows = P(("dp", "expert"), None)
    weights = P("expert", None, None)
    cut = P("expert", "dp", None)
    return jax.shard_map(
        shards,
        mesh=mesh,
        in_specs=(rows, rows, rows, rows, weights, weights, weights),
        out_specs=(rows, cut, cut, cut),
        check_vma=False,
    )
```

time: 249 us -> 227 us (0.912)
  waiting for transfers between devices: 100 us -> 58.8 us
  starting transfers between devices: 16.8 us -> 33.9 us
  Pallas kernels: 37.1 us -> 43.3 us
  local copies, waits for them, and re-layouts: 15.9 us -> 11.6 us
    all_to_all x2 -> x1, waiting for transfers between devices: 100 us -> 19.9 us  [shards(): lax.all_to_all(out_x, 'expert', split_axis=0, concat_axis=0, axis_index_g...]
    ppermute x0 -> x13, waiting for transfers between devices: none -> 38.9 us  [moved(): return lax.ppermute(value, 'expert', pairs)]
    ppermute x0 -> x13, starting transfers between devices: none -> 21.8 us  [moved(): return lax.ppermute(value, 'expert', pairs)]
    pallas_call x3 -> x4, Pallas kernels: 14.9 us -> 20 us  [the longest x1 10.1 us: forward(): pl.pallas_call(forward_kernel, out_shape=(pltpu.HBM((rows, 2 * hidden), F...]
    unnamed x28 -> x40, local copies, waits for them, and re-layouts: 15.9 us -> 11 us
    all_to_all x2 -> x1, starting transfers between devices: 16.6 us -> 12 us  [shards(): lax.all_to_all(out_x, 'expert', split_axis=0, concat_axis=0, axis_index_g...]
  transfers between devices with their start and end apart: 3 -> 15, of which waited for: 2 -> 7; matrix products, arithmetic and copies ran while one was open for 0% -> 0% of each run, Pallas kernels for 6% -> 8%
where the time goes in v3:
time: 227 us; the launch traced here: 226 us
  blocking collectives  64.6 us (28%)
  waiting for transfers between devices  58.8 us (26%)
  Pallas kernels  43.3 us (19%)
  starting transfers between devices  33.9 us (15%)
  between operations  14.3 us (6%)
  local copies, waits for them, and re-layouts  11.6 us (5%)
    all_to_all x1, blocking collectives, shards(): lax.all_to_all(outgoing, 'expert', split_axis=0, concat_axis=0, tiled=True)  64.6 us
    ppermute x13, waiting for transfers between devices, moved(): return lax.ppermute(value, 'expert', pairs)  38.9 us
    ppermute x13, starting transfers between devices, moved(): return lax.ppermute(value, 'expert', pairs)  21.8 us
    all_to_all x1, waiting for transfers between devices, shards(): lax.all_to_all(out_x, 'expert', split_axis=0, concat_axis=0, axis_index_g...  19.9 us
    pallas_call x1, Pallas kernels, middle(): pl.pallas_call(middle_kernel, out_shape=(pltpu.HBM((copies, length, 128),...  18.1 us
    all_to_all x1, starting transfers between devices, shards(): lax.all_to_all(out_x, 'expert', split_axis=0, concat_axis=0, axis_index_g...  12 us
    unnamed x40, local copies, waits for them, and re-layouts  11 us
    pallas_call x1, Pallas kernels, forward(): pl.pallas_call(forward_kernel, out_shape=(pltpu.HBM((rows, 2 * hidden), F...  10.1 us
  transfers between devices with their start and end apart: 15, of which 7 were waited for; matrix products, arithmetic and copies ran while one was open for 0% of the time, Pallas kernels for 8%

profile of v3, /device:TPU:1, one launch (start us, length us, event | category | flops | bytes accessed | tf_op | source)
XLA Modules:
  0.0 226.5 jit_solution(5531316548256227038)
XLA Ops:
  7.2 1.0 copy-done
  8.2 1.0 copy-done.1
  9.3 0.7 copy-done.2
  9.9 0.7 copy-done.4
  10.6 1.1 prepare.1
  11.7 3.4 %collective-permute-start.2 = (bf16[128,2176]{1,0:T(8,128)(2,1)}, bf16[128,2176]{1,0:T(8,128)(2,1)S(1)}, u32[]{:S(2)}, u32[]{:S(2)}) collective-permute-start(bf16[128,2176]{1,0:T(8,128)(2,1)} %get-tuple-element.33.refs_0_), channel_id=1, source_target_pairs={{0,24},{1,25},{2,26},{3,27},{4,28},{5,29},{6,30},{7,31},{8,0},{9,1... | collective-permute-start | bytes 1671176 | tf_op jit(solution)/shard_map/ppermute | solution.py:474
  15.1 0.5 collective-permute-start.1
  15.6 0.6 collective-permute-start
  16.2 2.7 %collective-permute-start.5 = (bf16[128,2176]{1,0:T(8,128)(2,1)}, bf16[128,2176]{1,0:T(8,128)(2,1)S(1)}, u32[]{:S(2)}, u32[]{:S(2)}) collective-permute-start(bf16[128,2176]{1,0:T(8,128)(2,1)} %get-tuple-element.38.refs_0_), channel_id=1, source_target_pairs={{0,6},{1,7},{2,0},{3,1},{4,2},{5,3},{6,4},{7,5},{8,14},{9,15},{10,... | collective-permute-start | bytes 1671176 | tf_op jit(solution)/shard_map/ppermute | solution.py:474
  18.9 0.3 collective-permute-start.4
  19.3 10.4 %collective-permute-done.2.refs_3_ = bf16[128,2176]{1,0:T(8,128)(2,1)S(1)} collective-permute-done((bf16[128,2176]{1,0:T(8,128)(2,1)}, bf16[128,2176]{1,0:T(8,128)(2,1)S(1)}, u32[]{:S(2)}, u32[]{:S(2)}) %collective-permute-start.2) | collective-permute-done | bytes 557088 | tf_op jit(solution)/shard_map/ppermute | solution.py:474
  29.7 0.1 stack.239
  29.8 0.2 collective-permute-done.1.refs_2_
  30.0 13.3 %collective-permute-done.refs_1_ = bf16[128,2176]{1,0:T(8,128)(2,1)S(1)} collective-permute-done((bf16[128,2176]{1,0:T(8,128)(2,1)}, bf16[128,2176]{1,0:T(8,128)(2,1)S(1)}, u32[]{:S(2)}, u32[]{:S(2)}) %collective-permute-start) | collective-permute-done | bytes 557088 | tf_op jit(solution)/shard_map/ppermute | solution.py:474
  43.3 0.1 broadcast_in_dim.42.wanted_ref
  43.4 1.5 copy-done.18
  44.9 4.2 %dispatch.2 = bf16[8,144,2048]{2,1,0:T(8,128)(2,1)} custom-call(s32[8,128]{1,0:T(8,128)S(1)} %broadcast_in_dim.42.wanted_ref, s32[8,512]{1,0:T(8,128)S(1)} %broadcast_in_dim.45.slot_ref, bf16[128,2176]{1,0:T(8,128)(2,1)S(1)} %copy-done.18, bf16[128,2176]{1,0:T(8,128)(2,1)S(1)} %collective-permute-done.refs_1_, ...), custom_call_target="tpu_custom_call" | custom-call | flops 2415919104 | bytes 7340032 | tf_op jit(solution)/shard_map/dispatch/pallas_call | solution.py:153
  49.1 12.0 %all-to-all-start = ((bf16[8,144,2048]{2,1,0:T(8,128)(2,1)}), bf16[8,144,2048]{2,1,0:T(8,128)(2,1)}, u32[]{:S(2)}, u32[]{:S(2)}) async-start(bf16[8,144,2048]{2,1,0:T(8,128)(2,1)} %dispatch.2), calls=%async_computation | async-start | bytes 9437184 | tf_op jit(solution)/shard_map/all_to_all | solution.py:500
  61.2 0.0 reduce-scatter.2.cloned.1.call-start
  61.3 0.1 stack.230
  61.4 0.1 broadcast_bitcast_fusion
  61.5 0.1 broadcast_in_dim.41.wanted_ref
  61.6 1.3 copy-done.11
  62.8 1.1 copy-done.13
  63.9 1.1 copy-done.15
  64.9 1.1 copy-done.17
  66.0 4.6 %dispatch.3 = (bf16[144,2048]{1,0:T(8,128)(2,1)}, bf16[144,2048]{1,0:T(8,128)(2,1)}, bf16[144,2048]{1,0:T(8,128)(2,1)}, bf16[144,2048]{1,0:T(8,128)(2,1)}, bf16[...) custom-call(s32[8,128]{1,0:T(8,128)S(1)} %broadcast_in_dim.41.wanted_re, ...), custom_call_target="tpu_custom_call" | custom-call | flops 2415919104 | bytes 7340032 | tf_op jit(solution)/shard_map/dispatch/pallas_call | solution.py:153
  70.6 0.3 collective-permute-start.6
  70.9 0.0 collective-permute-start.8
  70.9 8.7 %collective-permute-start.9 = (bf16[144,2048]{1,0:T(8,128)(2,1)}, bf16[144,2048]{1,0:T(8,128)(2,1)}, u32[]{:S(2)}, u32[]{:S(2)}) collective-permute-start(bf16[144,2048]{1,0:T(8,128)(2,1)} %get-tuple-element.46), channel_id=1, source_target_pairs={{0,16},{1,17},{2,18},{3,19},{4,20},{5,21},{6,22},{7,23},{8,24},{9,... | collective-permute-start | bytes 1769480 | tf_op jit(solution)/shard_map/ppermute | solution.py:474
  79.6 0.3 collective-permute-start.10
  79.9 0.8 copy-done.7
  80.7 2.0 collective-permute-start.11
  82.8 9.2 %collective-permute-done.7.refs_4_ = bf16[144,2048]{1,0:T(8,128)(2,1)S(1)} collective-permute-done((bf16[144,2048]{1,0:T(8,128)(2,1)}, bf16[144,2048]{1,0:T(8,128)(2,1)S(1)}, u32[]{:S(2)}, u32[]{:S(2)}) %collective-permute-start.7) | collective-permute-done | bytes 589856 | tf_op jit(solution)/shard_map/ppermute | solution.py:474
  91.9 0.8 copy-done.9
  92.7 2.9 %collective-permute-start.12 = (bf16[144,2048]{1,0:T(8,128)(2,1)}, bf16[144,2048]{1,0:T(8,128)(2,1)}, u32[]{:S(2)}, u32[]{:S(2)}) collective-permute-start(bf16[144,2048]{1,0:T(8,128)(2,1)} %get-tuple-element.49), channel_id=1, source_target_pairs={{0,25},{1,24},{2,27},{3,26},{4,29},{5,28},{6,31},{7,30},{8,1},{9,0... | collective-permute-start | bytes 1769480 | tf_op jit(solution)/shard_map/ppermute | solution.py:474
  95.6 0.1 stack.221.refs_1_
  95.7 0.1 stack.212.refs_0_
  95.8 19.9 %all-to-all-done.refs_0_.refs_10_ = bf16[8,144,2048]{2,1,0:T(8,128)(2,1)} async-done(((bf16[8,144,2048]{2,1,0:T(8,128)(2,1)}), bf16[8,144,2048]{2,1,0:T(8,128)(2,1)}, u32[]{:S(2)}, u32[]{:S(2)}) %all-to-all-start) | async-done | bytes 4718624 | tf_op jit(solution)/shard_map/all_to_all | solution.py:500
  115.7 10.1 %forward.1 = (f32[1152,768]{1,0:T(8,128)}, bf16[384,1152]{1,0:T(8,128)(2,1)}, bf16[2048,768]{1,0:T(8,128)(2,1)}) custom-call(bf16[8,144,2048]{2,1,0:T(8,128)(2,1)} %all-to-all-done.refs_0_.refs_10_, bf16[2048,384]{1,0:T(8,128)(2,1)S(1)} %bitcast.72, bf16[2048,384]{1,0:T(8,128)(2,1)S(1)} %bitcast.73), custom_call_target="tpu_custom_call" | custom-call | flops 3623878656 | bytes 16777216 | tf_op jit(solution)/shard_map/forward/pallas_call | solution.py:227
  125.9 5.3 %collective-permute-done.10.refs_7_ = bf16[144,2048]{1,0:T(8,128)(2,1)} collective-permute-done((bf16[144,2048]{1,0:T(8,128)(2,1)}, bf16[144,2048]{1,0:T(8,128)(2,1)}, u32[]{:S(2)}, u32[]{:S(2)}) %collective-permute-start.10) | collective-permute-done | bytes 589856 | tf_op jit(solution)/shard_map/ppermute | solution.py:474
  131.2 0.5 collective-permute-done.12.refs_9_
  131.7 18.1 %middle.1 = (bf16[8,2304,128]{2,1,0:T(8,128)(2,1)}, bf16[32,72,1024]{2,1,0:T(8,128)(2,1)}) custom-call(s32[32]{0:T(128)S(1)} %stack.212.refs_0_, s32[8]{0:T(128)S(1)} %stack.221.refs_1_, bf16[144,2048]{1,0:T(8,128)(2,1)S(1)} %copy-done.19, bf16[144,2048]{1,0:T(8,128)(2,1)S(1)} %copy-done.8, bf16[144,2048]{1,0:T(8,128)(2,1)S(1)} %copy-done.10, ...), custom_call_target="tpu_custom_call" | custom-call | flops 10871635968 | bytes 29360128 | tf_op jit(solution)/shard_map/middle/pallas_call | solution.py:354
  149.8 0.0 reduce-scatter.2.cloned.1.call-update
  149.8 0.0 copy-start.3
  149.8 64.6 %all_to_all.10.ret_ref = bf16[32,72,1024]{2,1,0:T(8,128)(2,1)S(1)} all-to-all(bf16[32,72,1024]{2,1,0:T(8,128)(2,1)} %get-tuple-element.53), channel_id=1, replica_groups=mesh['dp'=8,'expert'=32] {'expert'}, dimensions={0} | all-to-all | bytes 9437184 | tf_op jit(solution)/shard_map/all_to_all | solution.py:507
  214.4 3.2 %combine.1 = bf16[128,2048]{1,0:T(8,128)(2,1)} custom-call(s32[8,128]{1,0:T(8,128)S(1)} %bitcast.70, bf16[32,72,1024]{2,1,0:T(8,128)(2,1)S(1)} %all_to_all.10.ret_ref), custom_call_target="tpu_custom_call" | custom-call | flops 671088640 | bytes 6291456 | tf_op jit(solution)/shard_map/combine/pallas_call | solution.py:438
  217.6 2.0 unpack.1
  (42 shorter events, 0.1 us)
Async XLA Ops:
  7.2 1.0 copy-start
  8.2 1.0 copy-start.1
  9.2 0.7 copy-start.2
  9.9 0.7 copy-start.4
  11.7 18.0 %collective-permute-start.2 = (bf16[128,2176]{1,0:T(8,128)(2,1)}, bf16[128,2176]{1,0:T(8,128)(2,1)S(1)}, u32[]{:S(2)}, u32[]{:S(2)}) collective-permute-start(bf16[128,2176]{1,0:T(8,128)(2,1)} %get-tuple-element.33.refs_0_), channel_id=1, source_target_pairs={{0,24},{1,25},{2,26},{3,27},{4,28},{5,29},{6,30},{7,31},{8,0},{9,1... | collective-permute-start | bytes 1671176 | tf_op jit(solution)/shard_map/ppermute | solution.py:474
  15.1 14.9 %collective-permute-start.1 = (bf16[128,2176]{1,0:T(8,128)(2,1)}, bf16[128,2176]{1,0:T(8,128)(2,1)S(1)}, u32[]{:S(2)}, u32[]{:S(2)}) collective-permute-start(bf16[128,2176]{1,0:T(8,128)(2,1)} %get-tuple-element.33.refs_0_), channel_id=1, source_target_pairs={{0,16},{1,17},{2,18},{3,19},{4,20},{5,21},{6,22},{7,23},{8,24},{9,... | collective-permute-start | bytes 1671176 | tf_op jit(solution)/shard_map/ppermute | solution.py:474
  15.6 27.7 %collective-permute-start = (bf16[128,2176]{1,0:T(8,128)(2,1)}, bf16[128,2176]{1,0:T(8,128)(2,1)S(1)}, u32[]{:S(2)}, u32[]{:S(2)}) collective-permute-start(bf16[128,2176]{1,0:T(8,128)(2,1)} %get-tuple-element.33.refs_0_), channel_id=1, source_target_pairs={{0,8},{1,9},{2,10},{3,11},{4,12},{5,13},{6,14},{7,15},{8,16},{9,17... | collective-permute-start | bytes 1671176 | tf_op jit(solution)/shard_map/ppermute | solution.py:474
  16.2 27.1 %collective-permute-start.5 = (bf16[128,2176]{1,0:T(8,128)(2,1)}, bf16[128,2176]{1,0:T(8,128)(2,1)S(1)}, u32[]{:S(2)}, u32[]{:S(2)}) collective-permute-start(bf16[128,2176]{1,0:T(8,128)(2,1)} %get-tuple-element.38.refs_0_), channel_id=1, source_target_pairs={{0,6},{1,7},{2,0},{3,1},{4,2},{5,3},{6,4},{7,5},{8,14},{9,15},{10,... | collective-permute-start | bytes 1671176 | tf_op jit(solution)/shard_map/ppermute | solution.py:474
  18.9 24.3 %collective-permute-start.4 = (bf16[128,2176]{1,0:T(8,128)(2,1)}, bf16[128,2176]{1,0:T(8,128)(2,1)S(1)}, u32[]{:S(2)}, u32[]{:S(2)}) collective-permute-start(bf16[128,2176]{1,0:T(8,128)(2,1)} %get-tuple-element.38.refs_0_), channel_id=1, source_target_pairs={{0,4},{1,5},{2,6},{3,7},{4,0},{5,1},{6,2},{7,3},{8,12},{9,13},{10,... | collective-permute-start | bytes 1671176 | tf_op jit(solution)/shard_map/ppermute | solution.py:474
  29.7 13.6 %collective-permute-start.3 = (bf16[128,2176]{1,0:T(8,128)(2,1)}, bf16[128,2176]{1,0:T(8,128)(2,1)S(1)}, u32[]{:S(2)}, u32[]{:S(2)}) collective-permute-start(bf16[128,2176]{1,0:T(8,128)(2,1)} %get-tuple-element.38.refs_0_), channel_id=1, source_target_pairs={{0,2},{1,3},{2,4},{3,5},{4,6},{5,7},{6,0},{7,1},{8,10},{9,11},{10,... | collective-permute-start | bytes 1671176 | tf_op jit(solution)/shard_map/ppermute | solution.py:474
  43.3 5.8 %copy-start.12 = (bf16[128,2176]{1,0:T(8,128)(2,1)}, bf16[128,2176]{1,0:T(8,128)(2,1)S(1)}, u32[]{:S(2)}) copy-start(bf16[128,2176]{1,0:T(8,128)(2,1)S(1)} %collective-permute-done.5.refs_3_) | copy-start | bytes 1671172
  43.3 5.8 %copy-start.14 = (bf16[128,2176]{1,0:T(8,128)(2,1)}, bf16[128,2176]{1,0:T(8,128)(2,1)S(1)}, u32[]{:S(2)}) copy-start(bf16[128,2176]{1,0:T(8,128)(2,1)S(1)} %collective-permute-done.4.refs_2_) | copy-start | bytes 1671172
  43.3 5.8 %copy-start.16 = (bf16[128,2176]{1,0:T(8,128)(2,1)}, bf16[128,2176]{1,0:T(8,128)(2,1)S(1)}, u32[]{:S(2)}) copy-start(bf16[128,2176]{1,0:T(8,128)(2,1)S(1)} %collective-permute-done.3.refs_1_) | copy-start | bytes 1671172
  43.4 1.5 copy-start.18
  49.1 66.6 %all-to-all-start = ((bf16[8,144,2048]{2,1,0:T(8,128)(2,1)}), bf16[8,144,2048]{2,1,0:T(8,128)(2,1)}, u32[]{:S(2)}, u32[]{:S(2)}) async-start(bf16[8,144,2048]{2,1,0:T(8,128)(2,1)} %dispatch.2), calls=%async_computation | async-start | bytes 9437184 | tf_op jit(solution)/shard_map/all_to_all | solution.py:500
  61.2 54.5 %copy-start.5 = (bf16[1,2048,384]{2,1,0:T(8,128)(2,1)S(1)}, bf16[1,2048,384]{2,1,0:T(8,128)(2,1)}, u32[]{:S(2)}) copy-start(bf16[1,2048,384]{2,1,0:T(8,128)(2,1)} %param.11) | copy-start | bytes 4718596
  61.2 54.5 %copy-start.6 = (bf16[1,2048,384]{2,1,0:T(8,128)(2,1)S(1)}, bf16[1,2048,384]{2,1,0:T(8,128)(2,1)}, u32[]{:S(2)}) copy-start(bf16[1,2048,384]{2,1,0:T(8,128)(2,1)} %param.12) | copy-start | bytes 4718596
  61.2 156.4 %reduce-scatter.2.cloned.1.call-start = ((), (), s32[]{:S(2)}) async-start(), calls=%async_computation.3 | async-start | bytes 5308416 | tf_op jit(solution)/shard_map/reduce_scatter | solution.py:506
  61.6 1.3 copy-start.11
  62.8 1.1 copy-start.13
  63.9 1.1 copy-start.15
  64.9 1.1 copy-start.17
  70.6 9.3 %collective-permute-start.6 = (bf16[144,2048]{1,0:T(8,128)(2,1)}, bf16[144,2048]{1,0:T(8,128)(2,1)S(1)}, u32[]{:S(2)}, u32[]{:S(2)}) collective-permute-start(bf16[144,2048]{1,0:T(8,128)(2,1)} %get-tuple-element.43), channel_id=1, source_target_pairs={{0,1},{1,0},{2,3},{3,2},{4,5},{5,4},{6,7},{7,6},{8,9},{9,8},{10,11... | collective-permute-start | bytes 1769480 | tf_op jit(solution)/shard_map/ppermute | solution.py:474
  70.9 21.1 %collective-permute-start.7 = (bf16[144,2048]{1,0:T(8,128)(2,1)}, bf16[144,2048]{1,0:T(8,128)(2,1)S(1)}, u32[]{:S(2)}, u32[]{:S(2)}) collective-permute-start(bf16[144,2048]{1,0:T(8,128)(2,1)} %get-tuple-element.44), channel_id=1, source_target_pairs={{0,8},{1,9},{2,10},{3,11},{4,12},{5,13},{6,14},{7,15},{8,16},{9,17... | collective-permute-start | bytes 1769480 | tf_op jit(solution)/shard_map/ppermute | solution.py:474
  70.9 55.0 %collective-permute-start.8 = (bf16[144,2048]{1,0:T(8,128)(2,1)}, bf16[144,2048]{1,0:T(8,128)(2,1)}, u32[]{:S(2)}, u32[]{:S(2)}) collective-permute-start(bf16[144,2048]{1,0:T(8,128)(2,1)} %get-tuple-element.45), channel_id=1, source_target_pairs={{0,9},{1,8},{2,11},{3,10},{4,13},{5,12},{6,15},{7,14},{8,17},{9,16... | collective-permute-start | bytes 1769480 | tf_op jit(solution)/shard_map/ppermute | solution.py:474
  70.9 55.0 %collective-permute-start.9 = (bf16[144,2048]{1,0:T(8,128)(2,1)}, bf16[144,2048]{1,0:T(8,128)(2,1)}, u32[]{:S(2)}, u32[]{:S(2)}) collective-permute-start(bf16[144,2048]{1,0:T(8,128)(2,1)} %get-tuple-element.46), channel_id=1, source_target_pairs={{0,16},{1,17},{2,18},{3,19},{4,20},{5,21},{6,22},{7,23},{8,24},{9,... | collective-permute-start | bytes 1769480 | tf_op jit(solution)/shard_map/ppermute | solution.py:474
  79.6 51.6 %collective-permute-start.10 = (bf16[144,2048]{1,0:T(8,128)(2,1)}, bf16[144,2048]{1,0:T(8,128)(2,1)}, u32[]{:S(2)}, u32[]{:S(2)}) collective-permute-start(bf16[144,2048]{1,0:T(8,128)(2,1)} %get-tuple-element.47), channel_id=1, source_target_pairs={{0,17},{1,16},{2,19},{3,18},{4,21},{5,20},{6,23},{7,22},{8,25},{9,... | collective-permute-start | bytes 1769480 | tf_op jit(solution)/shard_map/ppermute | solution.py:474
  79.9 0.8 copy-start.7
  80.7 50.5 %collective-permute-start.11 = (bf16[144,2048]{1,0:T(8,128)(2,1)}, bf16[144,2048]{1,0:T(8,128)(2,1)}, u32[]{:S(2)}, u32[]{:S(2)}) collective-permute-start(bf16[144,2048]{1,0:T(8,128)(2,1)} %get-tuple-element.48), channel_id=1, source_target_pairs={{0,24},{1,25},{2,26},{3,27},{4,28},{5,29},{6,30},{7,31},{8,0},{9,1... | collective-permute-start | bytes 1769480 | tf_op jit(solution)/shard_map/ppermute | solution.py:474
  91.9 0.8 copy-start.9
  92.7 38.9 %collective-permute-start.12 = (bf16[144,2048]{1,0:T(8,128)(2,1)}, bf16[144,2048]{1,0:T(8,128)(2,1)}, u32[]{:S(2)}, u32[]{:S(2)}) collective-permute-start(bf16[144,2048]{1,0:T(8,128)(2,1)} %get-tuple-element.49), channel_id=1, source_target_pairs={{0,25},{1,24},{2,27},{3,26},{4,29},{5,28},{6,31},{7,30},{8,1},{9,0... | collective-permute-start | bytes 1769480 | tf_op jit(solution)/shard_map/ppermute | solution.py:474
  115.7 15.9 %copy-start.8 = (bf16[144,2048]{1,0:T(8,128)(2,1)S(1)}, bf16[144,2048]{1,0:T(8,128)(2,1)}, u32[]{:S(2)}) copy-start(bf16[144,2048]{1,0:T(8,128)(2,1)} %copy-done.7) | copy-start | bytes 1769476
  115.7 15.9 %copy-start.10 = (bf16[144,2048]{1,0:T(8,128)(2,1)S(1)}, bf16[144,2048]{1,0:T(8,128)(2,1)}, u32[]{:S(2)}) copy-start(bf16[144,2048]{1,0:T(8,128)(2,1)} %copy-done.9) | copy-start | bytes 1769476
  115.7 15.9 %copy-start.19 = (bf16[144,2048]{1,0:T(8,128)(2,1)S(1)}, bf16[144,2048]{1,0:T(8,128)(2,1)}, u32[]{:S(2)}) copy-start(bf16[144,2048]{1,0:T(8,128)(2,1)} %get-tuple-element.42.refs_2_) | copy-start | bytes 1769476
  149.8 64.6 %copy-start.3 = (s32[128,8]{0,1:T(8,128)S(1)}, s32[128,8]{0,1:T(8,128)}, u32[]{:S(2)}) copy-start(s32[128,8]{0,1:T(8,128)} %param.10) | copy-start | bytes 12292
Sparse Core Ops, SparseCore 0:
  150.0 63.5 reduce-scatter.1

commit v4 on v3

--- a/solution.py
+++ b/solution.py
@@ -14,6 +14,12 @@
 MAIN = 32
 REM = 4
 PACK = 2 * (MAIN + REM)
+
+
+SIDE = 4
+CORES = 2
+SHIFTS = [(d, f) for d in range(SIDE) for f in range(CORES)]
+SPREAD = [(0, 0), (1, 0), (3, 0), (2, 0), (1, 1), (3, 1), (2, 1), (0, 1)]
 
 
 def dot(a, b, ca=1, cb=0):
@@ -76,6 +82,10 @@
 VMEM = pl.BlockSpec(memory_space=pltpu.VMEM)
 
 
+def in_hbm(*arrays):
+    return [pltpu.with_memory_space_constraint(a, pltpu.HBM) for a in arrays]
+
+
 def prepare(ids, gates, tokens, grads):
     toks, width = tokens.shape
     shape = pltpu.HBM((toks, width + 128), BF)
@@ -88,24 +98,23 @@
         compiler_params=pltpu.CompilerParams(vmem_limit_bytes=16 * MIB),
         cost_estimate=pl.CostEstimate(flops=1 << 20, bytes_accessed=2 * MIB, transcendentals=0),
         name="prepare",
-    )(ids, gates, tokens, grads)
-
-
-def dispatch_kernel(scaled, per, wanted_ref, slot_ref, *refs):
-    lines = 4
-    sources = refs[:lines]
+    )(ids, gates, *in_hbm(tokens, grads))
+
+
+def dispatch_kernel(scaled, per, wanted_ref, starts_ref, *refs):
+    lines, pieces = 4, 5
+    sources = refs[:pieces]
     count = 8 if scaled else 1
-    outs = refs[lines : lines + count]
-    data_ref, s_ref, out_ref, scale_ref, in_sems, out_sems = refs[lines + count :]
+    outs = refs[pieces : pieces + count]
+    data_ref, s_ref, out_ref, scale_ref, in_sems, out_sems = refs[pieces + count :]
     experts, rows, width = out_ref.shape
     toks = sources[0].shape[0]
 
-    loads = [
-        pltpu.make_async_copy(src, data_ref.at[k * toks : (k + 1) * toks, :], in_sems.at[k])
-        for k, src in enumerate(sources)
-    ]
-    for load in loads:
-        load.start()
+    loads = []
+    for k, (src, line, above) in enumerate(zip(sources, (0, 1, 2, 2, 3), (0, 0, 0, toks // 2, 0))):
+        row = pl.multiple_of(starts_ref[line] + above, 16)
+        loads.append(pltpu.make_async_copy(src, data_ref.at[pl.ds(row, src.shape[0]), :], in_sems.at[k]))
+        loads[-1].start()
     for load in loads:
         load.wait()
 
@@ -118,24 +127,29 @@
         return dot(pick, extra, 1, 1)
 
     pos = column(0)
-    target = jnp.where(pos >= 0.0, pos + slot_ref[0:1, :].astype(F32) * float(per), -1.0)
-    chosen = target[:, None, :] == iota((experts, rows, lines * toks), 1).astype(F32)
-    chosen = chosen.astype(F32)
-    s_ref[...] = chosen.reshape(experts * rows, lines * toks).astype(BF)
-    if scaled:
-        weight = column(1) + (column(2) + column(3))
-        total = jnp.sum(chosen * weight[:, None, :], axis=2, keepdims=True)
-        scale_ref[...] = jnp.broadcast_to(total, (experts, rows, 128)).reshape(experts * rows, 128)
+    pair, some = rows // 2, lines * toks // 2
+    for h in range(2):
+        mine = slice(h * some, (h + 1) * some)
+        first = (iota((experts, some), 1) // toks * per).astype(F32)
+        target = jnp.where(pos[:, mine] >= 0.0, pos[:, mine] + first, -1.0)
+        chosen = target[:, None, :] == iota((experts, pair, some), 1).astype(F32)
+        chosen = chosen.astype(F32)
+        s_ref[h] = chosen.reshape(experts * pair, some).astype(BF)
+        if scaled:
+            weight = (column(1) + (column(2) + column(3)))[:, mine]
+            total = jnp.sum(chosen * weight[:, None, :], axis=2, keepdims=True)
+            scale_ref[h] = jnp.broadcast_to(total, (experts, pair, 128)).reshape(experts * pair, 128)
 
     stores = []
     parts = 4
     columns = width // parts
     for c in range(parts):
         cols = slice(c * columns, (c + 1) * columns)
-        got = dot(s_ref[...], data_ref[:, cols])
-        if scaled:
-            got = got * jnp.concatenate([scale_ref[...]] * (columns // 128), axis=1)
-        out_ref[:, :, cols] = got.astype(BF).reshape(experts, rows, columns)
+        for h in range(2):
+            got = dot(s_ref[h], data_ref[h * some : (h + 1) * some, cols])
+            if scaled:
+                got = got * jnp.concatenate([scale_ref[h]] * (columns // 128), axis=1)
+            out_ref[:, h * pair : (h + 1) * pair, cols] = got.astype(BF).reshape(experts, pair, columns)
         for k, out in enumerate(outs):
             here, there = (out_ref.at[k], out) if scaled else (out_ref, out)
             at = (slice(None),) * (len(there.shape) - 1) + (cols,)
@@ -145,21 +159,21 @@
         store.wait()
 
 
-def dispatch(wanted, slots, lines, scaled):
+def dispatch(wanted, starts, lines, scaled):
     toks, width = lines[0].shape[0], lines[0].shape[1] - 128
     per, experts = MAIN + REM, 8
-    rows, all_toks = len(lines) * per, len(lines) * toks
+    rows, all_toks = SIDE * per, SIDE * toks
     shapes = (pltpu.HBM((rows, width), BF),) * experts if scaled else (pltpu.HBM((experts, rows, width), BF),)
     return pl.pallas_call(
         functools.partial(dispatch_kernel, scaled, per),
         out_shape=shapes,
-        in_specs=[VMEM, VMEM] + [HBM] * len(lines),
+        in_specs=[VMEM, pl.BlockSpec(memory_space=pltpu.SMEM)] + [HBM] * len(lines),
         out_specs=(HBM,) * len(shapes),
         scratch_shapes=[
             pltpu.VMEM((all_toks, width + 128), BF),
-            pltpu.VMEM((experts * rows, all_toks), BF),
+            pltpu.VMEM((2, experts * rows // 2, all_toks // 2), BF),
             pltpu.VMEM((experts, rows, width), BF),
-            pltpu.VMEM((experts * rows, 128), F32),
+            pltpu.VMEM((2, experts * rows // 2, 128), F32),
             pltpu.SemaphoreType.DMA((len(lines),)),
             pltpu.SemaphoreType.DMA((4 * len(shapes),)),
         ],
@@ -168,7 +182,7 @@
             flops=2 * experts * rows * all_toks * width, bytes_accessed=7 * MIB, transcendentals=0
         ),
         name="dispatch",
-    )(wanted, slots, *lines)
+    )(wanted, starts, *in_hbm(*lines))
 
 
 def regrouped(block):
@@ -177,8 +191,8 @@
 
 def forward_kernel(*refs):
     blocks, wg_hbm, wu_hbm = refs[:3]
-    cs_hbm, act_hbm, wcat_hbm = refs[3:6]
-    x_ref, wcat_ref, cs_ref, act_ref, turn_ref, at_ref, sems = refs[6:]
+    cs_ref, at_ref, wcat_ref = refs[3:6]
+    x_ref, act_ref, turn_ref, sems = refs[6:]
     rows = blocks.shape[1]
     hidden = wg_hbm.shape[1]
     loads = [
@@ -192,9 +206,7 @@
         load.start()
     loads[0].wait()
     loads[1].wait()
-    stores = [pltpu.make_async_copy(wcat_ref, wcat_hbm, sems.at[10])]
-    stores[0].start()
-    parts = 2
+    parts = 4
     most = 8 // parts * rows
     for i in range(parts):
         for load in loads[2 + i * 8 // parts : 2 + (i + 1) * 8 // parts]:
@@ -207,18 +219,11 @@
         cs_ref[some, :hidden] = up * sigma * (1.0 + gate * (1.0 - sigma))
         cs_ref[some, hidden:] = silu
         act_ref[some, :] = silu * up
-        store = pltpu.make_async_copy(cs_ref.at[some, :], cs_hbm.at[some, :], sems.at[11 + i])
-        store.start()
-        stores.append(store)
     per = MAIN + REM
     for b in range(32):
         to = regrouped(b)
         turn_ref[to * per : (to + 1) * per, :] = act_ref[b * per : (b + 1) * per, :]
     at_ref[...] = turn_ref[...].astype(BF).T
-    stores.append(pltpu.make_async_copy(at_ref, act_hbm, sems.at[13]))
-    stores[-1].start()
-    for store in stores:
-        store.wait()
 
 
 def forward(blocks, wg, wu):
@@ -227,34 +232,31 @@
     return pl.pallas_call(
         forward_kernel,
         out_shape=(
-            pltpu.HBM((rows, 2 * hidden), F32),
-            pltpu.HBM((hidden, rows), BF),
-            pltpu.HBM((width, 2 * hidden), BF),
+            jax.ShapeDtypeStruct((rows, 2 * hidden), F32),
+            jax.ShapeDtypeStruct((hidden, rows), BF),
+            jax.ShapeDtypeStruct((width, 2 * hidden), BF),
         ),
         in_specs=[HBM] * 3,
-        out_specs=(HBM,) * 3,
+        out_specs=(VMEM,) * 3,
         scratch_shapes=[
             pltpu.VMEM((rows, width), BF),
-            pltpu.VMEM((width, 2 * hidden), BF),
-            pltpu.VMEM((rows, 2 * hidden), F32),
             pltpu.VMEM((rows, hidden), F32),
             pltpu.VMEM((rows, hidden), F32),
-            pltpu.VMEM((hidden, rows), BF),
-            pltpu.SemaphoreType.DMA((14,)),
+            pltpu.SemaphoreType.DMA((10,)),
         ],
-        compiler_params=pltpu.CompilerParams(vmem_limit_bytes=36 * MIB),
+        compiler_params=pltpu.CompilerParams(vmem_limit_bytes=20 * MIB),
         cost_estimate=pl.CostEstimate(
             flops=2 * rows * width * 2 * hidden, bytes_accessed=16 * MIB, transcendentals=rows * hidden
         ),
         name="forward",
-    )(blocks, wg, wu)
+    )(*in_hbm(blocks, wg, wu))
 
 
 def middle_kernel(*refs):
     to_ref, at_row_ref, gs, xs = refs[0], refs[1], refs[2:10], refs[10]
-    wd_hbm, wcat_hbm, cs_hbm, act_hbm = refs[11:15]
+    wd_ref, wcat_ref, cs_ref, at_ref = refs[11:15]
     packed_hbm, pair_hbm = refs[15:17]
-    (g_ref, x_ref, wd_ref, wcat_ref, cs_ref, at_ref, raw_ref, turn_ref, d_ref, dt_ref, dm_ref, dr_ref, packed_ref,
+    (g_ref, x_ref, raw_ref, turn_ref, d_ref, dt_ref, dm_ref, dr_ref, packed_ref,
      pair_ref, sems, out_sems) = refs[17:]
     rows = gs[0].shape[0]
     copies = packed_ref.shape[0]
@@ -267,17 +269,11 @@
         copy.start()
         return copy
 
-    wd_in = load(wd_hbm, wd_ref, 16)
-    g_in = [
-        load(b, g_ref.at[pl.ds(pl.multiple_of(at_row_ref[k], 16), rows), :], k) for k, b in enumerate(gs)
-    ]
-    cs_in = load(cs_hbm, cs_ref, 17)
+    order = sorted(range(8), key=lambda k: SPREAD[k])
+    g_in = [load(gs[k], g_ref.at[pl.ds(pl.multiple_of(at_row_ref[k], 16), rows), :], k) for k in order]
     x_in = [load(xs.at[k], x_ref.at[k * rows : (k + 1) * rows, :], 8 + k) for k in range(8)]
-    act_in = load(act_hbm, at_ref, 18)
-    wcat_in = load(wcat_hbm, wcat_ref, 19)
-
-    wd_in.wait()
-    parts = 4
+
+    parts = 2
     most = 8 // parts * rows
     for i in range(parts):
         for copy in g_in[i * 8 // parts : (i + 1) * 8 // parts]:
@@ -287,7 +283,6 @@
     for b in range(n):
         to = regrouped(b)
         turn_ref[to * per_block : (to + 1) * per_block, :] = raw_ref[b * per_block : (b + 1) * per_block, :]
-    cs_in.wait()
     for i in range(parts):
         some = slice(i * most, (i + 1) * most)
         d_act = turn_ref[some, :]
@@ -301,7 +296,6 @@
 
     for copy in x_in:
         copy.wait()
-    act_in.wait()
     tile = 256
     per = 2 * half // copies
     slab = hidden // copies
@@ -320,8 +314,8 @@
     packed_out = pltpu.make_async_copy(packed_ref, packed_hbm, out_sems.at[n])
     packed_out.start()
 
-    wcat_in.wait()
     sent = []
+    parts = 4
     step = n // parts
     most, few = step * MAIN, step * 2 * REM
     for i in range(parts):
@@ -354,15 +348,11 @@
     return pl.pallas_call(
         middle_kernel,
         out_shape=(pltpu.HBM((copies, length, 128), BF), pltpu.HBM((n, PACK, half), BF)),
-        in_specs=[smem] * 2 + [HBM] * 13,
+        in_specs=[smem] * 2 + [pl.BlockSpec(memory_space=pl.ANY)] * 9 + [VMEM] * 4,
         out_specs=(HBM,) * 2,
         scratch_shapes=[
             pltpu.VMEM((rows, width), BF),
             pltpu.VMEM((rows, width), BF),
-            pltpu.VMEM((hidden, width), BF),
-            pltpu.VMEM((width, both), BF),
-            pltpu.VMEM((rows, both), F32),
-            pltpu.VMEM((hidden, rows), BF),
             pltpu.VMEM((rows, hidden), F32),
             pltpu.VMEM((rows, hidden), F32),
             pltpu.VMEM((rows, both), F32),
@@ -371,10 +361,10 @@
             pltpu.VMEM((n * 2 * REM, both), F32),
             pltpu.VMEM((copies, length, 128), BF),
             pltpu.VMEM((n, PACK, half), BF),
-            pltpu.SemaphoreType.DMA((20,)),
+            pltpu.SemaphoreType.DMA((16,)),
             pltpu.SemaphoreType.DMA((n + 1,)),
         ],
-        compiler_params=pltpu.CompilerParams(vmem_limit_bytes=50 * MIB),
+        compiler_params=pltpu.CompilerParams(vmem_limit_bytes=40 * MIB),
         cost_estimate=pl.CostEstimate(flops=2 * rows * width * 6 * hidden, bytes_accessed=28 * MIB, transcendentals=0),
         name="middle",
     )(to, at_row, *gs, xs, wd, wcat, cs, act)
@@ -454,11 +444,6 @@
     )(ids, ret)
 
 
-SIDE = 4
-CORES = 2
-SHIFTS = [(d, f) for d in range(SIDE) for f in range(CORES)]
-
-
 def place(x, y, core):
     return (x % SIDE * SIDE + y % SIDE) * CORES + core
 
@@ -482,25 +467,30 @@
     x, y, core = me // (SIDE * CORES), me // CORES % SIDE, me % CORES
     wide = lambda values: jnp.broadcast_to(jnp.stack(values).astype(jnp.int32)[:, None], (len(values), 128))
     along_y = wide([place(x, d, f) for d, f in SHIFTS])
-    along_x = wide([place(x + d, y, core ^ f) for d, f in SHIFTS])
+    along_x = wide([place(x + d, y, core ^ f) for d, f in SPREAD])
     toks = tokens.shape[0]
     near = jnp.arange(SIDE, dtype=jnp.int32)
-    slots_x = jnp.broadcast_to(jnp.repeat(near, toks)[None, :], (8, SIDE * toks))
-    slots_g = jnp.broadcast_to(jnp.repeat((y - near + SIDE) % SIDE, toks)[None, :], (8, SIDE * toks))
+    starts_x = near * toks
+    starts_g = (y - near + SIDE) % SIDE * toks
     origin = jnp.stack([place(x - d + SIDE, b, f) for b, f in SHIFTS for d in range(SIDE)]).astype(jnp.int32)
-    at_row = jnp.stack([(d * CORES + (core ^ f)) * SIDE * (MAIN + REM) for d, f in SHIFTS]).astype(jnp.int32)
+    at_row = jnp.stack([(d * CORES + (core ^ f)) * SIDE * (MAIN + REM) for d, f in SPREAD]).astype(jnp.int32)
 
     ids_t = expert_ids.T
     tokens, grad_out = prepare(ids_t, gates.T, tokens, grad_out)
-    lines_x = [moved(tokens, d, 0, 0) for d in range(SIDE)]
-    lines_g = [moved(grad_out, 0, d, 0) for d in range(SIDE)]
+    near_x, near_g = [tokens], [grad_out]
+    for d in (1, SIDE - 1):
+        near_x.append(moved(tokens, d, 0, 0))
+        near_g.append(moved(grad_out, 0, d, 0))
+    cut = toks // 2
+    lines_x = [tokens, near_x[1], moved(near_x[1][:cut], 1, 0, 0), moved(near_x[2][cut:], SIDE - 1, 0, 0), near_x[2]]
+    lines_g = [grad_out, near_g[1], moved(near_g[1][:cut], 0, 1, 0), moved(near_g[2][cut:], 0, SIDE - 1, 0), near_g[2]]
     lines_x, lines_g = lax.optimization_barrier((lines_x, lines_g))
-    (out_x,) = dispatch(along_y, slots_x, lines_x, False)
+    (out_x,) = dispatch(along_y, starts_x, lines_x, False)
     columns = [[place(a, b, f) for b in range(SIDE) for f in range(CORES)] for a in range(SIDE)]
     xs = lax.all_to_all(out_x, "expert", split_axis=0, concat_axis=0, axis_index_groups=columns, tiled=True)
     along_x, _ = lax.optimization_barrier((along_x, out_x))
-    out_g = dispatch(along_x, slots_g, lines_g, True)
-    gs = [moved(v, d, 0, f) for v, (d, f) in zip(out_g, SHIFTS)]
+    out_g = dispatch(along_x, starts_g, lines_g, True)
+    gs = [moved(v, d, 0, f) for v, (d, f) in zip(out_g, SPREAD)]
     cs, act, wcat = forward(xs, wg, wu)
     packed, outgoing = middle(origin, at_row, gs, xs, wd, wcat, cs, act, copies)
     summed = lax.psum_scatter(packed, "dp", scatter_dimension=0, tiled=True)[0]

time: 227 us -> 238 us (1.048)
  Pallas kernels: 43.3 us -> 73.7 us
  waiting for transfers between devices: 58.8 us -> 43.8 us
  local copies, waits for them, and re-layouts: 11.6 us -> 1.99 us
  starting transfers between devices: 33.9 us -> 41.1 us
    pallas_call x1, Pallas kernels: 1.05 us -> 32.9 us  [prepare(): pl.pallas_call(prepare_kernel, out_shape=(shape, shape), in_specs=[VMEM,...]
    ppermute x13 -> x15, waiting for transfers between devices: 38.9 us -> 25.4 us  [moved(): return lax.ppermute(value, 'expert', pairs)]
    ppermute x13 -> x15, starting transfers between devices: 21.8 us -> 33.6 us  [moved(): return lax.ppermute(value, 'expert', pairs)]
    unnamed x40 -> x18, local copies, waits for them, and re-layouts: 11 us -> 1.4 us
    all_to_all x1, starting transfers between devices: 12 us -> 7.51 us  [shards(): lax.all_to_all(out_x, 'expert', split_axis=0, concat_axis=0, axis_index_g...]
  transfers between devices with their start and end apart: 15 -> 17, of which waited for: 7 -> 6; matrix products, arithmetic and copies ran while one was open for 0% -> 0% of each run, Pallas kernels for 8% -> 7%
where the time goes in v4:
time: 238 us; the launch traced here: 237 us
  Pallas kernels  73.7 us (31%)
  blocking collectives  62.4 us (26%)
  waiting for transfers between devices  43.8 us (18%)
  starting transfers between devices  41.1 us (17%)
  between operations  14.3 us (6%)
    all_to_all x1, blocking collectives, shards(): lax.all_to_all(outgoing, 'expert', split_axis=0, concat_axis=0, tiled=True)  62.4 us
    ppermute x15, starting transfers between devices, moved(): return lax.ppermute(value, 'expert', pairs)  33.6 us
    pallas_call x1, Pallas kernels, prepare(): pl.pallas_call(prepare_kernel, out_shape=(shape, shape), in_specs=[VMEM,...  32.9 us
    ppermute x15, waiting for transfers between devices, moved(): return lax.ppermute(value, 'expert', pairs)  25.4 us
    all_to_all x1, waiting for transfers between devices, shards(): lax.all_to_all(out_x, 'expert', split_axis=0, concat_axis=0, axis_index_g...  18.4 us
    pallas_call x1, Pallas kernels, middle(): pl.pallas_call(middle_kernel, out_shape=(pltpu.HBM((copies, length, 128),...  17.1 us
    pallas_call x2, Pallas kernels, dispatch(): pl.pallas_call(functools.partial(dispatch_kernel, scaled, per), out_shape...  10.3 us
    pallas_call x1, Pallas kernels, forward(): pl.pallas_call(forward_kernel, out_shape=(jax.ShapeDtypeStruct((rows, 2 *...  8.17 us
  transfers between devices with their start and end apart: 17, of which 6 were waited for; matrix products, arithmetic and copies ran while one was open for 0% of the time, Pallas kernels for 7%

profile of v4, /device:TPU:1, one launch (start us, length us, event | category | flops | bytes accessed | tf_op | source)
XLA Modules:
  0.0 237.3 jit_solution(11578076789557817058)
XLA Ops:
  7.2 0.0 copy-start
  7.2 0.7 copy-done
  7.9 0.7 copy-done.2
  8.5 32.9 %prepare.1 = (bf16[128,2176]{1,0:T(8,128)(2,1)}, bf16[128,2176]{1,0:T(8,128)(2,1)}) custom-call(s32[8,128]{1,0:T(8,128)S(1)} %bitcast.65, f32[8,128]{1,0:T(8,128)S(1)} %bitcast.67, bf16[128,2048]{1,0:T(8,128)(2,1)} %tokens_hbm.1, bf16[128,2048]{1,0:T(8,128)(2,1)} %grads_hbm.1), custom_call_target="tpu_custom_call" | custom-call | flops 1048576 | bytes 2097152 | tf_op jit(solution)/shard_map/prepare/pallas_call | solution.py:92
  41.5 3.4 %collective-permute-start.2 = (bf16[128,2176]{1,0:T(8,128)(2,1)}, bf16[128,2176]{1,0:T(8,128)(2,1)S(1)}, u32[]{:S(2)}, u32[]{:S(2)}) collective-permute-start(bf16[128,2176]{1,0:T(8,128)(2,1)} %get-tuple-element.35.refs_0_), channel_id=1, source_target_pairs={{0,24},{1,25},{2,26},{3,27},{4,28},{5,29},{6,30},{7,31},{8,0},{9,1... | collective-permute-start | bytes 1671176 | tf_op jit(solution)/shard_map/ppermute | solution.py:459
  44.8 0.0 collective-permute-start
  44.8 2.7 %collective-permute-start.6 = (bf16[128,2176]{1,0:T(8,128)(2,1)}, bf16[128,2176]{1,0:T(8,128)(2,1)S(1)}, u32[]{:S(2)}, u32[]{:S(2)}) collective-permute-start(bf16[128,2176]{1,0:T(8,128)(2,1)} %get-tuple-element.41.refs_0_), channel_id=1, source_target_pairs={{0,6},{1,7},{2,0},{3,1},{4,2},{5,3},{6,4},{7,5},{8,14},{9,15},{10,... | collective-permute-start | bytes 1671176 | tf_op jit(solution)/shard_map/ppermute | solution.py:459
  47.6 0.0 collective-permute-start.4
  47.6 8.9 %collective-permute-done.2.refs_4_ = bf16[128,2176]{1,0:T(8,128)(2,1)S(1)} collective-permute-done((bf16[128,2176]{1,0:T(8,128)(2,1)}, bf16[128,2176]{1,0:T(8,128)(2,1)S(1)}, u32[]{:S(2)}, u32[]{:S(2)}) %collective-permute-start.2) | collective-permute-done | bytes 557088 | tf_op jit(solution)/shard_map/ppermute | solution.py:459
  56.5 3.4 %collective-permute-start.3 = (bf16[64,2176]{1,0:T(8,128)(2,1)S(1)}, bf16[64,2176]{1,0:T(8,128)(2,1)}, u32[]{:S(2)}, u32[]{:S(2)}) collective-permute-start(bf16[64,2176]{1,0:T(8,128)(2,1)S(1)} %slice.17), channel_id=1, source_target_pairs={{0,24},{1,25},{2,26},{3,27},{4,28},{5,29},{6,30},{7,31},{8,0},{9,1... | collective-permute-start | bytes 835592 | tf_op jit(solution)/shard_map/ppermute | solution.py:459
  59.9 0.0 collective-permute-done.refs_1_
  59.9 0.1 collective-permute-start.1
  60.0 0.0 collective-permute-done.6.refs_4_
  60.0 2.8 %collective-permute-start.7 = (bf16[64,2176]{1,0:T(8,128)(2,1)S(1)}, bf16[64,2176]{1,0:T(8,128)(2,1)}, u32[]{:S(2)}, u32[]{:S(2)}) collective-permute-start(bf16[64,2176]{1,0:T(8,128)(2,1)S(1)} %slice.19), channel_id=1, source_target_pairs={{0,6},{1,7},{2,0},{3,1},{4,2},{5,3},{6,4},{7,5},{8,14},{9,15},{10,... | collective-permute-start | bytes 835592 | tf_op jit(solution)/shard_map/ppermute | solution.py:459
  62.9 0.1 collective-permute-start.5
  63.0 0.1 stack.239
  63.1 1.2 collective-permute-done.3.refs_3_
  64.3 3.3 %collective-permute-done.1.refs_2_ = bf16[64,2176]{1,0:T(8,128)(2,1)} collective-permute-done((bf16[64,2176]{1,0:T(8,128)(2,1)S(1)}, bf16[64,2176]{1,0:T(8,128)(2,1)}, u32[]{:S(2)}, u32[]{:S(2)}) %collective-permute-start.1) | collective-permute-done | bytes 278560 | tf_op jit(solution)/shard_map/ppermute | solution.py:459
  67.6 0.0 collective-permute-done.7.refs_3_
  67.6 2.7 %collective-permute-done.5.refs_2_ = bf16[64,2176]{1,0:T(8,128)(2,1)} collective-permute-done((bf16[64,2176]{1,0:T(8,128)(2,1)S(1)}, bf16[64,2176]{1,0:T(8,128)(2,1)}, u32[]{:S(2)}, u32[]{:S(2)}) %collective-permute-start.5) | collective-permute-done | bytes 278560 | tf_op jit(solution)/shard_map/ppermute | solution.py:459
  70.3 0.1 broadcast_in_dim.22.wanted_ref
  70.4 5.0 %dispatch.2 = bf16[8,144,2048]{2,1,0:T(8,128)(2,1)} custom-call(s32[8,128]{1,0:T(8,128)S(1)} %broadcast_in_dim.22.wanted_ref, s32[4]{0:T(128)S(1)} %iota_multiply_fusion.starts_ref, bf16[128,2176]{1,0:T(8,128)(2,1)} %get-tuple-element.35.refs_0_, bf16[128,2176]{1,0:T(8,128)(2,1)} %copy-done.8, bf16[64,2176]{1,0:T(8,128)(2,1)} %collective-permute-done.1.refs_2_, ...), custom_call_target="tpu_custom_call" | custom-call | flops 2415919104 | bytes 7340032 | tf_op jit(solution)/shard_map/dispatch/pallas_call | solution.py:167
  75.4 7.5 %all-to-all-start = ((bf16[8,144,2048]{2,1,0:T(8,128)(2,1)}), bf16[8,144,2048]{2,1,0:T(8,128)(2,1)}, u32[]{:S(2)}, u32[]{:S(2)}) async-start(bf16[8,144,2048]{2,1,0:T(8,128)(2,1)} %dispatch.2), calls=%async_computation | async-start | bytes 9437184 | tf_op jit(solution)/shard_map/all_to_all | solution.py:490
  82.9 0.1 stack.230
  83.0 0.1 broadcast_in_dim.10.wanted_ref
  83.1 5.3 %dispatch.3 = (bf16[144,2048]{1,0:T(8,128)(2,1)}, bf16[144,2048]{1,0:T(8,128)(2,1)}, bf16[144,2048]{1,0:T(8,128)(2,1)}, bf16[144,2048]{1,0:T(8,128)(2,1)}, bf16[...) custom-call(s32[8,128]{1,0:T(8,128)S(1)} %broadcast_in_dim.10.wanted_re, ...), custom_call_target="tpu_custom_call" | custom-call | flops 2415919104 | bytes 7340032 | tf_op jit(solution)/shard_map/dispatch/pallas_call | solution.py:167
  88.4 0.1 collective-permute-start.8
  88.5 2.7 %collective-permute-start.9 = (bf16[144,2048]{1,0:T(8,128)(2,1)}, bf16[144,2048]{1,0:T(8,128)(2,1)S(1)}, u32[]{:S(2)}, u32[]{:S(2)}) collective-permute-start(bf16[144,2048]{1,0:T(8,128)(2,1)} %get-tuple-element.48), channel_id=1, source_target_pairs={{0,24},{1,25},{2,26},{3,27},{4,28},{5,29},{6,30},{7,31},{8,0},{9,1... | collective-permute-start | bytes 1769480 | tf_op jit(solution)/shard_map/ppermute | solution.py:459
  91.2 1.1 collective-permute-start.10
  92.3 1.9 collective-permute-start.11
  94.2 1.1 collective-permute-start.12
  95.3 9.3 %collective-permute-done.8.refs_3_ = bf16[144,2048]{1,0:T(8,128)(2,1)S(1)} collective-permute-done((bf16[144,2048]{1,0:T(8,128)(2,1)}, bf16[144,2048]{1,0:T(8,128)(2,1)S(1)}, u32[]{:S(2)}, u32[]{:S(2)}) %collective-permute-start.8) | collective-permute-done | bytes 589856 | tf_op jit(solution)/shard_map/ppermute | solution.py:459
  104.5 14.3 %collective-permute-start.13 = (bf16[144,2048]{1,0:T(8,128)(2,1)}, bf16[144,2048]{1,0:T(8,128)(2,1)S(1)}, u32[]{:S(2)}, u32[]{:S(2)}) collective-permute-start(bf16[144,2048]{1,0:T(8,128)(2,1)} %get-tuple-element.52), channel_id=1, source_target_pairs={{0,17},{1,16},{2,19},{3,18},{4,21},{5,20},{6,23},{7,22},{8,25},{9,... | collective-permute-start | bytes 1769480 | tf_op jit(solution)/shard_map/ppermute | solution.py:459
  118.8 0.0 collective-permute-done.9.refs_4_
  118.8 0.0 collective-permute-start.14
  118.8 0.1 stack.221.refs_1_
  118.9 0.1 stack.212.refs_0_
  119.0 18.4 %all-to-all-done.refs_0_.refs_10_ = bf16[8,144,2048]{2,1,0:T(8,128)(2,1)} async-done(((bf16[8,144,2048]{2,1,0:T(8,128)(2,1)}), bf16[8,144,2048]{2,1,0:T(8,128)(2,1)}, u32[]{:S(2)}, u32[]{:S(2)}) %all-to-all-start) | async-done | bytes 4718624 | tf_op jit(solution)/shard_map/all_to_all | solution.py:490
  137.5 8.2 %forward.1 = (f32[1152,768]{1,0:T(8,128)S(1)}, bf16[384,1152]{1,0:T(8,128)(2,1)S(1)}, bf16[2048,768]{1,0:T(8,128)(2,1)S(1)}) custom-call(bf16[8,144,2048]{2,1,0:T(8,128)(2,1)} %all-to-all-done.refs_0_.refs_10_, bf16[2048,384]{1,0:T(8,128)(2,1)} %bitcast.70, bf16[2048,384]{1,0:T(8,128)(2,1)} %bitcast.71), custom_call_target="tpu_custom_call" | custom-call | flops 3623878656 | bytes 16777216 | tf_op jit(solution)/shard_map/forward/pallas_call | solution.py:232
  145.6 0.0 collective-permute-done.10.refs_5_
  145.7 0.0 collective-permute-done.12.refs_7_
  145.7 0.0 collective-permute-done.13.refs_8_
  145.7 17.1 %middle.1 = (bf16[8,2304,128]{2,1,0:T(8,128)(2,1)}, bf16[32,72,1024]{2,1,0:T(8,128)(2,1)}) custom-call(s32[32]{0:T(128)S(1)} %stack.212.refs_0_, s32[8]{0:T(128)S(1)} %stack.221.refs_1_, bf16[144,2048]{1,0:T(8,128)(2,1)S(1)} %copy-done.4, bf16[144,2048]{1,0:T(8,128)(2,1)S(1)} %collective-permute-done.8.refs_3_, ...), custom_call_target="tpu_custom_call" | custom-call | flops 10871635968 | bytes 29360128 | tf_op jit(solution)/shard_map/middle/pallas_call | solution.py:348
  162.8 0.0 reduce-scatter.2.cloned.1.call-update
  162.9 0.0 copy-start.1
  162.9 62.4 %all_to_all.10.ret_ref = bf16[32,72,1024]{2,1,0:T(8,128)(2,1)S(1)} all-to-all(bf16[32,72,1024]{2,1,0:T(8,128)(2,1)} %get-tuple-element.57), channel_id=1, replica_groups=mesh['dp'=8,'expert'=32] {'expert'}, dimensions={0} | all-to-all | bytes 9437184 | tf_op jit(solution)/shard_map/all_to_all | solution.py:497
  225.2 3.2 %combine.1 = bf16[128,2048]{1,0:T(8,128)(2,1)} custom-call(s32[8,128]{1,0:T(8,128)S(1)} %bitcast.66, bf16[32,72,1024]{2,1,0:T(8,128)(2,1)S(1)} %all_to_all.10.ret_ref), custom_call_target="tpu_custom_call" | custom-call | flops 671088640 | bytes 6291456 | tf_op jit(solution)/shard_map/combine/pallas_call | solution.py:428
  228.4 2.0 unpack.1
  (25 shorter events, 0.1 us)
Async XLA Ops:
  7.2 0.7 copy-start
  7.9 0.7 copy-start.2
  41.5 15.0 %collective-permute-start.2 = (bf16[128,2176]{1,0:T(8,128)(2,1)}, bf16[128,2176]{1,0:T(8,128)(2,1)S(1)}, u32[]{:S(2)}, u32[]{:S(2)}) collective-permute-start(bf16[128,2176]{1,0:T(8,128)(2,1)} %get-tuple-element.35.refs_0_), channel_id=1, source_target_pairs={{0,24},{1,25},{2,26},{3,27},{4,28},{5,29},{6,30},{7,31},{8,0},{9,1... | collective-permute-start | bytes 1671176 | tf_op jit(solution)/shard_map/ppermute | solution.py:459
  44.8 15.0 %collective-permute-start = (bf16[128,2176]{1,0:T(8,128)(2,1)}, bf16[128,2176]{1,0:T(8,128)(2,1)S(1)}, u32[]{:S(2)}, u32[]{:S(2)}) collective-permute-start(bf16[128,2176]{1,0:T(8,128)(2,1)} %get-tuple-element.35.refs_0_), channel_id=1, source_target_pairs={{0,8},{1,9},{2,10},{3,11},{4,12},{5,13},{6,14},{7,15},{8,16},{9,17... | collective-permute-start | bytes 1671176 | tf_op jit(solution)/shard_map/ppermute | solution.py:459
  44.8 15.1 %collective-permute-start.6 = (bf16[128,2176]{1,0:T(8,128)(2,1)}, bf16[128,2176]{1,0:T(8,128)(2,1)S(1)}, u32[]{:S(2)}, u32[]{:S(2)}) collective-permute-start(bf16[128,2176]{1,0:T(8,128)(2,1)} %get-tuple-element.41.refs_0_), channel_id=1, source_target_pairs={{0,6},{1,7},{2,0},{3,1},{4,2},{5,3},{6,4},{7,5},{8,14},{9,15},{10,... | collective-permute-start | bytes 1671176 | tf_op jit(solution)/shard_map/ppermute | solution.py:459
  47.6 15.3 %collective-permute-start.4 = (bf16[128,2176]{1,0:T(8,128)(2,1)}, bf16[128,2176]{1,0:T(8,128)(2,1)S(1)}, u32[]{:S(2)}, u32[]{:S(2)}) collective-permute-start(bf16[128,2176]{1,0:T(8,128)(2,1)} %get-tuple-element.41.refs_0_), channel_id=1, source_target_pairs={{0,2},{1,3},{2,4},{3,5},{4,6},{5,7},{6,0},{7,1},{8,10},{9,11},{10,... | collective-permute-start | bytes 1671176 | tf_op jit(solution)/shard_map/ppermute | solution.py:459
  56.5 13.9 %copy-start.7 = (bf16[128,2176]{1,0:T(8,128)(2,1)}, bf16[128,2176]{1,0:T(8,128)(2,1)S(1)}, u32[]{:S(2)}) copy-start(bf16[128,2176]{1,0:T(8,128)(2,1)S(1)} %collective-permute-done.2.refs_4_) | copy-start | bytes 1671172
  56.5 7.8 %collective-permute-start.3 = (bf16[64,2176]{1,0:T(8,128)(2,1)S(1)}, bf16[64,2176]{1,0:T(8,128)(2,1)}, u32[]{:S(2)}, u32[]{:S(2)}) collective-permute-start(bf16[64,2176]{1,0:T(8,128)(2,1)S(1)} %slice.17), channel_id=1, source_target_pairs={{0,24},{1,25},{2,26},{3,27},{4,28},{5,29},{6,30},{7,31},{8,0},{9,1... | collective-permute-start | bytes 835592 | tf_op jit(solution)/shard_map/ppermute | solution.py:459
  59.9 10.5 %copy-start.8 = (bf16[128,2176]{1,0:T(8,128)(2,1)}, bf16[128,2176]{1,0:T(8,128)(2,1)S(1)}, u32[]{:S(2)}) copy-start(bf16[128,2176]{1,0:T(8,128)(2,1)S(1)} %collective-permute-done.refs_1_) | copy-start | bytes 1671172
  59.9 7.7 %collective-permute-start.1 = (bf16[64,2176]{1,0:T(8,128)(2,1)S(1)}, bf16[64,2176]{1,0:T(8,128)(2,1)}, u32[]{:S(2)}, u32[]{:S(2)}) collective-permute-start(bf16[64,2176]{1,0:T(8,128)(2,1)S(1)} %slice.16), channel_id=1, source_target_pairs={{0,8},{1,9},{2,10},{3,11},{4,12},{5,13},{6,14},{7,15},{8,16},{9,17... | collective-permute-start | bytes 835592 | tf_op jit(solution)/shard_map/ppermute | solution.py:459
  60.0 15.4 %copy-start.5 = (bf16[128,2176]{1,0:T(8,128)(2,1)}, bf16[128,2176]{1,0:T(8,128)(2,1)S(1)}, u32[]{:S(2)}) copy-start(bf16[128,2176]{1,0:T(8,128)(2,1)S(1)} %collective-permute-done.6.refs_4_) | copy-start | bytes 1671172
  60.0 7.6 %collective-permute-start.7 = (bf16[64,2176]{1,0:T(8,128)(2,1)S(1)}, bf16[64,2176]{1,0:T(8,128)(2,1)}, u32[]{:S(2)}, u32[]{:S(2)}) collective-permute-start(bf16[64,2176]{1,0:T(8,128)(2,1)S(1)} %slice.19), channel_id=1, source_target_pairs={{0,6},{1,7},{2,0},{3,1},{4,2},{5,3},{6,4},{7,5},{8,14},{9,15},{10,... | collective-permute-start | bytes 835592 | tf_op jit(solution)/shard_map/ppermute | solution.py:459
  62.8 12.5 %copy-start.6 = (bf16[128,2176]{1,0:T(8,128)(2,1)}, bf16[128,2176]{1,0:T(8,128)(2,1)S(1)}, u32[]{:S(2)}) copy-start(bf16[128,2176]{1,0:T(8,128)(2,1)S(1)} %collective-permute-done.4.refs_1_) | copy-start | bytes 1671172
  62.9 7.4 %collective-permute-start.5 = (bf16[64,2176]{1,0:T(8,128)(2,1)S(1)}, bf16[64,2176]{1,0:T(8,128)(2,1)}, u32[]{:S(2)}, u32[]{:S(2)}) collective-permute-start(bf16[64,2176]{1,0:T(8,128)(2,1)S(1)} %slice.18), channel_id=1, source_target_pairs={{0,2},{1,3},{2,4},{3,5},{4,6},{5,7},{6,0},{7,1},{8,10},{9,11},{10,... | collective-permute-start | bytes 835592 | tf_op jit(solution)/shard_map/ppermute | solution.py:459
  75.4 62.1 %all-to-all-start = ((bf16[8,144,2048]{2,1,0:T(8,128)(2,1)}), bf16[8,144,2048]{2,1,0:T(8,128)(2,1)}, u32[]{:S(2)}, u32[]{:S(2)}) async-start(bf16[8,144,2048]{2,1,0:T(8,128)(2,1)} %dispatch.2), calls=%async_computation | async-start | bytes 9437184 | tf_op jit(solution)/shard_map/all_to_all | solution.py:490
  82.9 145.5 %reduce-scatter.2.cloned.1.call-start = ((), (), s32[]{:S(2)}) async-start(), calls=%async_computation.3 | async-start | bytes 5308416 | tf_op jit(solution)/shard_map/reduce_scatter | solution.py:496
  88.4 16.1 %collective-permute-start.8 = (bf16[144,2048]{1,0:T(8,128)(2,1)}, bf16[144,2048]{1,0:T(8,128)(2,1)S(1)}, u32[]{:S(2)}, u32[]{:S(2)}) collective-permute-start(bf16[144,2048]{1,0:T(8,128)(2,1)} %get-tuple-element.47), channel_id=1, source_target_pairs={{0,8},{1,9},{2,10},{3,11},{4,12},{5,13},{6,14},{7,15},{8,16},{9,17... | collective-permute-start | bytes 1769480 | tf_op jit(solution)/shard_map/ppermute | solution.py:459
  88.5 30.3 %collective-permute-start.9 = (bf16[144,2048]{1,0:T(8,128)(2,1)}, bf16[144,2048]{1,0:T(8,128)(2,1)S(1)}, u32[]{:S(2)}, u32[]{:S(2)}) collective-permute-start(bf16[144,2048]{1,0:T(8,128)(2,1)} %get-tuple-element.48), channel_id=1, source_target_pairs={{0,24},{1,25},{2,26},{3,27},{4,28},{5,29},{6,30},{7,31},{8,0},{9,1... | collective-permute-start | bytes 1769480 | tf_op jit(solution)/shard_map/ppermute | solution.py:459
  91.2 54.4 %collective-permute-start.10 = (bf16[144,2048]{1,0:T(8,128)(2,1)}, bf16[144,2048]{1,0:T(8,128)(2,1)S(1)}, u32[]{:S(2)}, u32[]{:S(2)}) collective-permute-start(bf16[144,2048]{1,0:T(8,128)(2,1)} %get-tuple-element.49), channel_id=1, source_target_pairs={{0,16},{1,17},{2,18},{3,19},{4,20},{5,21},{6,22},{7,23},{8,24},{9,... | collective-permute-start | bytes 1769480 | tf_op jit(solution)/shard_map/ppermute | solution.py:459
  92.3 53.3 %collective-permute-start.11 = (bf16[144,2048]{1,0:T(8,128)(2,1)}, bf16[144,2048]{1,0:T(8,128)(2,1)S(1)}, u32[]{:S(2)}, u32[]{:S(2)}) collective-permute-start(bf16[144,2048]{1,0:T(8,128)(2,1)} %get-tuple-element.50), channel_id=1, source_target_pairs={{0,9},{1,8},{2,11},{3,10},{4,13},{5,12},{6,15},{7,14},{8,17},{9,16... | collective-permute-start | bytes 1769480 | tf_op jit(solution)/shard_map/ppermute | solution.py:459
  94.2 51.5 %collective-permute-start.12 = (bf16[144,2048]{1,0:T(8,128)(2,1)}, bf16[144,2048]{1,0:T(8,128)(2,1)S(1)}, u32[]{:S(2)}, u32[]{:S(2)}) collective-permute-start(bf16[144,2048]{1,0:T(8,128)(2,1)} %get-tuple-element.51), channel_id=1, source_target_pairs={{0,25},{1,24},{2,27},{3,26},{4,29},{5,28},{6,31},{7,30},{8,1},{9,0... | collective-permute-start | bytes 1769480 | tf_op jit(solution)/shard_map/ppermute | solution.py:459
  104.5 41.1 %collective-permute-start.13 = (bf16[144,2048]{1,0:T(8,128)(2,1)}, bf16[144,2048]{1,0:T(8,128)(2,1)S(1)}, u32[]{:S(2)}, u32[]{:S(2)}) collective-permute-start(bf16[144,2048]{1,0:T(8,128)(2,1)} %get-tuple-element.52), channel_id=1, source_target_pairs={{0,17},{1,16},{2,19},{3,18},{4,21},{5,20},{6,23},{7,22},{8,25},{9,... | collective-permute-start | bytes 1769480 | tf_op jit(solution)/shard_map/ppermute | solution.py:459
  118.8 26.9 %collective-permute-start.14 = (bf16[144,2048]{1,0:T(8,128)(2,1)}, bf16[144,2048]{1,0:T(8,128)(2,1)}, u32[]{:S(2)}, u32[]{:S(2)}) collective-permute-start(bf16[144,2048]{1,0:T(8,128)(2,1)} %get-tuple-element.53), channel_id=1, source_target_pairs={{0,1},{1,0},{2,3},{3,2},{4,5},{5,4},{6,7},{7,6},{8,9},{9,8},{10,11... | collective-permute-start | bytes 1769480 | tf_op jit(solution)/shard_map/ppermute | solution.py:459
  137.4 8.2 %copy-start.3 = (bf16[1,384,2048]{2,1,0:T(8,128)(2,1)S(1)}, bf16[1,384,2048]{2,1,0:T(8,128)(2,1)}, u32[]{:S(2)}) copy-start(bf16[1,384,2048]{2,1,0:T(8,128)(2,1)} %param.13) | copy-start | bytes 4718596
  137.5 8.2 %copy-start.4 = (bf16[144,2048]{1,0:T(8,128)(2,1)S(1)}, bf16[144,2048]{1,0:T(8,128)(2,1)}, u32[]{:S(2)}) copy-start(bf16[144,2048]{1,0:T(8,128)(2,1)} %get-tuple-element.46.refs_2_) | copy-start | bytes 1769476
  162.9 62.4 %copy-start.1 = (s32[128,8]{0,1:T(8,128)S(1)}, s32[128,8]{0,1:T(8,128)}, u32[]{:S(2)}) copy-start(s32[128,8]{0,1:T(8,128)} %param.10) | copy-start | bytes 12292
Sparse Core Ops, SparseCore 0:
  163.0 61.2 reduce-scatter.1

commit v5 on v4

--- a/solution.py
+++ b/solution.py
@@ -54,14 +54,13 @@
     return iota((rows, cols), 0) % (2 * REM) < REM
 
 
-def prepare_kernel(ids_ref, gates_ref, tokens_hbm, grads_hbm, tokens_out, grads_out, extra_ref, sems):
+def prepare_kernel(ids_ref, gates_ref, tokens_hbm, grads_hbm, tokens_out, grads_out, row_ref, sems):
     width = tokens_hbm.shape[1]
-    copies = [
-        pltpu.make_async_copy(tokens_hbm, tokens_out.at[:, :width], sems.at[0]),
-        pltpu.make_async_copy(grads_hbm, grads_out.at[:, :width], sems.at[1]),
+    loads = [
+        pltpu.make_async_copy(src, row_ref.at[n, :, :width], sems.at[n]) for n, src in enumerate((tokens_hbm, grads_hbm))
     ]
-    for copy in copies:
-        copy.start()
+    for load in loads:
+        load.start()
     pos, ids_t, ident = positions(ids_ref[...], 32)
     gates_t = gates_ref[...]
     weight = jnp.zeros(pos.shape, F32)
@@ -70,12 +69,15 @@
     high = weight.astype(BF).astype(F32)
     mid = (weight - high).astype(BF).astype(F32)
     low = weight - high - mid
-    extra_ref[...] = jnp.concatenate([pos, high, mid, low], axis=0).T.astype(BF)
+    extra = jnp.concatenate([pos, high, mid, low], axis=0).T.astype(BF)
+    stores = []
     for n, dst in enumerate((tokens_out, grads_out)):
-        copies.append(pltpu.make_async_copy(extra_ref, dst.at[:, width:], sems.at[2 + n]))
-        copies[-1].start()
-    for copy in copies:
-        copy.wait()
+        row_ref[n, :, width:] = extra
+        loads[n].wait()
+        stores.append(pltpu.make_async_copy(row_ref.at[n], dst, sems.at[2 + n]))
+        stores[-1].start()
+    for store in stores:
+        store.wait()
 
 
 HBM = pl.BlockSpec(memory_space=pltpu.HBM)
@@ -94,7 +96,7 @@
         out_shape=(shape, shape),
         in_specs=[VMEM, VMEM, HBM, HBM],
         out_specs=(HBM, HBM),
-        scratch_shapes=[pltpu.VMEM((toks, 128), BF), pltpu.SemaphoreType.DMA((4,))],
+        scratch_shapes=[pltpu.VMEM((2, toks, width + 128), BF), pltpu.SemaphoreType.DMA((4,))],
         compiler_params=pltpu.CompilerParams(vmem_limit_bytes=16 * MIB),
         cost_estimate=pl.CostEstimate(flops=1 << 20, bytes_accessed=2 * MIB, transcendentals=0),
         name="prepare",
@@ -189,112 +191,103 @@
     return block % 4 * 8 + block // 4 % 2 * 4 + block // 8
 
 
-def forward_kernel(*refs):
-    blocks, wg_hbm, wu_hbm = refs[:3]
-    cs_ref, at_ref, wcat_ref = refs[3:6]
-    x_ref, act_ref, turn_ref, sems = refs[6:]
-    rows = blocks.shape[1]
-    hidden = wg_hbm.shape[1]
-    loads = [
-        pltpu.make_async_copy(wg_hbm, wcat_ref.at[:, :hidden], sems.at[8]),
-        pltpu.make_async_copy(wu_hbm, wcat_ref.at[:, hidden:], sems.at[9]),
+def place_g(gs, at_row_ref, g_ref, sems):
+    rows = gs[0].shape[0]
+    copies = []
+    for k in sorted(range(8), key=lambda k: SPREAD[k]):
+        at = pl.ds(pl.multiple_of(at_row_ref[k], 16), rows)
+        copies.append(pltpu.make_async_copy(gs[k], g_ref.at[at, :], sems.at[k]))
+        copies[-1].start()
+    return copies
+
+
+def back_kernel(*refs):
+    at_row_ref, gs, (wd_ref, wg_ref, wu_ref) = refs[0], refs[1:9], refs[9:12]
+    out_ref, wcat_ref, g_ref, raw_ref, sems = refs[12:]
+    hidden = wd_ref.shape[0]
+    rows = gs[0].shape[0]
+    copies = place_g(gs, at_row_ref, g_ref, sems)
+    wcat_ref[:, :hidden] = wg_ref[...]
+    wcat_ref[:, hidden:] = wu_ref[...]
+    parts = 2
+    most = 8 // parts * rows
+    for i in range(parts):
+        for copy in copies[i * 8 // parts : (i + 1) * 8 // parts]:
+            copy.wait()
+        some = slice(i * most, (i + 1) * most)
+        raw_ref[some, :] = dot(g_ref[some, :], wd_ref[...], 1, 1)
+    per = MAIN + REM
+    for b in range(32):
+        to = regrouped(b)
+        out_ref[to * per : (to + 1) * per, :] = raw_ref[b * per : (b + 1) * per, :]
+
+
+def back(at_row, gs, wd, wg, wu):
+    hidden, width = wd.shape
+    rows = 8 * gs[0].shape[0]
+    smem = pl.BlockSpec(memory_space=pltpu.SMEM)
+    return pl.pallas_call(
+        back_kernel,
+        out_shape=(
+            jax.ShapeDtypeStruct((rows, hidden), F32),
+            jax.ShapeDtypeStruct((width, 2 * hidden), BF),
+        ),
+        in_specs=[smem] + [pl.BlockSpec(memory_space=pl.ANY)] * 8 + [VMEM] * 3,
+        out_specs=(VMEM, VMEM),
+        scratch_shapes=[
+            pltpu.VMEM((rows, width), BF),
+            pltpu.VMEM((rows, hidden), F32),
+            pltpu.SemaphoreType.DMA((8,)),
+        ],
+        compiler_params=pltpu.CompilerParams(vmem_limit_bytes=20 * MIB),
+        cost_estimate=pl.CostEstimate(flops=2 * rows * width * hidden, bytes_accessed=12 * MIB, transcendentals=0),
+        name="back",
+    )(at_row, *gs, wd, wg, wu)
+
+
+def middle_kernel(*refs):
+    to_ref, at_row_ref, gs, xs = refs[0], refs[1], refs[2:10], refs[10]
+    back_ref, wcat_ref, packed_hbm, pair_hbm = refs[11:15]
+    (g_ref, x_ref, act_ref, turn_ref, d_ref, dt_ref, at_ref, dm_ref, dr_ref, packed_ref,
+     pair_ref, sems, out_sems) = refs[15:]
+    rows = gs[0].shape[0]
+    copies = packed_ref.shape[0]
+    n, _, half = pair_ref.shape
+    both = wcat_ref.shape[1]
+    hidden = both // 2
+    per_block = MAIN + REM
+
+    x_in = [
+        pltpu.make_async_copy(xs.at[k], x_ref.at[k * rows : (k + 1) * rows, :], sems.at[8 + k]) for k in range(8)
     ]
-    loads += [
-        pltpu.make_async_copy(blocks.at[k], x_ref.at[k * rows : (k + 1) * rows, :], sems.at[k]) for k in range(8)
-    ]
-    for load in loads:
-        load.start()
-    loads[0].wait()
-    loads[1].wait()
+    for copy in x_in:
+        copy.start()
+    g_in = place_g(gs, at_row_ref, g_ref, sems)
+
     parts = 4
     most = 8 // parts * rows
     for i in range(parts):
-        for load in loads[2 + i * 8 // parts : 2 + (i + 1) * 8 // parts]:
-            load.wait()
+        for copy in x_in[i * 8 // parts : (i + 1) * 8 // parts]:
+            copy.wait()
         some = slice(i * most, (i + 1) * most)
         pre = dot(x_ref[some, :], wcat_ref[...])
         gate, up = pre[:, :hidden], pre[:, hidden:]
         sigma = jax.nn.sigmoid(gate)
         silu = gate * sigma
-        cs_ref[some, :hidden] = up * sigma * (1.0 + gate * (1.0 - sigma))
-        cs_ref[some, hidden:] = silu
+        d_act = back_ref[some, :]
+        d_ref[some, :hidden] = d_act * up * sigma * (1.0 + gate * (1.0 - sigma))
+        d_ref[some, hidden:] = d_act * silu
         act_ref[some, :] = silu * up
-    per = MAIN + REM
-    for b in range(32):
-        to = regrouped(b)
-        turn_ref[to * per : (to + 1) * per, :] = act_ref[b * per : (b + 1) * per, :]
-    at_ref[...] = turn_ref[...].astype(BF).T
-
-
-def forward(blocks, wg, wu):
-    width, hidden = wg.shape
-    rows = 8 * blocks.shape[1]
-    return pl.pallas_call(
-        forward_kernel,
-        out_shape=(
-            jax.ShapeDtypeStruct((rows, 2 * hidden), F32),
-            jax.ShapeDtypeStruct((hidden, rows), BF),
-            jax.ShapeDtypeStruct((width, 2 * hidden), BF),
-        ),
-        in_specs=[HBM] * 3,
-        out_specs=(VMEM,) * 3,
-        scratch_shapes=[
-            pltpu.VMEM((rows, width), BF),
-            pltpu.VMEM((rows, hidden), F32),
-            pltpu.VMEM((rows, hidden), F32),
-            pltpu.SemaphoreType.DMA((10,)),
-        ],
-        compiler_params=pltpu.CompilerParams(vmem_limit_bytes=20 * MIB),
-        cost_estimate=pl.CostEstimate(
-            flops=2 * rows * width * 2 * hidden, bytes_accessed=16 * MIB, transcendentals=rows * hidden
-        ),
-        name="forward",
-    )(*in_hbm(blocks, wg, wu))
-
-
-def middle_kernel(*refs):
-    to_ref, at_row_ref, gs, xs = refs[0], refs[1], refs[2:10], refs[10]
-    wd_ref, wcat_ref, cs_ref, at_ref = refs[11:15]
-    packed_hbm, pair_hbm = refs[15:17]
-    (g_ref, x_ref, raw_ref, turn_ref, d_ref, dt_ref, dm_ref, dr_ref, packed_ref,
-     pair_ref, sems, out_sems) = refs[17:]
-    rows = gs[0].shape[0]
-    copies = packed_ref.shape[0]
-    n, _, half = pair_ref.shape
-    hidden, both = at_ref.shape[0], wcat_ref.shape[1]
-    per_block = MAIN + REM
-
-    def load(src, dst, sem):
-        copy = pltpu.make_async_copy(src, dst, sems.at[sem])
-        copy.start()
-        return copy
-
-    order = sorted(range(8), key=lambda k: SPREAD[k])
-    g_in = [load(gs[k], g_ref.at[pl.ds(pl.multiple_of(at_row_ref[k], 16), rows), :], k) for k in order]
-    x_in = [load(xs.at[k], x_ref.at[k * rows : (k + 1) * rows, :], 8 + k) for k in range(8)]
-
-    parts = 2
-    most = 8 // parts * rows
-    for i in range(parts):
-        for copy in g_in[i * 8 // parts : (i + 1) * 8 // parts]:
-            copy.wait()
-        some = slice(i * most, (i + 1) * most)
-        raw_ref[some, :] = dot(g_ref[some, :], wd_ref[...], 1, 1)
+    dr_ref[...] = jnp.zeros_like(dr_ref)
     for b in range(n):
         to = regrouped(b)
-        turn_ref[to * per_block : (to + 1) * per_block, :] = raw_ref[b * per_block : (b + 1) * per_block, :]
-    for i in range(parts):
-        some = slice(i * most, (i + 1) * most)
-        d_act = turn_ref[some, :]
-        grad = jnp.concatenate([d_act, d_act], axis=1) * cs_ref[some, :]
-        d_ref[some, :] = grad
-    dt_ref[...] = d_ref[...].astype(BF).T
-    dr_ref[...] = jnp.zeros_like(dr_ref)
-    for b in range(n):
+        turn_ref[to * per_block : (to + 1) * per_block, :] = act_ref[b * per_block : (b + 1) * per_block, :]
         dm_ref[b * MAIN : (b + 1) * MAIN, :] = d_ref[b * per_block : b * per_block + MAIN, :].astype(BF)
         dr_ref[b * 2 * REM : b * 2 * REM + REM, :] = d_ref[b * per_block + MAIN : (b + 1) * per_block, :]
-
-    for copy in x_in:
+    dt_ref[...] = d_ref[...].astype(BF).T
+    at_ref[...] = turn_ref[...].astype(BF).T
+
+    for copy in g_in:
         copy.wait()
     tile = 256
     per = 2 * half // copies
@@ -315,7 +308,6 @@
     packed_out.start()
 
     sent = []
-    parts = 4
     step = n // parts
     most, few = step * MAIN, step * 2 * REM
     for i in range(parts):
@@ -339,16 +331,16 @@
     packed_out.wait()
 
 
-def middle(to, at_row, gs, xs, wd, wcat, cs, act, copies):
-    hidden, width = wd.shape
-    both, rows = cs.shape[1], cs.shape[0]
+def middle(to, at_row, gs, xs, back_x, wcat, copies):
+    width, both = wcat.shape
+    rows, hidden = back_x.shape
     n, half = to.shape[0], width // 2
     length = 3 * hidden * width // copies // 128
     smem = pl.BlockSpec(memory_space=pltpu.SMEM)
     return pl.pallas_call(
         middle_kernel,
         out_shape=(pltpu.HBM((copies, length, 128), BF), pltpu.HBM((n, PACK, half), BF)),
-        in_specs=[smem] * 2 + [pl.BlockSpec(memory_space=pl.ANY)] * 9 + [VMEM] * 4,
+        in_specs=[smem] * 2 + [pl.BlockSpec(memory_space=pl.ANY)] * 9 + [VMEM] * 2,
         out_specs=(HBM,) * 2,
         scratch_shapes=[
             pltpu.VMEM((rows, width), BF),
@@ -357,6 +349,7 @@
             pltpu.VMEM((rows, hidden), F32),
             pltpu.VMEM((rows, both), F32),
             pltpu.VMEM((both, rows), BF),
+            pltpu.VMEM((hidden, rows), BF),
             pltpu.VMEM((n * MAIN, both), BF),
             pltpu.VMEM((n * 2 * REM, both), F32),
             pltpu.VMEM((copies, length, 128), BF),
@@ -364,10 +357,12 @@
             pltpu.SemaphoreType.DMA((16,)),
             pltpu.SemaphoreType.DMA((n + 1,)),
         ],
-        compiler_params=pltpu.CompilerParams(vmem_limit_bytes=40 * MIB),
-        cost_estimate=pl.CostEstimate(flops=2 * rows * width * 6 * hidden, bytes_accessed=28 * MIB, transcendentals=0),
+        compiler_params=pltpu.CompilerParams(vmem_limit_bytes=42 * MIB),
+        cost_estimate=pl.CostEstimate(
+            flops=2 * rows * width * 7 * hidden, bytes_accessed=24 * MIB, transcendentals=rows * hidden
+        ),
         name="middle",
-    )(to, at_row, *gs, xs, wd, wcat, cs, act)
+    )(to, at_row, *gs, xs, back_x, wcat)
 
 
 def unpack_kernel(in_ref, gate_ref, up_ref, down_ref):
@@ -491,8 +486,8 @@
     along_x, _ = lax.optimization_barrier((along_x, out_x))
     out_g = dispatch(along_x, starts_g, lines_g, True)
     gs = [moved(v, d, 0, f) for v, (d, f) in zip(out_g, SPREAD)]
-    cs, act, wcat = forward(xs, wg, wu)
-    packed, outgoing = middle(origin, at_row, gs, xs, wd, wcat, cs, act, copies)
+    back_x, wcat = back(at_row, gs, wd, wg, wu)
+    packed, outgoing = middle(origin, at_row, gs, xs, back_x, wcat, copies)
     summed = lax.psum_scatter(packed, "dp", scatter_dimension=0, tiled=True)[0]
     ret = lax.all_to_all(outgoing, "expert", split_axis=0, concat_axis=0, tiled=True)
     grad_tokens = combine(ids_t, ret)

time: 238 us -> 228 us (0.958)
  Pallas kernels: 73.7 us -> 42.5 us
  local copies, waits for them, and re-layouts: 1.99 us -> 17.7 us
  waiting for transfers between devices: 43.8 us -> 49.2 us
    pallas_call x1, Pallas kernels: 32.9 us -> 2.1 us  [prepare(): pl.pallas_call(prepare_kernel, out_shape=(shape, shape), in_specs=[VMEM,...]
    ppermute x15, waiting for transfers between devices: 25.4 us -> 49.2 us  [moved(): return lax.ppermute(value, 'expert', pairs)]
    all_to_all x1, waiting for transfers between devices: 18.4 us -> 0.01 us  [shards(): lax.all_to_all(out_x, 'expert', split_axis=0, concat_axis=0, axis_index_g...]
    unnamed x18 -> x48, local copies, waits for them, and re-layouts: 1.4 us -> 17.1 us
    pallas_call x1, Pallas kernels: 8.17 us -> 4.92 us  [back(): pl.pallas_call(back_kernel, out_shape=(jax.ShapeDtypeStruct((rows, hidden...]
    pallas_call x1, Pallas kernels: 17.1 us -> 19.8 us  [middle(): pl.pallas_call(middle_kernel, out_shape=(pltpu.HBM((copies, length, 128),...]
  transfers between devices with their start and end apart: 17 -> 17, of which waited for: 6 -> 8; matrix products, arithmetic and copies ran while one was open for 0% -> 0% of each run, Pallas kernels for 7% -> 6%
where the time goes in v5:
time: 228 us; the launch traced here: 227 us
  blocking collectives  62.6 us (27%)
  waiting for transfers between devices  49.2 us (22%)
  Pallas kernels  42.5 us (19%)
  starting transfers between devices  40.8 us (18%)
  local copies, waits for them, and re-layouts  17.7 us (8%)
  between operations  14.4 us (6%)
    all_to_all x1, blocking collectives, shards(): lax.all_to_all(outgoing, 'expert', split_axis=0, concat_axis=0, tiled=True)  62.6 us
    ppermute x15, waiting for transfers between devices, moved(): return lax.ppermute(value, 'expert', pairs)  49.2 us
    ppermute x15, starting transfers between devices, moved(): return lax.ppermute(value, 'expert', pairs)  33.2 us
    pallas_call x1, Pallas kernels, middle(): pl.pallas_call(middle_kernel, out_shape=(pltpu.HBM((copies, length, 128),...  19.8 us
    unnamed x48, local copies, waits for them, and re-layouts  17.1 us
    pallas_call x2, Pallas kernels, dispatch(): pl.pallas_call(functools.partial(dispatch_kernel, scaled, per), out_shape...  10.5 us
    all_to_all x1, starting transfers between devices, shards(): lax.all_to_all(out_x, 'expert', split_axis=0, concat_axis=0, axis_index_g...  7.51 us
    pallas_call x1, Pallas kernels, back(): pl.pallas_call(back_kernel, out_shape=(jax.ShapeDtypeStruct((rows, hidden...  4.92 us
  transfers between devices with their start and end apart: 17, of which 8 were waited for; matrix products, arithmetic and copies ran while one was open for 0% of the time, Pallas kernels for 6%

profile of v5, /device:TPU:1, one launch (start us, length us, event | category | flops | bytes accessed | tf_op | source)
XLA Modules:
  0.0 227.1 jit_solution(3158302459323370009)
XLA Ops:
  7.2 0.7 copy-done.11
  7.9 0.7 copy-done.13
  8.5 2.1 prepare.1
  10.7 3.4 %collective-permute-start.2 = (bf16[128,2176]{1,0:T(8,128)(2,1)}, bf16[128,2176]{1,0:T(8,128)(2,1)S(1)}, u32[]{:S(2)}, u32[]{:S(2)}) collective-permute-start(bf16[128,2176]{1,0:T(8,128)(2,1)} %get-tuple-element.34.refs_0_), channel_id=1, source_target_pairs={{0,24},{1,25},{2,26},{3,27},{4,28},{5,29},{6,30},{7,31},{8,0},{9,1... | collective-permute-start | bytes 1671176 | tf_op jit(solution)/shard_map/ppermute | solution.py:454
  14.0 2.7 %collective-permute-start.6 = (bf16[128,2176]{1,0:T(8,128)(2,1)}, bf16[128,2176]{1,0:T(8,128)(2,1)S(1)}, u32[]{:S(2)}, u32[]{:S(2)}) collective-permute-start(bf16[128,2176]{1,0:T(8,128)(2,1)} %get-tuple-element.40.refs_0_), channel_id=1, source_target_pairs={{0,6},{1,7},{2,0},{3,1},{4,2},{5,3},{6,4},{7,5},{8,14},{9,15},{10,... | collective-permute-start | bytes 1671176 | tf_op jit(solution)/shard_map/ppermute | solution.py:454
  16.8 8.9 %collective-permute-done.2.refs_4_ = bf16[128,2176]{1,0:T(8,128)(2,1)S(1)} collective-permute-done((bf16[128,2176]{1,0:T(8,128)(2,1)}, bf16[128,2176]{1,0:T(8,128)(2,1)S(1)}, u32[]{:S(2)}, u32[]{:S(2)}) %collective-permute-start.2) | collective-permute-done | bytes 557088 | tf_op jit(solution)/shard_map/ppermute | solution.py:454
  25.7 3.4 %collective-permute-start.3 = (bf16[64,2176]{1,0:T(8,128)(2,1)S(1)}, bf16[64,2176]{1,0:T(8,128)(2,1)}, u32[]{:S(2)}, u32[]{:S(2)}) collective-permute-start(bf16[64,2176]{1,0:T(8,128)(2,1)S(1)} %slice.17), channel_id=1, source_target_pairs={{0,24},{1,25},{2,26},{3,27},{4,28},{5,29},{6,30},{7,31},{8,0},{9,1... | collective-permute-start | bytes 835592 | tf_op jit(solution)/shard_map/ppermute | solution.py:454
  29.1 0.1 collective-permute-start.1
  29.2 2.8 %collective-permute-start.7 = (bf16[64,2176]{1,0:T(8,128)(2,1)S(1)}, bf16[64,2176]{1,0:T(8,128)(2,1)S(1)}, u32[]{:S(2)}, u32[]{:S(2)}) collective-permute-start(bf16[64,2176]{1,0:T(8,128)(2,1)S(1)} %slice.19), channel_id=1, source_target_pairs={{0,6},{1,7},{2,0},{3,1},{4,2},{5,3},{6,4},{7,5},{8,14},{9,15},{10,... | collective-permute-start | bytes 835592 | tf_op jit(solution)/shard_map/ppermute | solution.py:454
  32.1 0.1 collective-permute-start.5
  32.2 0.1 stack.239
  32.3 1.2 collective-permute-done.3.refs_3_
  33.5 3.3 %collective-permute-done.1.refs_2_ = bf16[64,2176]{1,0:T(8,128)(2,1)} collective-permute-done((bf16[64,2176]{1,0:T(8,128)(2,1)S(1)}, bf16[64,2176]{1,0:T(8,128)(2,1)}, u32[]{:S(2)}, u32[]{:S(2)}) %collective-permute-start.1) | collective-permute-done | bytes 278560 | tf_op jit(solution)/shard_map/ppermute | solution.py:454
  36.8 2.6 %collective-permute-done.5.refs_2_ = bf16[64,2176]{1,0:T(8,128)(2,1)S(1)} collective-permute-done((bf16[64,2176]{1,0:T(8,128)(2,1)S(1)}, bf16[64,2176]{1,0:T(8,128)(2,1)S(1)}, u32[]{:S(2)}, u32[]{:S(2)}) %collective-permute-start.5) | collective-permute-done | bytes 278560 | tf_op jit(solution)/shard_map/ppermute | solution.py:454
  39.5 5.0 %dispatch.2 = bf16[8,144,2048]{2,1,0:T(8,128)(2,1)} custom-call(s32[8,128]{1,0:T(8,128)S(1)} %broadcast_in_dim.22.wanted_ref, s32[4]{0:T(128)S(1)} %iota_multiply_fusion.starts_ref, bf16[128,2176]{1,0:T(8,128)(2,1)} %get-tuple-element.34.refs_0_, bf16[128,2176]{1,0:T(8,128)(2,1)} %copy-done.21, bf16[64,2176]{1,0:T(8,128)(2,1)} %collective-permute-done.1.refs_2_, ...), custom_call_target="tpu_custom_call" | custom-call | flops 2415919104 | bytes 7340032 | tf_op jit(solution)/shard_map/dispatch/pallas_call | solution.py:169
  44.6 7.5 %all-to-all-start = ((bf16[8,144,2048]{2,1,0:T(8,128)(2,1)}), bf16[8,144,2048]{2,1,0:T(8,128)(2,1)}, u32[]{:S(2)}, u32[]{:S(2)}) async-start(bf16[8,144,2048]{2,1,0:T(8,128)(2,1)} %dispatch.2), calls=%async_computation | async-start | bytes 9437184 | tf_op jit(solution)/shard_map/all_to_all | solution.py:485
  52.2 0.1 stack.230
  52.4 5.4 %dispatch.3 = (bf16[144,2048]{1,0:T(8,128)(2,1)}, bf16[144,2048]{1,0:T(8,128)(2,1)}, bf16[144,2048]{1,0:T(8,128)(2,1)}, bf16[144,2048]{1,0:T(8,128)(2,1)}, bf16[...) custom-call(s32[8,128]{1,0:T(8,128)S(1)} %broadcast_in_dim.10.wanted_re, ...), custom_call_target="tpu_custom_call" | custom-call | flops 2415919104 | bytes 7340032 | tf_op jit(solution)/shard_map/dispatch/pallas_call | solution.py:169
  57.8 0.1 collective-permute-start.8
  57.9 2.7 %collective-permute-start.9 = (bf16[144,2048]{1,0:T(8,128)(2,1)}, bf16[144,2048]{1,0:T(8,128)(2,1)S(1)}, u32[]{:S(2)}, u32[]{:S(2)}) collective-permute-start(bf16[144,2048]{1,0:T(8,128)(2,1)} %get-tuple-element.47), channel_id=1, source_target_pairs={{0,24},{1,25},{2,26},{3,27},{4,28},{5,29},{6,30},{7,31},{8,0},{9,1... | collective-permute-start | bytes 1769480 | tf_op jit(solution)/shard_map/ppermute | solution.py:454
  60.7 1.1 collective-permute-start.10
  61.8 1.7 collective-permute-start.11
  63.5 1.2 collective-permute-start.12
  64.7 9.4 %collective-permute-done.8.refs_2_.refs_3_ = bf16[144,2048]{1,0:T(8,128)(2,1)S(1)} collective-permute-done((bf16[144,2048]{1,0:T(8,128)(2,1)}, bf16[144,2048]{1,0:T(8,128)(2,1)S(1)}, u32[]{:S(2)}, u32[]{:S(2)}) %collective-permute-start.8) | collective-permute-done | bytes 589856 | tf_op jit(solution)/shard_map/ppermute | solution.py:454
  74.1 0.8 copy-done.5
  74.9 13.9 %collective-permute-start.13 = (bf16[144,2048]{1,0:T(8,128)(2,1)}, bf16[144,2048]{1,0:T(8,128)(2,1)}, u32[]{:S(2)}, u32[]{:S(2)}) collective-permute-start(bf16[144,2048]{1,0:T(8,128)(2,1)} %get-tuple-element.51), channel_id=1, source_target_pairs={{0,17},{1,16},{2,19},{3,18},{4,21},{5,20},{6,23},{7,22},{8,25},{9,... | collective-permute-start | bytes 1769480 | tf_op jit(solution)/shard_map/ppermute | solution.py:454
  88.8 0.8 copy-done.8
  89.6 0.1 stack.221.refs_0_.refs_1_
  89.7 0.1 stack.212.refs_0_
  89.9 10.2 %collective-permute-done.11.refs_5_.refs_6_ = bf16[144,2048]{1,0:T(8,128)(2,1)} collective-permute-done((bf16[144,2048]{1,0:T(8,128)(2,1)}, bf16[144,2048]{1,0:T(8,128)(2,1)}, u32[]{:S(2)}, u32[]{:S(2)}) %collective-permute-start.11) | collective-permute-done | bytes 589856 | tf_op jit(solution)/shard_map/ppermute | solution.py:454
  100.1 11.0 %collective-permute-done.12.refs_6_.refs_7_ = bf16[144,2048]{1,0:T(8,128)(2,1)} collective-permute-done((bf16[144,2048]{1,0:T(8,128)(2,1)}, bf16[144,2048]{1,0:T(8,128)(2,1)}, u32[]{:S(2)}, u32[]{:S(2)}) %collective-permute-start.12) | collective-permute-done | bytes 589856 | tf_op jit(solution)/shard_map/ppermute | solution.py:454
  111.1 2.5 %collective-permute-done.13.refs_7_.refs_8_ = bf16[144,2048]{1,0:T(8,128)(2,1)} collective-permute-done((bf16[144,2048]{1,0:T(8,128)(2,1)}, bf16[144,2048]{1,0:T(8,128)(2,1)}, u32[]{:S(2)}, u32[]{:S(2)}) %collective-permute-start.13) | collective-permute-done | bytes 589856 | tf_op jit(solution)/shard_map/ppermute | solution.py:454
  113.6 1.4 copy-done.2
  115.0 1.1 copy-done.3
  116.1 1.1 copy-done.6
  117.2 1.1 copy-done.9
  118.2 4.9 %back.1 = (f32[1152,384]{1,0:T(8,128)S(1)}, bf16[2048,768]{1,0:T(8,128)(2,1)S(1)}) custom-call(s32[8]{0:T(128)S(1)} %stack.221.refs_0_.refs_1_, bf16[144,2048]{1,0:T(8,128)(2,1)S(1)} %copy-done.3, bf16[144,2048]{1,0:T(8,128)(2,1)S(1)} %copy-done.6, bf16[144,2048]{1,0:T(8,128)(2,1)S(1)} %copy-done.9, ...), custom_call_target="tpu_custom_call" | custom-call | flops 1811939328 | bytes 12582912 | tf_op jit(solution)/shard_map/back/pallas_call | solution.py:229
  123.2 1.7 copy-done.14
  124.9 1.2 copy-done.16
  126.1 1.1 copy-done.4
  127.2 1.1 copy-done.7
  128.2 1.1 copy-done.10
  129.3 1.9 copy-done.15
  131.2 1.5 copy-done.17
  132.7 19.8 %middle.1 = (bf16[8,2304,128]{2,1,0:T(8,128)(2,1)}, bf16[32,72,1024]{2,1,0:T(8,128)(2,1)}) custom-call(s32[32]{0:T(128)S(1)} %stack.212.refs_0_, s32[8]{0:T(128)S(1)} %stack.221.refs_0_.refs_1_, bf16[144,2048]{1,0:T(8,128)(2,1)S(1)} %copy-done.4, bf16[144,2048]{1,0:T(8,128)(2,1)S(1)} %copy-done.7, bf16[144,2048]{1,0:T(8,128)(2,1)S(1)} %copy-done.10, ...), custom_call_target="tpu_custom_call" | custom-call | flops 12683575296 | bytes 25165824 | tf_op jit(solution)/shard_map/middle/pallas_call | solution.py:340
  152.5 62.6 %all_to_all.10.ret_ref = bf16[32,72,1024]{2,1,0:T(8,128)(2,1)S(1)} all-to-all(bf16[32,72,1024]{2,1,0:T(8,128)(2,1)} %get-tuple-element.55), channel_id=1, replica_groups=mesh['dp'=8,'expert'=32] {'expert'}, dimensions={0} | all-to-all | bytes 9437184 | tf_op jit(solution)/shard_map/all_to_all | solution.py:492
  215.1 3.2 %combine.1 = bf16[128,2048]{1,0:T(8,128)(2,1)} custom-call(s32[8,128]{1,0:T(8,128)S(1)} %bitcast.69, bf16[32,72,1024]{2,1,0:T(8,128)(2,1)S(1)} %all_to_all.10.ret_ref), custom_call_target="tpu_custom_call" | custom-call | flops 671088640 | bytes 6291456 | tf_op jit(solution)/shard_map/combine/pallas_call | solution.py:423
  218.3 2.0 unpack.1
  (55 shorter events, 0.4 us)
Async XLA Ops:
  7.2 0.7 copy-start.11
  7.9 0.7 copy-start.13
  10.7 15.0 %collective-permute-start.2 = (bf16[128,2176]{1,0:T(8,128)(2,1)}, bf16[128,2176]{1,0:T(8,128)(2,1)S(1)}, u32[]{:S(2)}, u32[]{:S(2)}) collective-permute-start(bf16[128,2176]{1,0:T(8,128)(2,1)} %get-tuple-element.34.refs_0_), channel_id=1, source_target_pairs={{0,24},{1,25},{2,26},{3,27},{4,28},{5,29},{6,30},{7,31},{8,0},{9,1... | collective-permute-start | bytes 1671176 | tf_op jit(solution)/shard_map/ppermute | solution.py:454
  14.0 15.0 %collective-permute-start = (bf16[128,2176]{1,0:T(8,128)(2,1)}, bf16[128,2176]{1,0:T(8,128)(2,1)S(1)}, u32[]{:S(2)}, u32[]{:S(2)}) collective-permute-start(bf16[128,2176]{1,0:T(8,128)(2,1)} %get-tuple-element.34.refs_0_), channel_id=1, source_target_pairs={{0,8},{1,9},{2,10},{3,11},{4,12},{5,13},{6,14},{7,15},{8,16},{9,17... | collective-permute-start | bytes 1671176 | tf_op jit(solution)/shard_map/ppermute | solution.py:454
  14.0 15.1 %collective-permute-start.6 = (bf16[128,2176]{1,0:T(8,128)(2,1)}, bf16[128,2176]{1,0:T(8,128)(2,1)S(1)}, u32[]{:S(2)}, u32[]{:S(2)}) collective-permute-start(bf16[128,2176]{1,0:T(8,128)(2,1)} %get-tuple-element.40.refs_0_), channel_id=1, source_target_pairs={{0,6},{1,7},{2,0},{3,1},{4,2},{5,3},{6,4},{7,5},{8,14},{9,15},{10,... | collective-permute-start | bytes 1671176 | tf_op jit(solution)/shard_map/ppermute | solution.py:454
  16.8 15.3 %collective-permute-start.4 = (bf16[128,2176]{1,0:T(8,128)(2,1)}, bf16[128,2176]{1,0:T(8,128)(2,1)S(1)}, u32[]{:S(2)}, u32[]{:S(2)}) collective-permute-start(bf16[128,2176]{1,0:T(8,128)(2,1)} %get-tuple-element.40.refs_0_), channel_id=1, source_target_pairs={{0,2},{1,3},{2,4},{3,5},{4,6},{5,7},{6,0},{7,1},{8,10},{9,11},{10,... | collective-permute-start | bytes 1671176 | tf_op jit(solution)/shard_map/ppermute | solution.py:454
  25.6 13.8 %copy-start.20 = (bf16[128,2176]{1,0:T(8,128)(2,1)}, bf16[128,2176]{1,0:T(8,128)(2,1)S(1)}, u32[]{:S(2)}) copy-start(bf16[128,2176]{1,0:T(8,128)(2,1)S(1)} %collective-permute-done.2.refs_4_) | copy-start | bytes 1671172
  25.7 7.8 %collective-permute-start.3 = (bf16[64,2176]{1,0:T(8,128)(2,1)S(1)}, bf16[64,2176]{1,0:T(8,128)(2,1)}, u32[]{:S(2)}, u32[]{:S(2)}) collective-permute-start(bf16[64,2176]{1,0:T(8,128)(2,1)S(1)} %slice.17), channel_id=1, source_target_pairs={{0,24},{1,25},{2,26},{3,27},{4,28},{5,29},{6,30},{7,31},{8,0},{9,1... | collective-permute-start | bytes 835592 | tf_op jit(solution)/shard_map/ppermute | solution.py:454
  29.1 10.4 %copy-start.21 = (bf16[128,2176]{1,0:T(8,128)(2,1)}, bf16[128,2176]{1,0:T(8,128)(2,1)S(1)}, u32[]{:S(2)}) copy-start(bf16[128,2176]{1,0:T(8,128)(2,1)S(1)} %collective-permute-done.refs_1_) | copy-start | bytes 1671172
  29.1 7.7 %collective-permute-start.1 = (bf16[64,2176]{1,0:T(8,128)(2,1)S(1)}, bf16[64,2176]{1,0:T(8,128)(2,1)}, u32[]{:S(2)}, u32[]{:S(2)}) collective-permute-start(bf16[64,2176]{1,0:T(8,128)(2,1)S(1)} %slice.16), channel_id=1, source_target_pairs={{0,8},{1,9},{2,10},{3,11},{4,12},{5,13},{6,14},{7,15},{8,16},{9,17... | collective-permute-start | bytes 835592 | tf_op jit(solution)/shard_map/ppermute | solution.py:454
  29.2 2.9 %copy-start.18 = (bf16[128,2176]{1,0:T(8,128)(2,1)}, bf16[128,2176]{1,0:T(8,128)(2,1)S(1)}, u32[]{:S(2)}) copy-start(bf16[128,2176]{1,0:T(8,128)(2,1)S(1)} %collective-permute-done.6.refs_4_) | copy-start | bytes 1671172
  29.2 7.6 %collective-permute-start.7 = (bf16[64,2176]{1,0:T(8,128)(2,1)S(1)}, bf16[64,2176]{1,0:T(8,128)(2,1)S(1)}, u32[]{:S(2)}, u32[]{:S(2)}) collective-permute-start(bf16[64,2176]{1,0:T(8,128)(2,1)S(1)} %slice.19), channel_id=1, source_target_pairs={{0,6},{1,7},{2,0},{3,1},{4,2},{5,3},{6,4},{7,5},{8,14},{9,15},{10,... | collective-permute-start | bytes 835592 | tf_op jit(solution)/shard_map/ppermute | solution.py:454
  32.0 12.5 %copy-start.19 = (bf16[128,2176]{1,0:T(8,128)(2,1)}, bf16[128,2176]{1,0:T(8,128)(2,1)S(1)}, u32[]{:S(2)}) copy-start(bf16[128,2176]{1,0:T(8,128)(2,1)S(1)} %collective-permute-done.4.refs_1_) | copy-start | bytes 1671172
  32.1 7.3 %collective-permute-start.5 = (bf16[64,2176]{1,0:T(8,128)(2,1)S(1)}, bf16[64,2176]{1,0:T(8,128)(2,1)S(1)}, u32[]{:S(2)}, u32[]{:S(2)}) collective-permute-start(bf16[64,2176]{1,0:T(8,128)(2,1)S(1)} %slice.18), channel_id=1, source_target_pairs={{0,2},{1,3},{2,4},{3,5},{4,6},{5,7},{6,0},{7,1},{8,10},{9,11},{10,... | collective-permute-start | bytes 835592 | tf_op jit(solution)/shard_map/ppermute | solution.py:454
  36.8 7.7 %copy-start.22 = (bf16[64,2176]{1,0:T(8,128)(2,1)}, bf16[64,2176]{1,0:T(8,128)(2,1)S(1)}, u32[]{:S(2)}) copy-start(bf16[64,2176]{1,0:T(8,128)(2,1)S(1)} %collective-permute-done.7.refs_3_) | copy-start | bytes 835588
  39.4 5.1 %copy-start.23 = (bf16[64,2176]{1,0:T(8,128)(2,1)}, bf16[64,2176]{1,0:T(8,128)(2,1)S(1)}, u32[]{:S(2)}) copy-start(bf16[64,2176]{1,0:T(8,128)(2,1)S(1)} %collective-permute-done.5.refs_2_) | copy-start | bytes 835588
  44.6 81.5 %all-to-all-start = ((bf16[8,144,2048]{2,1,0:T(8,128)(2,1)}), bf16[8,144,2048]{2,1,0:T(8,128)(2,1)}, u32[]{:S(2)}, u32[]{:S(2)}) async-start(bf16[8,144,2048]{2,1,0:T(8,128)(2,1)} %dispatch.2), calls=%async_computation | async-start | bytes 9437184 | tf_op jit(solution)/shard_map/all_to_all | solution.py:485
  52.1 61.6 %copy-start = (bf16[1,384,2048]{2,1,0:T(8,128)(2,1)S(1)}, bf16[1,384,2048]{2,1,0:T(8,128)(2,1)}, u32[]{:S(2)}) copy-start(bf16[1,384,2048]{2,1,0:T(8,128)(2,1)} %param.13) | copy-start | bytes 4718596
  52.1 61.6 %copy-start.1 = (bf16[1,2048,384]{2,1,0:T(8,128)(2,1)S(1)}, bf16[1,2048,384]{2,1,0:T(8,128)(2,1)}, u32[]{:S(2)}) copy-start(bf16[1,2048,384]{2,1,0:T(8,128)(2,1)} %param.11) | copy-start | bytes 4718596
  52.1 166.2 %reduce-scatter.2.cloned.1.call-start = ((), (), s32[]{:S(2)}) async-start(), calls=%async_computation.3 | async-start | bytes 5308416 | tf_op jit(solution)/shard_map/reduce_scatter | solution.py:491
  57.8 16.3 %collective-permute-start.8 = (bf16[144,2048]{1,0:T(8,128)(2,1)}, bf16[144,2048]{1,0:T(8,128)(2,1)S(1)}, u32[]{:S(2)}, u32[]{:S(2)}) collective-permute-start(bf16[144,2048]{1,0:T(8,128)(2,1)} %get-tuple-element.46), channel_id=1, source_target_pairs={{0,8},{1,9},{2,10},{3,11},{4,12},{5,13},{6,14},{7,15},{8,16},{9,17... | collective-permute-start | bytes 1769480 | tf_op jit(solution)/shard_map/ppermute | solution.py:454
  57.9 30.9 %collective-permute-start.9 = (bf16[144,2048]{1,0:T(8,128)(2,1)}, bf16[144,2048]{1,0:T(8,128)(2,1)S(1)}, u32[]{:S(2)}, u32[]{:S(2)}) collective-permute-start(bf16[144,2048]{1,0:T(8,128)(2,1)} %get-tuple-element.47), channel_id=1, source_target_pairs={{0,24},{1,25},{2,26},{3,27},{4,28},{5,29},{6,30},{7,31},{8,0},{9,1... | collective-permute-start | bytes 1769480 | tf_op jit(solution)/shard_map/ppermute | solution.py:454
  60.7 29.2 %collective-permute-start.10 = (bf16[144,2048]{1,0:T(8,128)(2,1)}, bf16[144,2048]{1,0:T(8,128)(2,1)}, u32[]{:S(2)}, u32[]{:S(2)}) collective-permute-start(bf16[144,2048]{1,0:T(8,128)(2,1)} %get-tuple-element.48), channel_id=1, source_target_pairs={{0,16},{1,17},{2,18},{3,19},{4,20},{5,21},{6,22},{7,23},{8,24},{9,... | collective-permute-start | bytes 1769480 | tf_op jit(solution)/shard_map/ppermute | solution.py:454
  61.8 38.3 %collective-permute-start.11 = (bf16[144,2048]{1,0:T(8,128)(2,1)}, bf16[144,2048]{1,0:T(8,128)(2,1)}, u32[]{:S(2)}, u32[]{:S(2)}) collective-permute-start(bf16[144,2048]{1,0:T(8,128)(2,1)} %get-tuple-element.49), channel_id=1, source_target_pairs={{0,9},{1,8},{2,11},{3,10},{4,13},{5,12},{6,15},{7,14},{8,17},{9,16... | collective-permute-start | bytes 1769480 | tf_op jit(solution)/shard_map/ppermute | solution.py:454
  63.5 47.6 %collective-permute-start.12 = (bf16[144,2048]{1,0:T(8,128)(2,1)}, bf16[144,2048]{1,0:T(8,128)(2,1)}, u32[]{:S(2)}, u32[]{:S(2)}) collective-permute-start(bf16[144,2048]{1,0:T(8,128)(2,1)} %get-tuple-element.50), channel_id=1, source_target_pairs={{0,25},{1,24},{2,27},{3,26},{4,29},{5,28},{6,31},{7,30},{8,1},{9,0... | collective-permute-start | bytes 1769480 | tf_op jit(solution)/shard_map/ppermute | solution.py:454
  74.1 0.8 copy-start.5
  74.9 38.7 %collective-permute-start.13 = (bf16[144,2048]{1,0:T(8,128)(2,1)}, bf16[144,2048]{1,0:T(8,128)(2,1)}, u32[]{:S(2)}, u32[]{:S(2)}) collective-permute-start(bf16[144,2048]{1,0:T(8,128)(2,1)} %get-tuple-element.51), channel_id=1, source_target_pairs={{0,17},{1,16},{2,19},{3,18},{4,21},{5,20},{6,23},{7,22},{8,25},{9,... | collective-permute-start | bytes 1769480 | tf_op jit(solution)/shard_map/ppermute | solution.py:454
  88.8 0.8 copy-start.8
  89.6 24.0 %collective-permute-start.14 = (bf16[144,2048]{1,0:T(8,128)(2,1)}, bf16[144,2048]{1,0:T(8,128)(2,1)}, u32[]{:S(2)}, u32[]{:S(2)}) collective-permute-start(bf16[144,2048]{1,0:T(8,128)(2,1)} %get-tuple-element.52), channel_id=1, source_target_pairs={{0,1},{1,0},{2,3},{3,2},{4,5},{5,4},{6,7},{7,6},{8,9},{9,8},{10,11... | collective-permute-start | bytes 1769480 | tf_op jit(solution)/shard_map/ppermute | solution.py:454
  113.6 1.4 copy-start.2
  115.0 1.1 copy-start.3
  116.1 1.1 copy-start.6
  117.2 1.1 copy-start.9
  123.2 1.7 copy-start.14
  124.9 1.2 copy-start.16
  126.1 1.1 copy-start.4
  127.2 1.1 copy-start.7
  128.2 1.1 copy-start.10
  129.3 1.9 copy-start.15
  131.2 1.5 copy-start.17
  152.5 62.6 %copy-start.12 = (s32[128,8]{0,1:T(8,128)S(1)}, s32[128,8]{0,1:T(8,128)}, u32[]{:S(2)}) copy-start(s32[128,8]{0,1:T(8,128)} %param.10) | copy-start | bytes 12292
Sparse Core Ops, SparseCore 0:
  152.6 61.5 reduce-scatter.1

commit v6 on v4

--- a/solution.py
+++ b/solution.py
@@ -54,14 +54,16 @@
     return iota((rows, cols), 0) % (2 * REM) < REM
 
 
-def prepare_kernel(ids_ref, gates_ref, tokens_hbm, grads_hbm, tokens_out, grads_out, extra_ref, sems):
+def prepare_kernel(ids_hbm, gates_hbm, tokens_hbm, grads_hbm, tokens_out, grads_out, row_ref, ids_ref, gates_ref, sems):
     width = tokens_hbm.shape[1]
-    copies = [
-        pltpu.make_async_copy(tokens_hbm, tokens_out.at[:, :width], sems.at[0]),
-        pltpu.make_async_copy(grads_hbm, grads_out.at[:, :width], sems.at[1]),
+    loads = [
+        pltpu.make_async_copy(src, row_ref.at[n, :, :width], sems.at[n]) for n, src in enumerate((tokens_hbm, grads_hbm))
     ]
-    for copy in copies:
-        copy.start()
+    small = [pltpu.make_async_copy(ids_hbm, ids_ref, sems.at[4]), pltpu.make_async_copy(gates_hbm, gates_ref, sems.at[5])]
+    for load in small + loads:
+        load.start()
+    for load in small:
+        load.wait()
     pos, ids_t, ident = positions(ids_ref[...], 32)
     gates_t = gates_ref[...]
     weight = jnp.zeros(pos.shape, F32)
@@ -70,12 +72,15 @@
     high = weight.astype(BF).astype(F32)
     mid = (weight - high).astype(BF).astype(F32)
     low = weight - high - mid
-    extra_ref[...] = jnp.concatenate([pos, high, mid, low], axis=0).T.astype(BF)
+    extra = jnp.concatenate([pos, high, mid, low], axis=0).T.astype(BF)
+    stores = []
     for n, dst in enumerate((tokens_out, grads_out)):
-        copies.append(pltpu.make_async_copy(extra_ref, dst.at[:, width:], sems.at[2 + n]))
-        copies[-1].start()
-    for copy in copies:
-        copy.wait()
+        row_ref[n, :, width:] = extra
+        loads[n].wait()
+        stores.append(pltpu.make_async_copy(row_ref.at[n], dst, sems.at[2 + n]))
+        stores[-1].start()
+    for store in stores:
+        store.wait()
 
 
 HBM = pl.BlockSpec(memory_space=pltpu.HBM)
@@ -92,13 +97,18 @@
     return pl.pallas_call(
         prepare_kernel,
         out_shape=(shape, shape),
-        in_specs=[VMEM, VMEM, HBM, HBM],
+        in_specs=[HBM] * 4,
         out_specs=(HBM, HBM),
-        scratch_shapes=[pltpu.VMEM((toks, 128), BF), pltpu.SemaphoreType.DMA((4,))],
+        scratch_shapes=[
+            pltpu.VMEM((2, toks, width + 128), BF),
+            pltpu.VMEM(ids.shape, ids.dtype),
+            pltpu.VMEM(gates.shape, F32),
+            pltpu.SemaphoreType.DMA((6,)),
+        ],
         compiler_params=pltpu.CompilerParams(vmem_limit_bytes=16 * MIB),
         cost_estimate=pl.CostEstimate(flops=1 << 20, bytes_accessed=2 * MIB, transcendentals=0),
         name="prepare",
-    )(ids, gates, *in_hbm(tokens, grads))
+    )(*in_hbm(ids, gates, tokens, grads))
 
 
 def dispatch_kernel(scaled, per, wanted_ref, starts_ref, *refs):

time: 238 us -> 206 us (0.87)
  Pallas kernels: 73.7 us -> 43 us
    pallas_call x1, Pallas kernels: 32.9 us -> 2.14 us  [prepare(): pl.pallas_call(prepare_kernel, out_shape=(shape, shape), in_specs=[HBM] *...]
  transfers between devices with their start and end apart: 17 -> 17, of which waited for: 6 -> 6; matrix products, arithmetic and copies ran while one was open for 0% -> 0% of each run, Pallas kernels for 7% -> 8%
where the time goes in v6:
time: 206 us; the launch traced here: 205 us
  blocking collectives  62.4 us (30%)
  waiting for transfers between devices  43.8 us (21%)
  Pallas kernels  43 us (21%)
  starting transfers between devices  41.2 us (20%)
  between operations  14.3 us (7%)
    all_to_all x1, blocking collectives, shards(): lax.all_to_all(outgoing, 'expert', split_axis=0, concat_axis=0, tiled=True)  62.4 us
    ppermute x15, starting transfers between devices, moved(): return lax.ppermute(value, 'expert', pairs)  33.6 us
    ppermute x15, waiting for transfers between devices, moved(): return lax.ppermute(value, 'expert', pairs)  25.4 us
    all_to_all x1, waiting for transfers between devices, shards(): lax.all_to_all(out_x, 'expert', split_axis=0, concat_axis=0, axis_index_g...  18.4 us
    pallas_call x1, Pallas kernels, middle(): pl.pallas_call(middle_kernel, out_shape=(pltpu.HBM((copies, length, 128),...  17.1 us
    pallas_call x2, Pallas kernels, dispatch(): pl.pallas_call(functools.partial(dispatch_kernel, scaled, per), out_shape...  10.3 us
    pallas_call x1, Pallas kernels, forward(): pl.pallas_call(forward_kernel, out_shape=(jax.ShapeDtypeStruct((rows, 2 *...  8.17 us
    all_to_all x1, starting transfers between devices, shards(): lax.all_to_all(out_x, 'expert', split_axis=0, concat_axis=0, axis_index_g...  7.52 us
  transfers between devices with their start and end apart: 17, of which 6 were waited for; matrix products, arithmetic and copies ran while one was open for 0% of the time, Pallas kernels for 8%

profile of v6, /device:TPU:1, one launch (start us, length us, event | category | flops | bytes accessed | tf_op | source)
XLA Modules:
  0.0 205.2 jit_solution(17148147937273277395)
XLA Ops:
  7.2 2.1 %prepare.1 = (bf16[128,2176]{1,0:T(8,128)(2,1)}, bf16[128,2176]{1,0:T(8,128)(2,1)}) custom-call(s32[8,128]{1,0:T(8,128)} %bitcast.65, f32[8,128]{1,0:T(8,128)} %bitcast.69, bf16[128,2048]{1,0:T(8,128)(2,1)} %tokens_hbm.1, bf16[128,2048]{1,0:T(8,128)(2,1)} %grads_hbm.1), custom_call_target="tpu_custom_call" | custom-call | flops 1048576 | bytes 2097152 | tf_op jit(solution)/shard_map/prepare/pallas_call | solution.py:97
  9.3 3.4 %collective-permute-start.2 = (bf16[128,2176]{1,0:T(8,128)(2,1)}, bf16[128,2176]{1,0:T(8,128)(2,1)S(1)}, u32[]{:S(2)}, u32[]{:S(2)}) collective-permute-start(bf16[128,2176]{1,0:T(8,128)(2,1)} %get-tuple-element.35.refs_0_), channel_id=1, source_target_pairs={{0,24},{1,25},{2,26},{3,27},{4,28},{5,29},{6,30},{7,31},{8,0},{9,1... | collective-permute-start | bytes 1671176 | tf_op jit(solution)/shard_map/ppermute | solution.py:469
  12.7 0.0 collective-permute-start
  12.7 2.7 %collective-permute-start.6 = (bf16[128,2176]{1,0:T(8,128)(2,1)}, bf16[128,2176]{1,0:T(8,128)(2,1)S(1)}, u32[]{:S(2)}, u32[]{:S(2)}) collective-permute-start(bf16[128,2176]{1,0:T(8,128)(2,1)} %get-tuple-element.41.refs_0_), channel_id=1, source_target_pairs={{0,6},{1,7},{2,0},{3,1},{4,2},{5,3},{6,4},{7,5},{8,14},{9,15},{10,... | collective-permute-start | bytes 1671176 | tf_op jit(solution)/shard_map/ppermute | solution.py:469
  15.4 0.0 collective-permute-start.4
  15.4 8.9 %collective-permute-done.2.refs_4_ = bf16[128,2176]{1,0:T(8,128)(2,1)S(1)} collective-permute-done((bf16[128,2176]{1,0:T(8,128)(2,1)}, bf16[128,2176]{1,0:T(8,128)(2,1)S(1)}, u32[]{:S(2)}, u32[]{:S(2)}) %collective-permute-start.2) | collective-permute-done | bytes 557088 | tf_op jit(solution)/shard_map/ppermute | solution.py:469
  24.3 3.4 %collective-permute-start.3 = (bf16[64,2176]{1,0:T(8,128)(2,1)S(1)}, bf16[64,2176]{1,0:T(8,128)(2,1)}, u32[]{:S(2)}, u32[]{:S(2)}) collective-permute-start(bf16[64,2176]{1,0:T(8,128)(2,1)S(1)} %slice.17), channel_id=1, source_target_pairs={{0,24},{1,25},{2,26},{3,27},{4,28},{5,29},{6,30},{7,31},{8,0},{9,1... | collective-permute-start | bytes 835592 | tf_op jit(solution)/shard_map/ppermute | solution.py:469
  27.7 0.0 collective-permute-done.refs_1_
  27.8 0.1 collective-permute-start.1
  27.8 0.0 collective-permute-done.6.refs_4_
  27.9 2.8 %collective-permute-start.7 = (bf16[64,2176]{1,0:T(8,128)(2,1)S(1)}, bf16[64,2176]{1,0:T(8,128)(2,1)}, u32[]{:S(2)}, u32[]{:S(2)}) collective-permute-start(bf16[64,2176]{1,0:T(8,128)(2,1)S(1)} %slice.19), channel_id=1, source_target_pairs={{0,6},{1,7},{2,0},{3,1},{4,2},{5,3},{6,4},{7,5},{8,14},{9,15},{10,... | collective-permute-start | bytes 835592 | tf_op jit(solution)/shard_map/ppermute | solution.py:469
  30.7 0.0 collective-permute-done.4.refs_1_
  30.7 0.1 collective-permute-start.5
  30.9 0.1 stack.239
  31.0 1.2 collective-permute-done.3.refs_3_
  32.1 3.3 %collective-permute-done.1.refs_2_ = bf16[64,2176]{1,0:T(8,128)(2,1)} collective-permute-done((bf16[64,2176]{1,0:T(8,128)(2,1)S(1)}, bf16[64,2176]{1,0:T(8,128)(2,1)}, u32[]{:S(2)}, u32[]{:S(2)}) %collective-permute-start.1) | collective-permute-done | bytes 278560 | tf_op jit(solution)/shard_map/ppermute | solution.py:469
  35.5 0.0 collective-permute-done.7.refs_3_
  35.5 2.7 %collective-permute-done.5.refs_2_ = bf16[64,2176]{1,0:T(8,128)(2,1)} collective-permute-done((bf16[64,2176]{1,0:T(8,128)(2,1)S(1)}, bf16[64,2176]{1,0:T(8,128)(2,1)}, u32[]{:S(2)}, u32[]{:S(2)}) %collective-permute-start.5) | collective-permute-done | bytes 278560 | tf_op jit(solution)/shard_map/ppermute | solution.py:469
  38.2 0.1 broadcast_in_dim.22.wanted_ref
  38.2 5.0 %dispatch.2 = bf16[8,144,2048]{2,1,0:T(8,128)(2,1)} custom-call(s32[8,128]{1,0:T(8,128)S(1)} %broadcast_in_dim.22.wanted_ref, s32[4]{0:T(128)S(1)} %iota_multiply_fusion.starts_ref, bf16[128,2176]{1,0:T(8,128)(2,1)} %get-tuple-element.35.refs_0_, bf16[128,2176]{1,0:T(8,128)(2,1)} %copy-done.6, bf16[64,2176]{1,0:T(8,128)(2,1)} %collective-permute-done.1.refs_2_, ...), custom_call_target="tpu_custom_call" | custom-call | flops 2415919104 | bytes 7340032 | tf_op jit(solution)/shard_map/dispatch/pallas_call | solution.py:177
  43.3 7.5 %all-to-all-start = ((bf16[8,144,2048]{2,1,0:T(8,128)(2,1)}), bf16[8,144,2048]{2,1,0:T(8,128)(2,1)}, u32[]{:S(2)}, u32[]{:S(2)}) async-start(bf16[8,144,2048]{2,1,0:T(8,128)(2,1)} %dispatch.2), calls=%async_computation | async-start | bytes 9437184 | tf_op jit(solution)/shard_map/all_to_all | solution.py:500
  50.8 0.1 stack.230
  50.9 0.1 broadcast_in_dim.10.wanted_ref
  50.9 5.3 %dispatch.3 = (bf16[144,2048]{1,0:T(8,128)(2,1)}, bf16[144,2048]{1,0:T(8,128)(2,1)}, bf16[144,2048]{1,0:T(8,128)(2,1)}, bf16[144,2048]{1,0:T(8,128)(2,1)}, bf16[...) custom-call(s32[8,128]{1,0:T(8,128)S(1)} %broadcast_in_dim.10.wanted_re, ...), custom_call_target="tpu_custom_call" | custom-call | flops 2415919104 | bytes 7340032 | tf_op jit(solution)/shard_map/dispatch/pallas_call | solution.py:177
  56.3 0.1 collective-permute-start.8
  56.4 2.7 %collective-permute-start.9 = (bf16[144,2048]{1,0:T(8,128)(2,1)}, bf16[144,2048]{1,0:T(8,128)(2,1)S(1)}, u32[]{:S(2)}, u32[]{:S(2)}) collective-permute-start(bf16[144,2048]{1,0:T(8,128)(2,1)} %get-tuple-element.48), channel_id=1, source_target_pairs={{0,24},{1,25},{2,26},{3,27},{4,28},{5,29},{6,30},{7,31},{8,0},{9,1... | collective-permute-start | bytes 1769480 | tf_op jit(solution)/shard_map/ppermute | solution.py:469
  59.1 1.1 collective-permute-start.10
  60.2 1.9 collective-permute-start.11
  62.1 1.1 collective-permute-start.12
  63.2 9.2 %collective-permute-done.8.refs_3_ = bf16[144,2048]{1,0:T(8,128)(2,1)S(1)} collective-permute-done((bf16[144,2048]{1,0:T(8,128)(2,1)}, bf16[144,2048]{1,0:T(8,128)(2,1)S(1)}, u32[]{:S(2)}, u32[]{:S(2)}) %collective-permute-start.8) | collective-permute-done | bytes 589856 | tf_op jit(solution)/shard_map/ppermute | solution.py:469
  72.4 14.3 %collective-permute-start.13 = (bf16[144,2048]{1,0:T(8,128)(2,1)}, bf16[144,2048]{1,0:T(8,128)(2,1)S(1)}, u32[]{:S(2)}, u32[]{:S(2)}) collective-permute-start(bf16[144,2048]{1,0:T(8,128)(2,1)} %get-tuple-element.52), channel_id=1, source_target_pairs={{0,17},{1,16},{2,19},{3,18},{4,21},{5,20},{6,23},{7,22},{8,25},{9,... | collective-permute-start | bytes 1769480 | tf_op jit(solution)/shard_map/ppermute | solution.py:469
  86.7 0.0 collective-permute-done.9.refs_4_
  86.7 0.0 collective-permute-start.14
  86.7 0.1 stack.221.refs_1_
  86.8 0.1 stack.212.refs_0_
  86.9 18.4 %all-to-all-done.refs_0_.refs_10_ = bf16[8,144,2048]{2,1,0:T(8,128)(2,1)} async-done(((bf16[8,144,2048]{2,1,0:T(8,128)(2,1)}), bf16[8,144,2048]{2,1,0:T(8,128)(2,1)}, u32[]{:S(2)}, u32[]{:S(2)}) %all-to-all-start) | async-done | bytes 4718624 | tf_op jit(solution)/shard_map/all_to_all | solution.py:500
  105.3 8.2 %forward.1 = (f32[1152,768]{1,0:T(8,128)S(1)}, bf16[384,1152]{1,0:T(8,128)(2,1)S(1)}, bf16[2048,768]{1,0:T(8,128)(2,1)S(1)}) custom-call(bf16[8,144,2048]{2,1,0:T(8,128)(2,1)} %all-to-all-done.refs_0_.refs_10_, bf16[2048,384]{1,0:T(8,128)(2,1)} %bitcast.70, bf16[2048,384]{1,0:T(8,128)(2,1)} %bitcast.71), custom_call_target="tpu_custom_call" | custom-call | flops 3623878656 | bytes 16777216 | tf_op jit(solution)/shard_map/forward/pallas_call | solution.py:242
  113.5 0.0 collective-permute-done.10.refs_5_
  113.5 0.0 collective-permute-done.11.refs_6_
  113.5 0.0 collective-permute-done.12.refs_7_
  113.5 0.0 collective-permute-done.13.refs_8_
  113.6 0.0 collective-permute-done.14.refs_9_
  113.6 17.1 %middle.1 = (bf16[8,2304,128]{2,1,0:T(8,128)(2,1)}, bf16[32,72,1024]{2,1,0:T(8,128)(2,1)}) custom-call(s32[32]{0:T(128)S(1)} %stack.212.refs_0_, s32[8]{0:T(128)S(1)} %stack.221.refs_1_, bf16[144,2048]{1,0:T(8,128)(2,1)S(1)} %copy-done.2, bf16[144,2048]{1,0:T(8,128)(2,1)S(1)} %collective-permute-done.8.refs_3_, ...), custom_call_target="tpu_custom_call" | custom-call | flops 10871635968 | bytes 29360128 | tf_op jit(solution)/shard_map/middle/pallas_call | solution.py:358
  130.7 0.0 reduce-scatter.2.cloned.1.call-update
  130.7 0.0 copy-start
  130.8 62.4 %all_to_all.10.ret_ref = bf16[32,72,1024]{2,1,0:T(8,128)(2,1)S(1)} all-to-all(bf16[32,72,1024]{2,1,0:T(8,128)(2,1)} %get-tuple-element.57), channel_id=1, replica_groups=mesh['dp'=8,'expert'=32] {'expert'}, dimensions={0} | all-to-all | bytes 9437184 | tf_op jit(solution)/shard_map/all_to_all | solution.py:507
  193.2 3.2 %combine.1 = bf16[128,2048]{1,0:T(8,128)(2,1)} custom-call(s32[8,128]{1,0:T(8,128)S(1)} %bitcast.66, bf16[32,72,1024]{2,1,0:T(8,128)(2,1)S(1)} %all_to_all.10.ret_ref), custom_call_target="tpu_custom_call" | custom-call | flops 671088640 | bytes 6291456 | tf_op jit(solution)/shard_map/combine/pallas_call | solution.py:438
  196.4 2.0 unpack.1
  (21 shorter events, 0.1 us)
Async XLA Ops:
  9.3 15.0 %collective-permute-start.2 = (bf16[128,2176]{1,0:T(8,128)(2,1)}, bf16[128,2176]{1,0:T(8,128)(2,1)S(1)}, u32[]{:S(2)}, u32[]{:S(2)}) collective-permute-start(bf16[128,2176]{1,0:T(8,128)(2,1)} %get-tuple-element.35.refs_0_), channel_id=1, source_target_pairs={{0,24},{1,25},{2,26},{3,27},{4,28},{5,29},{6,30},{7,31},{8,0},{9,1... | collective-permute-start | bytes 1671176 | tf_op jit(solution)/shard_map/ppermute | solution.py:469
  12.7 15.0 %collective-permute-start = (bf16[128,2176]{1,0:T(8,128)(2,1)}, bf16[128,2176]{1,0:T(8,128)(2,1)S(1)}, u32[]{:S(2)}, u32[]{:S(2)}) collective-permute-start(bf16[128,2176]{1,0:T(8,128)(2,1)} %get-tuple-element.35.refs_0_), channel_id=1, source_target_pairs={{0,8},{1,9},{2,10},{3,11},{4,12},{5,13},{6,14},{7,15},{8,16},{9,17... | collective-permute-start | bytes 1671176 | tf_op jit(solution)/shard_map/ppermute | solution.py:469
  12.7 15.1 %collective-permute-start.6 = (bf16[128,2176]{1,0:T(8,128)(2,1)}, bf16[128,2176]{1,0:T(8,128)(2,1)S(1)}, u32[]{:S(2)}, u32[]{:S(2)}) collective-permute-start(bf16[128,2176]{1,0:T(8,128)(2,1)} %get-tuple-element.41.refs_0_), channel_id=1, source_target_pairs={{0,6},{1,7},{2,0},{3,1},{4,2},{5,3},{6,4},{7,5},{8,14},{9,15},{10,... | collective-permute-start | bytes 1671176 | tf_op jit(solution)/shard_map/ppermute | solution.py:469
  15.4 15.3 %collective-permute-start.4 = (bf16[128,2176]{1,0:T(8,128)(2,1)}, bf16[128,2176]{1,0:T(8,128)(2,1)S(1)}, u32[]{:S(2)}, u32[]{:S(2)}) collective-permute-start(bf16[128,2176]{1,0:T(8,128)(2,1)} %get-tuple-element.41.refs_0_), channel_id=1, source_target_pairs={{0,2},{1,3},{2,4},{3,5},{4,6},{5,7},{6,0},{7,1},{8,10},{9,11},{10,... | collective-permute-start | bytes 1671176 | tf_op jit(solution)/shard_map/ppermute | solution.py:469
  24.3 13.9 %copy-start.5 = (bf16[128,2176]{1,0:T(8,128)(2,1)}, bf16[128,2176]{1,0:T(8,128)(2,1)S(1)}, u32[]{:S(2)}) copy-start(bf16[128,2176]{1,0:T(8,128)(2,1)S(1)} %collective-permute-done.2.refs_4_) | copy-start | bytes 1671172
  24.3 7.8 %collective-permute-start.3 = (bf16[64,2176]{1,0:T(8,128)(2,1)S(1)}, bf16[64,2176]{1,0:T(8,128)(2,1)}, u32[]{:S(2)}, u32[]{:S(2)}) collective-permute-start(bf16[64,2176]{1,0:T(8,128)(2,1)S(1)} %slice.17), channel_id=1, source_target_pairs={{0,24},{1,25},{2,26},{3,27},{4,28},{5,29},{6,30},{7,31},{8,0},{9,1... | collective-permute-start | bytes 835592 | tf_op jit(solution)/shard_map/ppermute | solution.py:469
  27.7 10.5 %copy-start.6 = (bf16[128,2176]{1,0:T(8,128)(2,1)}, bf16[128,2176]{1,0:T(8,128)(2,1)S(1)}, u32[]{:S(2)}) copy-start(bf16[128,2176]{1,0:T(8,128)(2,1)S(1)} %collective-permute-done.refs_1_) | copy-start | bytes 1671172
  27.8 7.7 %collective-permute-start.1 = (bf16[64,2176]{1,0:T(8,128)(2,1)S(1)}, bf16[64,2176]{1,0:T(8,128)(2,1)}, u32[]{:S(2)}, u32[]{:S(2)}) collective-permute-start(bf16[64,2176]{1,0:T(8,128)(2,1)S(1)} %slice.16), channel_id=1, source_target_pairs={{0,8},{1,9},{2,10},{3,11},{4,12},{5,13},{6,14},{7,15},{8,16},{9,17... | collective-permute-start | bytes 835592 | tf_op jit(solution)/shard_map/ppermute | solution.py:469
  27.9 15.4 %copy-start.3 = (bf16[128,2176]{1,0:T(8,128)(2,1)}, bf16[128,2176]{1,0:T(8,128)(2,1)S(1)}, u32[]{:S(2)}) copy-start(bf16[128,2176]{1,0:T(8,128)(2,1)S(1)} %collective-permute-done.6.refs_4_) | copy-start | bytes 1671172
  27.9 7.6 %collective-permute-start.7 = (bf16[64,2176]{1,0:T(8,128)(2,1)S(1)}, bf16[64,2176]{1,0:T(8,128)(2,1)}, u32[]{:S(2)}, u32[]{:S(2)}) collective-permute-start(bf16[64,2176]{1,0:T(8,128)(2,1)S(1)} %slice.19), channel_id=1, source_target_pairs={{0,6},{1,7},{2,0},{3,1},{4,2},{5,3},{6,4},{7,5},{8,14},{9,15},{10,... | collective-permute-start | bytes 835592 | tf_op jit(solution)/shard_map/ppermute | solution.py:469
  30.7 12.5 %copy-start.4 = (bf16[128,2176]{1,0:T(8,128)(2,1)}, bf16[128,2176]{1,0:T(8,128)(2,1)S(1)}, u32[]{:S(2)}) copy-start(bf16[128,2176]{1,0:T(8,128)(2,1)S(1)} %collective-permute-done.4.refs_1_) | copy-start | bytes 1671172
  30.7 7.4 %collective-permute-start.5 = (bf16[64,2176]{1,0:T(8,128)(2,1)S(1)}, bf16[64,2176]{1,0:T(8,128)(2,1)}, u32[]{:S(2)}, u32[]{:S(2)}) collective-permute-start(bf16[64,2176]{1,0:T(8,128)(2,1)S(1)} %slice.18), channel_id=1, source_target_pairs={{0,2},{1,3},{2,4},{3,5},{4,6},{5,7},{6,0},{7,1},{8,10},{9,11},{10,... | collective-permute-start | bytes 835592 | tf_op jit(solution)/shard_map/ppermute | solution.py:469
  43.3 62.1 %all-to-all-start = ((bf16[8,144,2048]{2,1,0:T(8,128)(2,1)}), bf16[8,144,2048]{2,1,0:T(8,128)(2,1)}, u32[]{:S(2)}, u32[]{:S(2)}) async-start(bf16[8,144,2048]{2,1,0:T(8,128)(2,1)} %dispatch.2), calls=%async_computation | async-start | bytes 9437184 | tf_op jit(solution)/shard_map/all_to_all | solution.py:500
  50.8 145.6 %reduce-scatter.2.cloned.1.call-start = ((), (), s32[]{:S(2)}) async-start(), calls=%async_computation.3 | async-start | bytes 5308416 | tf_op jit(solution)/shard_map/reduce_scatter | solution.py:506
  56.3 16.1 %collective-permute-start.8 = (bf16[144,2048]{1,0:T(8,128)(2,1)}, bf16[144,2048]{1,0:T(8,128)(2,1)S(1)}, u32[]{:S(2)}, u32[]{:S(2)}) collective-permute-start(bf16[144,2048]{1,0:T(8,128)(2,1)} %get-tuple-element.47), channel_id=1, source_target_pairs={{0,8},{1,9},{2,10},{3,11},{4,12},{5,13},{6,14},{7,15},{8,16},{9,17... | collective-permute-start | bytes 1769480 | tf_op jit(solution)/shard_map/ppermute | solution.py:469
  56.4 30.3 %collective-permute-start.9 = (bf16[144,2048]{1,0:T(8,128)(2,1)}, bf16[144,2048]{1,0:T(8,128)(2,1)S(1)}, u32[]{:S(2)}, u32[]{:S(2)}) collective-permute-start(bf16[144,2048]{1,0:T(8,128)(2,1)} %get-tuple-element.48), channel_id=1, source_target_pairs={{0,24},{1,25},{2,26},{3,27},{4,28},{5,29},{6,30},{7,31},{8,0},{9,1... | collective-permute-start | bytes 1769480 | tf_op jit(solution)/shard_map/ppermute | solution.py:469
  59.1 54.4 %collective-permute-start.10 = (bf16[144,2048]{1,0:T(8,128)(2,1)}, bf16[144,2048]{1,0:T(8,128)(2,1)S(1)}, u32[]{:S(2)}, u32[]{:S(2)}) collective-permute-start(bf16[144,2048]{1,0:T(8,128)(2,1)} %get-tuple-element.49), channel_id=1, source_target_pairs={{0,16},{1,17},{2,18},{3,19},{4,20},{5,21},{6,22},{7,23},{8,24},{9,... | collective-permute-start | bytes 1769480 | tf_op jit(solution)/shard_map/ppermute | solution.py:469
  60.2 53.3 %collective-permute-start.11 = (bf16[144,2048]{1,0:T(8,128)(2,1)}, bf16[144,2048]{1,0:T(8,128)(2,1)S(1)}, u32[]{:S(2)}, u32[]{:S(2)}) collective-permute-start(bf16[144,2048]{1,0:T(8,128)(2,1)} %get-tuple-element.50), channel_id=1, source_target_pairs={{0,9},{1,8},{2,11},{3,10},{4,13},{5,12},{6,15},{7,14},{8,17},{9,16... | collective-permute-start | bytes 1769480 | tf_op jit(solution)/shard_map/ppermute | solution.py:469
  62.1 51.4 %collective-permute-start.12 = (bf16[144,2048]{1,0:T(8,128)(2,1)}, bf16[144,2048]{1,0:T(8,128)(2,1)S(1)}, u32[]{:S(2)}, u32[]{:S(2)}) collective-permute-start(bf16[144,2048]{1,0:T(8,128)(2,1)} %get-tuple-element.51), channel_id=1, source_target_pairs={{0,25},{1,24},{2,27},{3,26},{4,29},{5,28},{6,31},{7,30},{8,1},{9,0... | collective-permute-start | bytes 1769480 | tf_op jit(solution)/shard_map/ppermute | solution.py:469
  72.4 41.1 %collective-permute-start.13 = (bf16[144,2048]{1,0:T(8,128)(2,1)}, bf16[144,2048]{1,0:T(8,128)(2,1)S(1)}, u32[]{:S(2)}, u32[]{:S(2)}) collective-permute-start(bf16[144,2048]{1,0:T(8,128)(2,1)} %get-tuple-element.52), channel_id=1, source_target_pairs={{0,17},{1,16},{2,19},{3,18},{4,21},{5,20},{6,23},{7,22},{8,25},{9,... | collective-permute-start | bytes 1769480 | tf_op jit(solution)/shard_map/ppermute | solution.py:469
  86.7 26.9 %collective-permute-start.14 = (bf16[144,2048]{1,0:T(8,128)(2,1)}, bf16[144,2048]{1,0:T(8,128)(2,1)}, u32[]{:S(2)}, u32[]{:S(2)}) collective-permute-start(bf16[144,2048]{1,0:T(8,128)(2,1)} %get-tuple-element.53), channel_id=1, source_target_pairs={{0,1},{1,0},{2,3},{3,2},{4,5},{5,4},{6,7},{7,6},{8,9},{9,8},{10,11... | collective-permute-start | bytes 1769480 | tf_op jit(solution)/shard_map/ppermute | solution.py:469
  105.3 8.2 %copy-start.1 = (bf16[1,384,2048]{2,1,0:T(8,128)(2,1)S(1)}, bf16[1,384,2048]{2,1,0:T(8,128)(2,1)}, u32[]{:S(2)}) copy-start(bf16[1,384,2048]{2,1,0:T(8,128)(2,1)} %param.13) | copy-start | bytes 4718596
  105.3 8.2 %copy-start.2 = (bf16[144,2048]{1,0:T(8,128)(2,1)S(1)}, bf16[144,2048]{1,0:T(8,128)(2,1)}, u32[]{:S(2)}) copy-start(bf16[144,2048]{1,0:T(8,128)(2,1)} %get-tuple-element.46.refs_2_) | copy-start | bytes 1769476
  130.7 62.4 %copy-start = (s32[128,8]{0,1:T(8,128)S(1)}, s32[128,8]{0,1:T(8,128)}, u32[]{:S(2)}) copy-start(s32[128,8]{0,1:T(8,128)} %param.10) | copy-start | bytes 12292
Sparse Core Ops, SparseCore 0:
  130.9 61.3 reduce-scatter.1

commit v7 on v6

--- a/solution.py
+++ b/solution.py
@@ -116,19 +116,22 @@
     sources = refs[:pieces]
     count = 8 if scaled else 1
     outs = refs[pieces : pieces + count]
-    data_ref, s_ref, out_ref, scale_ref, in_sems, out_sems = refs[pieces + count :]
+    data_ref, extra_ref, s_ref, out_ref, scale_ref, in_sems, out_sems = refs[pieces + count :]
     experts, rows, width = out_ref.shape
     toks = sources[0].shape[0]
 
     loads = []
     for k, (src, line, above) in enumerate(zip(sources, (0, 1, 2, 2, 3), (0, 0, 0, toks // 2, 0))):
         row = pl.multiple_of(starts_ref[line] + above, 16)
-        loads.append(pltpu.make_async_copy(src, data_ref.at[pl.ds(row, src.shape[0]), :], in_sems.at[k]))
-        loads[-1].start()
-    for load in loads:
+        some = pl.ds(row, src.shape[0])
+        loads.append(pltpu.make_async_copy(src.at[:, width:], extra_ref.at[some, :], in_sems.at[k]))
+        loads.append(pltpu.make_async_copy(src.at[:, :width], data_ref.at[some, :], in_sems.at[pieces + k]))
+    for load in loads[0::2] + loads[1::2]:
+        load.start()
+    for load in loads[0::2]:
         load.wait()
 
-    extra = data_ref[:, width:]
+    extra = extra_ref[...]
     wanted = wanted_ref[...]
     lane = iota(wanted.shape, 1)
 
@@ -150,6 +153,8 @@
             total = jnp.sum(chosen * weight[:, None, :], axis=2, keepdims=True)
             scale_ref[h] = jnp.broadcast_to(total, (experts, pair, 128)).reshape(experts * pair, 128)
 
+    for load in loads[1::2]:
+        load.wait()
     stores = []
     parts = 4
     columns = width // parts
@@ -180,11 +185,12 @@
         in_specs=[VMEM, pl.BlockSpec(memory_space=pltpu.SMEM)] + [HBM] * len(lines),
         out_specs=(HBM,) * len(shapes),
         scratch_shapes=[
-            pltpu.VMEM((all_toks, width + 128), BF),
+            pltpu.VMEM((all_toks, width), BF),
+            pltpu.VMEM((all_toks, 128), BF),
             pltpu.VMEM((2, experts * rows // 2, all_toks // 2), BF),
             pltpu.VMEM((experts, rows, width), BF),
             pltpu.VMEM((2, experts * rows // 2, 128), F32),
-            pltpu.SemaphoreType.DMA((len(lines),)),
+            pltpu.SemaphoreType.DMA((2 * len(lines),)),
             pltpu.SemaphoreType.DMA((4 * len(shapes),)),
         ],
         compiler_params=pltpu.CompilerParams(vmem_limit_bytes=32 * MIB),
@@ -201,8 +207,8 @@
 
 def forward_kernel(*refs):
     blocks, wg_hbm, wu_hbm = refs[:3]
-    cs_ref, at_ref, wcat_ref = refs[3:6]
-    x_ref, act_ref, turn_ref, sems = refs[6:]
+    cs_ref, at_ref, wcat_ref, x_ref = refs[3:7]
+    act_ref, turn_ref, sems = refs[7:]
     rows = blocks.shape[1]
     hidden = wg_hbm.shape[1]
     loads = [
@@ -245,11 +251,11 @@
             jax.ShapeDtypeStruct((rows, 2 * hidden), F32),
             jax.ShapeDtypeStruct((hidden, rows), BF),
             jax.ShapeDtypeStruct((width, 2 * hidden), BF),
+            jax.ShapeDtypeStruct((rows, width), BF),
         ),
         in_specs=[HBM] * 3,
-        out_specs=(VMEM,) * 3,
+        out_specs=(VMEM,) * 4,
         scratch_shapes=[
-            pltpu.VMEM((rows, width), BF),
             pltpu.VMEM((rows, hidden), F32),
             pltpu.VMEM((rows, hidden), F32),
             pltpu.SemaphoreType.DMA((10,)),
@@ -263,10 +269,10 @@
 
 
 def middle_kernel(*refs):
-    to_ref, at_row_ref, gs, xs = refs[0], refs[1], refs[2:10], refs[10]
+    to_ref, at_row_ref, gs, x_ref = refs[0], refs[1], refs[2:10], refs[10]
     wd_ref, wcat_ref, cs_ref, at_ref = refs[11:15]
     packed_hbm, pair_hbm = refs[15:17]
-    (g_ref, x_ref, raw_ref, turn_ref, d_ref, dt_ref, dm_ref, dr_ref, packed_ref,
+    (g_ref, raw_ref, turn_ref, d_ref, dt_ref, dm_ref, dr_ref, packed_ref,
      pair_ref, sems, out_sems) = refs[17:]
     rows = gs[0].shape[0]
     copies = packed_ref.shape[0]
@@ -281,7 +287,6 @@
 
     order = sorted(range(8), key=lambda k: SPREAD[k])
     g_in = [load(gs[k], g_ref.at[pl.ds(pl.multiple_of(at_row_ref[k], 16), rows), :], k) for k in order]
-    x_in = [load(xs.at[k], x_ref.at[k * rows : (k + 1) * rows, :], 8 + k) for k in range(8)]
 
     parts = 2
     most = 8 // parts * rows
@@ -298,29 +303,33 @@
         d_act = turn_ref[some, :]
         grad = jnp.concatenate([d_act, d_act], axis=1) * cs_ref[some, :]
         d_ref[some, :] = grad
-    dt_ref[...] = d_ref[...].astype(BF).T
     dr_ref[...] = jnp.zeros_like(dr_ref)
     for b in range(n):
         dm_ref[b * MAIN : (b + 1) * MAIN, :] = d_ref[b * per_block : b * per_block + MAIN, :].astype(BF)
         dr_ref[b * 2 * REM : b * 2 * REM + REM, :] = d_ref[b * per_block + MAIN : (b + 1) * per_block, :]
 
-    for copy in x_in:
-        copy.wait()
     tile = 256
     per = 2 * half // copies
     slab = hidden // copies
     base = both * per // 128
-    for j in range(2 * half // tile):
-        cols = slice(j * tile, (j + 1) * tile)
-        into = dot(dt_ref[...], x_ref[:, cols]).astype(BF)
-        down = dot(at_ref[...], g_ref[:, cols]).astype(BF)
+    tiles = 2 * half // tile
+    turns = 8 * rows // 128
+    for j in range(max(tiles, turns)):
+        if j < turns:
+            some = slice(j * 128, (j + 1) * 128)
+            dt_ref[:, some] = d_ref[some, :].astype(BF).T
+        if j < tiles:
+            down = dot(at_ref[...], g_ref[:, j * tile : (j + 1) * tile]).astype(BF)
+            for q in range(tile // 128):
+                at = j * tile // 128 + q
+                part = down[:, q * 128 : (q + 1) * 128].reshape(copies, slab, 128)
+                packed_ref[:, base + at * slab : base + (at + 1) * slab, :] = part
+    for j in range(tiles):
+        into = dot(dt_ref[...], x_ref[:, j * tile : (j + 1) * tile]).astype(BF)
         for q in range(tile // 128):
             at = j * tile // 128 + q
             owner, piece = at * 128 // per, at % (per // 128)
-            part = into[:, q * 128 : (q + 1) * 128]
-            packed_ref[owner, piece * both : (piece + 1) * both, :] = part
-            part = down[:, q * 128 : (q + 1) * 128].reshape(copies, slab, 128)
-            packed_ref[:, base + at * slab : base + (at + 1) * slab, :] = part
+            packed_ref[owner, piece * both : (piece + 1) * both, :] = into[:, q * 128 : (q + 1) * 128]
     packed_out = pltpu.make_async_copy(packed_ref, packed_hbm, out_sems.at[n])
     packed_out.start()
 
@@ -358,10 +367,9 @@
     return pl.pallas_call(
         middle_kernel,
         out_shape=(pltpu.HBM((copies, length, 128), BF), pltpu.HBM((n, PACK, half), BF)),
-        in_specs=[smem] * 2 + [pl.BlockSpec(memory_space=pl.ANY)] * 9 + [VMEM] * 4,
+        in_specs=[smem] * 2 + [pl.BlockSpec(memory_space=pl.ANY)] * 8 + [VMEM] * 5,
         out_specs=(HBM,) * 2,
         scratch_shapes=[
-            pltpu.VMEM((rows, width), BF),
             pltpu.VMEM((rows, width), BF),
             pltpu.VMEM((rows, hidden), F32),
             pltpu.VMEM((rows, hidden), F32),
@@ -371,10 +379,10 @@
             pltpu.VMEM((n * 2 * REM, both), F32),
             pltpu.VMEM((copies, length, 128), BF),
             pltpu.VMEM((n, PACK, half), BF),
-            pltpu.SemaphoreType.DMA((16,)),
+            pltpu.SemaphoreType.DMA((8,)),
             pltpu.SemaphoreType.DMA((n + 1,)),
         ],
-        compiler_params=pltpu.CompilerParams(vmem_limit_bytes=40 * MIB),
+        compiler_params=pltpu.CompilerParams(vmem_limit_bytes=36 * MIB),
         cost_estimate=pl.CostEstimate(flops=2 * rows * width * 6 * hidden, bytes_accessed=28 * MIB, transcendentals=0),
         name="middle",
     )(to, at_row, *gs, xs, wd, wcat, cs, act)
@@ -392,23 +400,7 @@
         down_ref[:, q * 128 : (q + 1) * 128] = in_ref[base + q * slab : base + (q + 1) * slab, :]
 
 
-def unpack(summed, per, hidden, width, slab):
-    vmem = pl.BlockSpec(memory_space=pltpu.VMEM)
-    return pl.pallas_call(
-        unpack_kernel,
-        out_shape=(
-            jax.ShapeDtypeStruct((per, hidden), BF),
-            jax.ShapeDtypeStruct((per, hidden), BF),
-            jax.ShapeDtypeStruct((slab, width), BF),
-        ),
-        in_specs=[vmem],
-        out_specs=(vmem, vmem, vmem),
-        cost_estimate=pl.CostEstimate(flops=0, bytes_accessed=2 * MIB, transcendentals=0),
-        name="unpack",
-    )(summed)
-
-
-def combine_kernel(ids_ref, ret_ref, out_ref, main_ref, rest_ref):
+def combine_kernel(ids_ref, ret_ref, sum_ref, out_ref, gate_ref, up_ref, down_ref, main_ref, rest_ref):
     experts, _, cols = ret_ref.shape
     toks = out_ref.shape[0]
     half = out_ref.shape[1] // 2
@@ -423,6 +415,10 @@
         rest_ref[0] = jnp.where(left, rest, 0.0).T.astype(BF)
         rest_ref[1] = jnp.where(left, 0.0, rest).T.astype(BF)
 
+    @pl.when(c == 1)
+    def _():
+        unpack_kernel(sum_ref, gate_ref, up_ref, down_ref)
+
     tail = ret_ref[:, 2 * MAIN : PACK, :].reshape(experts * 2 * REM, cols)
     for side in range(2):
         body = ret_ref[:, side * MAIN : (side + 1) * MAIN, :].reshape(experts * MAIN, cols)
@@ -430,20 +426,22 @@
         out_ref[:, pl.ds(pl.multiple_of(side * half + c * cols, 128), cols)] = total.astype(BF)
 
 
-def combine(ids, ret):
+def combine(ids, ret, summed, per, hidden, slab):
     experts, _, half = ret.shape
     toks = ids.shape[1]
     steps = 4
     cols = half // steps
+    shapes = ((toks, 2 * half), (per, hidden), (per, hidden), (slab, 2 * half))
     return pl.pallas_call(
         combine_kernel,
-        out_shape=jax.ShapeDtypeStruct((toks, 2 * half), BF),
+        out_shape=tuple(jax.ShapeDtypeStruct(shape, BF) for shape in shapes),
         grid=(steps,),
         in_specs=[
             pl.BlockSpec(ids.shape, lambda c: (0, 0)),
             pl.BlockSpec((experts, PACK, cols), lambda c: (0, 0, c)),
+            pl.BlockSpec(summed.shape, lambda c: (0, 0)),
         ],
-        out_specs=pl.BlockSpec((toks, 2 * half), lambda c: (0, 0)),
+        out_specs=tuple(pl.BlockSpec(shape, lambda c: (0, 0)) for shape in shapes),
         scratch_shapes=[
             pltpu.VMEM((toks, experts * MAIN), BF),
             pltpu.VMEM((2, toks, experts * 2 * REM), BF),
@@ -451,7 +449,7 @@
         compiler_params=pltpu.CompilerParams(vmem_limit_bytes=24 * MIB),
         cost_estimate=pl.CostEstimate(flops=2 * 1280 * toks * 2 * half, bytes_accessed=6 * MIB, transcendentals=0),
         name="combine",
-    )(ids, ret)
+    )(ids, ret, summed)
 
 
 def place(x, y, core):
@@ -501,12 +499,11 @@
     along_x, _ = lax.optimization_barrier((along_x, out_x))
     out_g = dispatch(along_x, starts_g, lines_g, True)
     gs = [moved(v, d, 0, f) for v, (d, f) in zip(out_g, SPREAD)]
-    cs, act, wcat = forward(xs, wg, wu)
-    packed, outgoing = middle(origin, at_row, gs, xs, wd, wcat, cs, act, copies)
+    cs, act, wcat, rows_x = forward(xs, wg, wu)
+    packed, outgoing = middle(origin, at_row, gs, rows_x, wd, wcat, cs, act, copies)
     summed = lax.psum_scatter(packed, "dp", scatter_dimension=0, tiled=True)[0]
     ret = lax.all_to_all(outgoing, "expert", split_axis=0, concat_axis=0, tiled=True)
-    grad_tokens = combine(ids_t, ret)
-    grad_g, grad_u, grad_d = unpack(summed, width // copies, hidden, width, hidden // copies)
+    grad_tokens, grad_g, grad_u, grad_d = combine(ids_t, ret, summed, width // copies, hidden, hidden // copies)
     return (grad_tokens, grad_g[None], grad_u[None], grad_d[None])
 
 

time: 206 us -> 207 us (level)
  local copies, waits for them, and re-layouts: 0.62 us -> 4.02 us
  Pallas kernels: 43 us -> 40.3 us
    unnamed x14 -> x18, local copies, waits for them, and re-layouts: 0.03 us -> 3.43 us
    pallas_call x2 -> x1, Pallas kernels: 5.22 us -> 3.39 us  [combine(): pl.pallas_call(combine_kernel, out_shape=tuple((jax.ShapeDtypeStruct(shap...]
  transfers between devices with their start and end apart: 17 -> 17, of which waited for: 6 -> 6; matrix products, arithmetic and copies ran while one was open for 0% -> 0% of each run, Pallas kernels for 8% -> 6%
where the time goes in v7:
time: 207 us; the launch traced here: 206 us
  blocking collectives  62.5 us (30%)
  waiting for transfers between devices  44 us (21%)
  starting transfers between devices  41.1 us (20%)
  Pallas kernels  40.3 us (19%)
  between operations  14.3 us (7%)
  local copies, waits for them, and re-layouts  4.02 us (2%)
    all_to_all x1, blocking collectives, shards(): lax.all_to_all(outgoing, 'expert', split_axis=0, concat_axis=0, tiled=True)  62.5 us
    ppermute x15, starting transfers between devices, moved(): return lax.ppermute(value, 'expert', pairs)  33.6 us
    ppermute x15, waiting for transfers between devices, moved(): return lax.ppermute(value, 'expert', pairs)  25.4 us
    all_to_all x1, waiting for transfers between devices, shards(): lax.all_to_all(out_x, 'expert', split_axis=0, concat_axis=0, axis_index_g...  18.6 us
    pallas_call x1, Pallas kernels, middle(): pl.pallas_call(middle_kernel, out_shape=(pltpu.HBM((copies, length, 128),...  16.5 us
    pallas_call x2, Pallas kernels, dispatch(): pl.pallas_call(functools.partial(dispatch_kernel, scaled, per), out_shape...  10.1 us
    pallas_call x1, Pallas kernels, forward(): pl.pallas_call(forward_kernel, out_shape=(jax.ShapeDtypeStruct((rows, 2 *...  8.17 us
    all_to_all x1, starting transfers between devices, shards(): lax.all_to_all(out_x, 'expert', split_axis=0, concat_axis=0, axis_index_g...  7.54 us
  transfers between devices with their start and end apart: 17, of which 6 were waited for; matrix products, arithmetic and copies ran while one was open for 0% of the time, Pallas kernels for 6%

profile of v7, /device:TPU:1, one launch (start us, length us, event | category | flops | bytes accessed | tf_op | source)
XLA Modules:
  0.0 206.2 jit_solution(13883489913845004204)
XLA Ops:
  7.2 2.1 %prepare.1 = (bf16[128,2176]{1,0:T(8,128)(2,1)}, bf16[128,2176]{1,0:T(8,128)(2,1)}) custom-call(s32[8,128]{1,0:T(8,128)} %bitcast.66, f32[8,128]{1,0:T(8,128)} %bitcast.69, bf16[128,2048]{1,0:T(8,128)(2,1)} %tokens_hbm.1, bf16[128,2048]{1,0:T(8,128)(2,1)} %grads_hbm.1), custom_call_target="tpu_custom_call" | custom-call | flops 1048576 | bytes 2097152 | tf_op jit(solution)/shard_map/prepare/pallas_call | solution.py:97
  9.3 3.4 %collective-permute-start.2 = (bf16[128,2176]{1,0:T(8,128)(2,1)}, bf16[128,2176]{1,0:T(8,128)(2,1)S(1)}, u32[]{:S(2)}, u32[]{:S(2)}) collective-permute-start(bf16[128,2176]{1,0:T(8,128)(2,1)} %get-tuple-element.37.refs_0_), channel_id=1, source_target_pairs={{0,24},{1,25},{2,26},{3,27},{4,28},{5,29},{6,30},{7,31},{8,0},{9,1... | collective-permute-start | bytes 1671176 | tf_op jit(solution)/shard_map/ppermute | solution.py:467
  12.7 0.0 collective-permute-start
  12.7 2.7 %collective-permute-start.6 = (bf16[128,2176]{1,0:T(8,128)(2,1)}, bf16[128,2176]{1,0:T(8,128)(2,1)S(1)}, u32[]{:S(2)}, u32[]{:S(2)}) collective-permute-start(bf16[128,2176]{1,0:T(8,128)(2,1)} %get-tuple-element.43.refs_0_), channel_id=1, source_target_pairs={{0,6},{1,7},{2,0},{3,1},{4,2},{5,3},{6,4},{7,5},{8,14},{9,15},{10,... | collective-permute-start | bytes 1671176 | tf_op jit(solution)/shard_map/ppermute | solution.py:467
  15.4 0.0 collective-permute-start.4
  15.4 8.9 %collective-permute-done.2.refs_4_ = bf16[128,2176]{1,0:T(8,128)(2,1)S(1)} collective-permute-done((bf16[128,2176]{1,0:T(8,128)(2,1)}, bf16[128,2176]{1,0:T(8,128)(2,1)S(1)}, u32[]{:S(2)}, u32[]{:S(2)}) %collective-permute-start.2) | collective-permute-done | bytes 557088 | tf_op jit(solution)/shard_map/ppermute | solution.py:467
  24.3 3.4 %collective-permute-start.3 = (bf16[64,2176]{1,0:T(8,128)(2,1)S(1)}, bf16[64,2176]{1,0:T(8,128)(2,1)}, u32[]{:S(2)}, u32[]{:S(2)}) collective-permute-start(bf16[64,2176]{1,0:T(8,128)(2,1)S(1)} %slice.17), channel_id=1, source_target_pairs={{0,24},{1,25},{2,26},{3,27},{4,28},{5,29},{6,30},{7,31},{8,0},{9,1... | collective-permute-start | bytes 835592 | tf_op jit(solution)/shard_map/ppermute | solution.py:467
  27.7 0.0 collective-permute-done.refs_1_
  27.8 0.1 collective-permute-start.1
  27.8 0.0 collective-permute-done.6.refs_4_
  27.9 2.8 %collective-permute-start.7 = (bf16[64,2176]{1,0:T(8,128)(2,1)S(1)}, bf16[64,2176]{1,0:T(8,128)(2,1)}, u32[]{:S(2)}, u32[]{:S(2)}) collective-permute-start(bf16[64,2176]{1,0:T(8,128)(2,1)S(1)} %slice.19), channel_id=1, source_target_pairs={{0,6},{1,7},{2,0},{3,1},{4,2},{5,3},{6,4},{7,5},{8,14},{9,15},{10,... | collective-permute-start | bytes 835592 | tf_op jit(solution)/shard_map/ppermute | solution.py:467
  30.7 0.0 collective-permute-done.4.refs_1_
  30.7 0.1 collective-permute-start.5
  30.9 0.1 stack.239
  31.0 1.2 collective-permute-done.3.refs_3_
  32.1 3.3 %collective-permute-done.1.refs_2_ = bf16[64,2176]{1,0:T(8,128)(2,1)} collective-permute-done((bf16[64,2176]{1,0:T(8,128)(2,1)S(1)}, bf16[64,2176]{1,0:T(8,128)(2,1)}, u32[]{:S(2)}, u32[]{:S(2)}) %collective-permute-start.1) | collective-permute-done | bytes 278560 | tf_op jit(solution)/shard_map/ppermute | solution.py:467
  35.5 0.0 collective-permute-done.7.refs_3_
  35.5 2.7 %collective-permute-done.5.refs_2_ = bf16[64,2176]{1,0:T(8,128)(2,1)} collective-permute-done((bf16[64,2176]{1,0:T(8,128)(2,1)S(1)}, bf16[64,2176]{1,0:T(8,128)(2,1)}, u32[]{:S(2)}, u32[]{:S(2)}) %collective-permute-start.5) | collective-permute-done | bytes 278560 | tf_op jit(solution)/shard_map/ppermute | solution.py:467
  38.2 0.1 broadcast_in_dim.22.wanted_ref
  38.2 5.0 %dispatch.2 = bf16[8,144,2048]{2,1,0:T(8,128)(2,1)} custom-call(s32[8,128]{1,0:T(8,128)S(1)} %broadcast_in_dim.22.wanted_ref, s32[4]{0:T(128)S(1)} %iota_multiply_fusion.starts_ref, bf16[128,2176]{1,0:T(8,128)(2,1)} %get-tuple-element.37.refs_0_, bf16[128,2176]{1,0:T(8,128)(2,1)} %copy-done.8, bf16[64,2176]{1,0:T(8,128)(2,1)} %collective-permute-done.1.refs_2_, ...), custom_call_target="tpu_custom_call" | custom-call | flops 2415919104 | bytes 7340032 | tf_op jit(solution)/shard_map/dispatch/pallas_call | solution.py:182
  43.2 7.5 %all-to-all-start = ((bf16[8,144,2048]{2,1,0:T(8,128)(2,1)}), bf16[8,144,2048]{2,1,0:T(8,128)(2,1)}, u32[]{:S(2)}, u32[]{:S(2)}) async-start(bf16[8,144,2048]{2,1,0:T(8,128)(2,1)} %dispatch.2), calls=%async_computation | async-start | bytes 9437184 | tf_op jit(solution)/shard_map/all_to_all | solution.py:498
  50.8 0.1 stack.230
  50.9 0.1 broadcast_in_dim.10.wanted_ref
  50.9 5.2 %dispatch.3 = (bf16[144,2048]{1,0:T(8,128)(2,1)}, bf16[144,2048]{1,0:T(8,128)(2,1)}, bf16[144,2048]{1,0:T(8,128)(2,1)}, bf16[144,2048]{1,0:T(8,128)(2,1)}, bf16[...) custom-call(s32[8,128]{1,0:T(8,128)S(1)} %broadcast_in_dim.10.wanted_re, ...), custom_call_target="tpu_custom_call" | custom-call | flops 2415919104 | bytes 7340032 | tf_op jit(solution)/shard_map/dispatch/pallas_call | solution.py:182
  56.1 0.1 collective-permute-start.8
  56.2 2.7 %collective-permute-start.9 = (bf16[144,2048]{1,0:T(8,128)(2,1)}, bf16[144,2048]{1,0:T(8,128)(2,1)S(1)}, u32[]{:S(2)}, u32[]{:S(2)}) collective-permute-start(bf16[144,2048]{1,0:T(8,128)(2,1)} %get-tuple-element.50), channel_id=1, source_target_pairs={{0,24},{1,25},{2,26},{3,27},{4,28},{5,29},{6,30},{7,31},{8,0},{9,1... | collective-permute-start | bytes 1769480 | tf_op jit(solution)/shard_map/ppermute | solution.py:467
  59.0 1.1 collective-permute-start.10
  60.0 1.9 collective-permute-start.11
  61.9 1.1 collective-permute-start.12
  63.0 9.3 %collective-permute-done.8.refs_3_ = bf16[144,2048]{1,0:T(8,128)(2,1)S(1)} collective-permute-done((bf16[144,2048]{1,0:T(8,128)(2,1)}, bf16[144,2048]{1,0:T(8,128)(2,1)S(1)}, u32[]{:S(2)}, u32[]{:S(2)}) %collective-permute-start.8) | collective-permute-done | bytes 589856 | tf_op jit(solution)/shard_map/ppermute | solution.py:467
  72.3 14.3 %collective-permute-start.13 = (bf16[144,2048]{1,0:T(8,128)(2,1)}, bf16[144,2048]{1,0:T(8,128)(2,1)S(1)}, u32[]{:S(2)}, u32[]{:S(2)}) collective-permute-start(bf16[144,2048]{1,0:T(8,128)(2,1)} %get-tuple-element.54), channel_id=1, source_target_pairs={{0,17},{1,16},{2,19},{3,18},{4,21},{5,20},{6,23},{7,22},{8,25},{9,... | collective-permute-start | bytes 1769480 | tf_op jit(solution)/shard_map/ppermute | solution.py:467
  86.5 0.0 collective-permute-done.9.refs_4_
  86.5 0.0 collective-permute-start.14
  86.5 0.1 stack.221.refs_1_
  86.6 0.1 stack.212.refs_0_
  86.7 18.6 %all-to-all-done.refs_0_ = bf16[8,144,2048]{2,1,0:T(8,128)(2,1)} async-done(((bf16[8,144,2048]{2,1,0:T(8,128)(2,1)}), bf16[8,144,2048]{2,1,0:T(8,128)(2,1)}, u32[]{:S(2)}, u32[]{:S(2)}) %all-to-all-start) | async-done | bytes 4718624 | tf_op jit(solution)/shard_map/all_to_all | solution.py:498
  105.3 8.2 %forward.1 = (f32[1152,768]{1,0:T(8,128)S(1)}, bf16[384,1152]{1,0:T(8,128)(2,1)S(1)}, bf16[2048,768]{1,0:T(8,128)(2,1)S(1)}, bf16[1152,2048]{1,0:T(8,128)(2,1)S(1)}) custom-call(bf16[8,144,2048]{2,1,0:T(8,128)(2,1)} %all-to-all-done.refs_0_, bf16[2048,384]{1,0:T(8,128)(2,1)} %bitcast.70, bf16[2048,384]{1,0:T(8,128)(2,1)} %bitcast.71), custom_call_target="tpu_custom_call" | custom-call | flops 3623878656 | bytes 16777216 | tf_op jit(solution)/shard_map/forward/pallas_call | solution.py:248
  113.5 0.0 collective-permute-done.10.refs_5_
  113.5 0.0 collective-permute-done.11.refs_6_
  113.5 0.0 collective-permute-done.13.refs_8_
  113.5 0.0 collective-permute-done.14.refs_9_
  113.6 16.5 %middle.1 = (bf16[8,2304,128]{2,1,0:T(8,128)(2,1)}, bf16[32,72,1024]{2,1,0:T(8,128)(2,1)}) custom-call(s32[32]{0:T(128)S(1)} %stack.212.refs_0_, s32[8]{0:T(128)S(1)} %stack.221.refs_1_, bf16[144,2048]{1,0:T(8,128)(2,1)S(1)} %copy-done.4, bf16[144,2048]{1,0:T(8,128)(2,1)S(1)} %collective-permute-done.8.refs_3_, ...), custom_call_target="tpu_custom_call" | custom-call | flops 10871635968 | bytes 29360128 | tf_op jit(solution)/shard_map/middle/pallas_call | solution.py:367
  130.1 0.0 reduce-scatter.2.cloned.1.call-update
  130.1 0.0 copy-start.2
  130.1 62.5 %all_to_all.10.ret_ref = bf16[32,72,1024]{2,1,0:T(8,128)(2,1)} all-to-all(bf16[32,72,1024]{2,1,0:T(8,128)(2,1)} %get-tuple-element.60), channel_id=1, replica_groups=mesh['dp'=8,'expert'=32] {'expert'}, dimensions={0} | all-to-all | bytes 9437184 | tf_op jit(solution)/shard_map/all_to_all | solution.py:505
  192.6 2.3 %copy-done = bf16[32,72,1024]{2,1,0:T(8,128)(2,1)S(1)} copy-done((bf16[32,72,1024]{2,1,0:T(8,128)(2,1)S(1)}, bf16[32,72,1024]{2,1,0:T(8,128)(2,1)}, u32[]{:S(2)}) %copy-start) | copy-done | bytes 4718616
  194.9 1.1 copy-done.1
  196.0 3.4 %combine.1 = (bf16[128,2048]{1,0:T(8,128)(2,1)}, bf16[256,384]{1,0:T(8,128)(2,1)}, bf16[256,384]{1,0:T(8,128)(2,1)}, bf16[48,2048]{1,0:T(8,128)(2,1)}) custom-call(s32[8,128]{1,0:T(8,128)S(1)} %bitcast.67, bf16[32,72,1024]{2,1,0:T(8,128)(2,1)S(1)} %copy-done, bf16[2304,128]{1,0:T(8,128)(2,1)S(1)} %bitcast.65), custom_call_target="tpu_custom_call" | custom-call | flops 671088640 | bytes 6291456 | tf_op jit(solution)/shard_map/combine/pallas_call | solution.py:435
  (24 shorter events, 0.1 us)
Async XLA Ops:
  9.3 15.0 %collective-permute-start.2 = (bf16[128,2176]{1,0:T(8,128)(2,1)}, bf16[128,2176]{1,0:T(8,128)(2,1)S(1)}, u32[]{:S(2)}, u32[]{:S(2)}) collective-permute-start(bf16[128,2176]{1,0:T(8,128)(2,1)} %get-tuple-element.37.refs_0_), channel_id=1, source_target_pairs={{0,24},{1,25},{2,26},{3,27},{4,28},{5,29},{6,30},{7,31},{8,0},{9,1... | collective-permute-start | bytes 1671176 | tf_op jit(solution)/shard_map/ppermute | solution.py:467
  12.7 15.0 %collective-permute-start = (bf16[128,2176]{1,0:T(8,128)(2,1)}, bf16[128,2176]{1,0:T(8,128)(2,1)S(1)}, u32[]{:S(2)}, u32[]{:S(2)}) collective-permute-start(bf16[128,2176]{1,0:T(8,128)(2,1)} %get-tuple-element.37.refs_0_), channel_id=1, source_target_pairs={{0,8},{1,9},{2,10},{3,11},{4,12},{5,13},{6,14},{7,15},{8,16},{9,17... | collective-permute-start | bytes 1671176 | tf_op jit(solution)/shard_map/ppermute | solution.py:467
  12.7 15.1 %collective-permute-start.6 = (bf16[128,2176]{1,0:T(8,128)(2,1)}, bf16[128,2176]{1,0:T(8,128)(2,1)S(1)}, u32[]{:S(2)}, u32[]{:S(2)}) collective-permute-start(bf16[128,2176]{1,0:T(8,128)(2,1)} %get-tuple-element.43.refs_0_), channel_id=1, source_target_pairs={{0,6},{1,7},{2,0},{3,1},{4,2},{5,3},{6,4},{7,5},{8,14},{9,15},{10,... | collective-permute-start | bytes 1671176 | tf_op jit(solution)/shard_map/ppermute | solution.py:467
  15.4 15.3 %collective-permute-start.4 = (bf16[128,2176]{1,0:T(8,128)(2,1)}, bf16[128,2176]{1,0:T(8,128)(2,1)S(1)}, u32[]{:S(2)}, u32[]{:S(2)}) collective-permute-start(bf16[128,2176]{1,0:T(8,128)(2,1)} %get-tuple-element.43.refs_0_), channel_id=1, source_target_pairs={{0,2},{1,3},{2,4},{3,5},{4,6},{5,7},{6,0},{7,1},{8,10},{9,11},{10,... | collective-permute-start | bytes 1671176 | tf_op jit(solution)/shard_map/ppermute | solution.py:467
  24.3 13.9 %copy-start.7 = (bf16[128,2176]{1,0:T(8,128)(2,1)}, bf16[128,2176]{1,0:T(8,128)(2,1)S(1)}, u32[]{:S(2)}) copy-start(bf16[128,2176]{1,0:T(8,128)(2,1)S(1)} %collective-permute-done.2.refs_4_) | copy-start | bytes 1671172
  24.3 7.8 %collective-permute-start.3 = (bf16[64,2176]{1,0:T(8,128)(2,1)S(1)}, bf16[64,2176]{1,0:T(8,128)(2,1)}, u32[]{:S(2)}, u32[]{:S(2)}) collective-permute-start(bf16[64,2176]{1,0:T(8,128)(2,1)S(1)} %slice.17), channel_id=1, source_target_pairs={{0,24},{1,25},{2,26},{3,27},{4,28},{5,29},{6,30},{7,31},{8,0},{9,1... | collective-permute-start | bytes 835592 | tf_op jit(solution)/shard_map/ppermute | solution.py:467
  27.7 10.5 %copy-start.8 = (bf16[128,2176]{1,0:T(8,128)(2,1)}, bf16[128,2176]{1,0:T(8,128)(2,1)S(1)}, u32[]{:S(2)}) copy-start(bf16[128,2176]{1,0:T(8,128)(2,1)S(1)} %collective-permute-done.refs_1_) | copy-start | bytes 1671172
  27.8 7.7 %collective-permute-start.1 = (bf16[64,2176]{1,0:T(8,128)(2,1)S(1)}, bf16[64,2176]{1,0:T(8,128)(2,1)}, u32[]{:S(2)}, u32[]{:S(2)}) collective-permute-start(bf16[64,2176]{1,0:T(8,128)(2,1)S(1)} %slice.16), channel_id=1, source_target_pairs={{0,8},{1,9},{2,10},{3,11},{4,12},{5,13},{6,14},{7,15},{8,16},{9,17... | collective-permute-start | bytes 835592 | tf_op jit(solution)/shard_map/ppermute | solution.py:467
  27.9 15.4 %copy-start.5 = (bf16[128,2176]{1,0:T(8,128)(2,1)}, bf16[128,2176]{1,0:T(8,128)(2,1)S(1)}, u32[]{:S(2)}) copy-start(bf16[128,2176]{1,0:T(8,128)(2,1)S(1)} %collective-permute-done.6.refs_4_) | copy-start | bytes 1671172
  27.9 7.6 %collective-permute-start.7 = (bf16[64,2176]{1,0:T(8,128)(2,1)S(1)}, bf16[64,2176]{1,0:T(8,128)(2,1)}, u32[]{:S(2)}, u32[]{:S(2)}) collective-permute-start(bf16[64,2176]{1,0:T(8,128)(2,1)S(1)} %slice.19), channel_id=1, source_target_pairs={{0,6},{1,7},{2,0},{3,1},{4,2},{5,3},{6,4},{7,5},{8,14},{9,15},{10,... | collective-permute-start | bytes 835592 | tf_op jit(solution)/shard_map/ppermute | solution.py:467
  30.7 12.5 %copy-start.6 = (bf16[128,2176]{1,0:T(8,128)(2,1)}, bf16[128,2176]{1,0:T(8,128)(2,1)S(1)}, u32[]{:S(2)}) copy-start(bf16[128,2176]{1,0:T(8,128)(2,1)S(1)} %collective-permute-done.4.refs_1_) | copy-start | bytes 1671172
  30.7 7.4 %collective-permute-start.5 = (bf16[64,2176]{1,0:T(8,128)(2,1)S(1)}, bf16[64,2176]{1,0:T(8,128)(2,1)}, u32[]{:S(2)}, u32[]{:S(2)}) collective-permute-start(bf16[64,2176]{1,0:T(8,128)(2,1)S(1)} %slice.18), channel_id=1, source_target_pairs={{0,2},{1,3},{2,4},{3,5},{4,6},{5,7},{6,0},{7,1},{8,10},{9,11},{10,... | collective-permute-start | bytes 835592 | tf_op jit(solution)/shard_map/ppermute | solution.py:467
  43.2 62.1 %all-to-all-start = ((bf16[8,144,2048]{2,1,0:T(8,128)(2,1)}), bf16[8,144,2048]{2,1,0:T(8,128)(2,1)}, u32[]{:S(2)}, u32[]{:S(2)}) async-start(bf16[8,144,2048]{2,1,0:T(8,128)(2,1)} %dispatch.2), calls=%async_computation | async-start | bytes 9437184 | tf_op jit(solution)/shard_map/all_to_all | solution.py:498
  50.8 141.8 %reduce-scatter.2.cloned.1.call-start = ((), (), s32[]{:S(2)}) async-start(), calls=%async_computation.3 | async-start | bytes 5308416 | tf_op jit(solution)/shard_map/reduce_scatter | solution.py:504
  56.1 16.1 %collective-permute-start.8 = (bf16[144,2048]{1,0:T(8,128)(2,1)}, bf16[144,2048]{1,0:T(8,128)(2,1)S(1)}, u32[]{:S(2)}, u32[]{:S(2)}) collective-permute-start(bf16[144,2048]{1,0:T(8,128)(2,1)} %get-tuple-element.49), channel_id=1, source_target_pairs={{0,8},{1,9},{2,10},{3,11},{4,12},{5,13},{6,14},{7,15},{8,16},{9,17... | collective-permute-start | bytes 1769480 | tf_op jit(solution)/shard_map/ppermute | solution.py:467
  56.2 30.3 %collective-permute-start.9 = (bf16[144,2048]{1,0:T(8,128)(2,1)}, bf16[144,2048]{1,0:T(8,128)(2,1)S(1)}, u32[]{:S(2)}, u32[]{:S(2)}) collective-permute-start(bf16[144,2048]{1,0:T(8,128)(2,1)} %get-tuple-element.50), channel_id=1, source_target_pairs={{0,24},{1,25},{2,26},{3,27},{4,28},{5,29},{6,30},{7,31},{8,0},{9,1... | collective-permute-start | bytes 1769480 | tf_op jit(solution)/shard_map/ppermute | solution.py:467
  59.0 54.6 %collective-permute-start.10 = (bf16[144,2048]{1,0:T(8,128)(2,1)}, bf16[144,2048]{1,0:T(8,128)(2,1)S(1)}, u32[]{:S(2)}, u32[]{:S(2)}) collective-permute-start(bf16[144,2048]{1,0:T(8,128)(2,1)} %get-tuple-element.51), channel_id=1, source_target_pairs={{0,16},{1,17},{2,18},{3,19},{4,20},{5,21},{6,22},{7,23},{8,24},{9,... | collective-permute-start | bytes 1769480 | tf_op jit(solution)/shard_map/ppermute | solution.py:467
  60.0 53.5 %collective-permute-start.11 = (bf16[144,2048]{1,0:T(8,128)(2,1)}, bf16[144,2048]{1,0:T(8,128)(2,1)S(1)}, u32[]{:S(2)}, u32[]{:S(2)}) collective-permute-start(bf16[144,2048]{1,0:T(8,128)(2,1)} %get-tuple-element.52), channel_id=1, source_target_pairs={{0,9},{1,8},{2,11},{3,10},{4,13},{5,12},{6,15},{7,14},{8,17},{9,16... | collective-permute-start | bytes 1769480 | tf_op jit(solution)/shard_map/ppermute | solution.py:467
  61.9 51.6 %collective-permute-start.12 = (bf16[144,2048]{1,0:T(8,128)(2,1)}, bf16[144,2048]{1,0:T(8,128)(2,1)S(1)}, u32[]{:S(2)}, u32[]{:S(2)}) collective-permute-start(bf16[144,2048]{1,0:T(8,128)(2,1)} %get-tuple-element.53), channel_id=1, source_target_pairs={{0,25},{1,24},{2,27},{3,26},{4,29},{5,28},{6,31},{7,30},{8,1},{9,0... | collective-permute-start | bytes 1769480 | tf_op jit(solution)/shard_map/ppermute | solution.py:467
  72.3 41.3 %collective-permute-start.13 = (bf16[144,2048]{1,0:T(8,128)(2,1)}, bf16[144,2048]{1,0:T(8,128)(2,1)S(1)}, u32[]{:S(2)}, u32[]{:S(2)}) collective-permute-start(bf16[144,2048]{1,0:T(8,128)(2,1)} %get-tuple-element.54), channel_id=1, source_target_pairs={{0,17},{1,16},{2,19},{3,18},{4,21},{5,20},{6,23},{7,22},{8,25},{9,... | collective-permute-start | bytes 1769480 | tf_op jit(solution)/shard_map/ppermute | solution.py:467
  86.5 27.0 %collective-permute-start.14 = (bf16[144,2048]{1,0:T(8,128)(2,1)}, bf16[144,2048]{1,0:T(8,128)(2,1)}, u32[]{:S(2)}, u32[]{:S(2)}) collective-permute-start(bf16[144,2048]{1,0:T(8,128)(2,1)} %get-tuple-element.55), channel_id=1, source_target_pairs={{0,1},{1,0},{2,3},{3,2},{4,5},{5,4},{6,7},{7,6},{8,9},{9,8},{10,11... | collective-permute-start | bytes 1769480 | tf_op jit(solution)/shard_map/ppermute | solution.py:467
  105.3 8.2 %copy-start.3 = (bf16[1,384,2048]{2,1,0:T(8,128)(2,1)S(1)}, bf16[1,384,2048]{2,1,0:T(8,128)(2,1)}, u32[]{:S(2)}) copy-start(bf16[1,384,2048]{2,1,0:T(8,128)(2,1)} %param.13) | copy-start | bytes 4718596
  105.3 8.2 %copy-start.4 = (bf16[144,2048]{1,0:T(8,128)(2,1)S(1)}, bf16[144,2048]{1,0:T(8,128)(2,1)}, u32[]{:S(2)}) copy-start(bf16[144,2048]{1,0:T(8,128)(2,1)} %get-tuple-element.48.refs_2_) | copy-start | bytes 1769476
  130.1 62.5 %copy-start.2 = (s32[128,8]{0,1:T(8,128)S(1)}, s32[128,8]{0,1:T(8,128)}, u32[]{:S(2)}) copy-start(s32[128,8]{0,1:T(8,128)} %param.10) | copy-start | bytes 12292
  192.6 2.3 %copy-start = (bf16[32,72,1024]{2,1,0:T(8,128)(2,1)S(1)}, bf16[32,72,1024]{2,1,0:T(8,128)(2,1)}, u32[]{:S(2)}) copy-start(bf16[32,72,1024]{2,1,0:T(8,128)(2,1)} %all_to_all.10.ret_ref) | copy-start | bytes 14155780
  194.9 1.1 copy-start.1
Sparse Core Ops, SparseCore 0:
  130.2 61.2 reduce-scatter.1

commit v8 on v7

--- a/solution.py
+++ b/solution.py
@@ -400,7 +400,23 @@
         down_ref[:, q * 128 : (q + 1) * 128] = in_ref[base + q * slab : base + (q + 1) * slab, :]
 
 
-def combine_kernel(ids_ref, ret_ref, sum_ref, out_ref, gate_ref, up_ref, down_ref, main_ref, rest_ref):
+def unpack(summed, per, hidden, width, slab):
+    vmem = pl.BlockSpec(memory_space=pltpu.VMEM)
+    return pl.pallas_call(
+        unpack_kernel,
+        out_shape=(
+            jax.ShapeDtypeStruct((per, hidden), BF),
+            jax.ShapeDtypeStruct((per, hidden), BF),
+            jax.ShapeDtypeStruct((slab, width), BF),
+        ),
+        in_specs=[vmem],
+        out_specs=(vmem, vmem, vmem),
+        cost_estimate=pl.CostEstimate(flops=0, bytes_accessed=2 * MIB, transcendentals=0),
+        name="unpack",
+    )(summed)
+
+
+def combine_kernel(ids_ref, ret_ref, out_ref, main_ref, rest_ref):
     experts, _, cols = ret_ref.shape
     toks = out_ref.shape[0]
     half = out_ref.shape[1] // 2
@@ -415,10 +431,6 @@
         rest_ref[0] = jnp.where(left, rest, 0.0).T.astype(BF)
         rest_ref[1] = jnp.where(left, 0.0, rest).T.astype(BF)
 
-    @pl.when(c == 1)
-    def _():
-        unpack_kernel(sum_ref, gate_ref, up_ref, down_ref)
-
     tail = ret_ref[:, 2 * MAIN : PACK, :].reshape(experts * 2 * REM, cols)
     for side in range(2):
         body = ret_ref[:, side * MAIN : (side + 1) * MAIN, :].reshape(experts * MAIN, cols)
@@ -426,30 +438,28 @@
         out_ref[:, pl.ds(pl.multiple_of(side * half + c * cols, 128), cols)] = total.astype(BF)
 
 
-def combine(ids, ret, summed, per, hidden, slab):
+def combine(ids, ret):
     experts, _, half = ret.shape
     toks = ids.shape[1]
-    steps = 4
+    steps = 1
     cols = half // steps
-    shapes = ((toks, 2 * half), (per, hidden), (per, hidden), (slab, 2 * half))
     return pl.pallas_call(
         combine_kernel,
-        out_shape=tuple(jax.ShapeDtypeStruct(shape, BF) for shape in shapes),
+        out_shape=jax.ShapeDtypeStruct((toks, 2 * half), BF),
         grid=(steps,),
         in_specs=[
             pl.BlockSpec(ids.shape, lambda c: (0, 0)),
             pl.BlockSpec((experts, PACK, cols), lambda c: (0, 0, c)),
-            pl.BlockSpec(summed.shape, lambda c: (0, 0)),
         ],
-        out_specs=tuple(pl.BlockSpec(shape, lambda c: (0, 0)) for shape in shapes),
+        out_specs=pl.BlockSpec((toks, 2 * half), lambda c: (0, 0)),
         scratch_shapes=[
             pltpu.VMEM((toks, experts * MAIN), BF),
             pltpu.VMEM((2, toks, experts * 2 * REM), BF),
         ],
-        compiler_params=pltpu.CompilerParams(vmem_limit_bytes=24 * MIB),
+        compiler_params=pltpu.CompilerParams(vmem_limit_bytes=32 * MIB),
         cost_estimate=pl.CostEstimate(flops=2 * 1280 * toks * 2 * half, bytes_accessed=6 * MIB, transcendentals=0),
         name="combine",
-    )(ids, ret, summed)
+    )(ids, ret)
 
 
 def place(x, y, core):
@@ -503,7 +513,8 @@
     packed, outgoing = middle(origin, at_row, gs, rows_x, wd, wcat, cs, act, copies)
     summed = lax.psum_scatter(packed, "dp", scatter_dimension=0, tiled=True)[0]
     ret = lax.all_to_all(outgoing, "expert", split_axis=0, concat_axis=0, tiled=True)
-    grad_tokens, grad_g, grad_u, grad_d = combine(ids_t, ret, summed, width // copies, hidden, hidden // copies)
+    grad_tokens = combine(ids_t, ret)
+    grad_g, grad_u, grad_d = unpack(summed, width // copies, hidden, width, hidden // copies)
     return (grad_tokens, grad_g[None], grad_u[None], grad_d[None])
 
 

time: 207 us -> 204 us (0.986)
  local copies, waits for them, and re-layouts: 4.02 us -> 0.62 us
    unnamed x18 -> x14, local copies, waits for them, and re-layouts: 3.43 us -> 0.03 us
  transfers between devices with their start and end apart: 17 -> 17, of which waited for: 6 -> 6; matrix products, arithmetic and copies ran while one was open for 0% -> 0% of each run, Pallas kernels for 6% -> 7%
where the time goes in v8:
time: 204 us; the launch traced here: 203 us
  blocking collectives  62.4 us (31%)
  waiting for transfers between devices  44 us (22%)
  starting transfers between devices  41.1 us (20%)
  Pallas kernels  40.8 us (20%)
  between operations  14.3 us (7%)
    all_to_all x1, blocking collectives, shards(): lax.all_to_all(outgoing, 'expert', split_axis=0, concat_axis=0, tiled=True)  62.4 us
    ppermute x15, starting transfers between devices, moved(): return lax.ppermute(value, 'expert', pairs)  33.6 us
    ppermute x15, waiting for transfers between devices, moved(): return lax.ppermute(value, 'expert', pairs)  25.4 us
    all_to_all x1, waiting for transfers between devices, shards(): lax.all_to_all(out_x, 'expert', split_axis=0, concat_axis=0, axis_index_g...  18.6 us
    pallas_call x1, Pallas kernels, middle(): pl.pallas_call(middle_kernel, out_shape=(pltpu.HBM((copies, length, 128),...  16.5 us
    pallas_call x2, Pallas kernels, dispatch(): pl.pallas_call(functools.partial(dispatch_kernel, scaled, per), out_shape...  10.2 us
    pallas_call x1, Pallas kernels, forward(): pl.pallas_call(forward_kernel, out_shape=(jax.ShapeDtypeStruct((rows, 2 *...  8.17 us
    all_to_all x1, starting transfers between devices, shards(): lax.all_to_all(out_x, 'expert', split_axis=0, concat_axis=0, axis_index_g...  7.54 us
  transfers between devices with their start and end apart: 17, of which 6 were waited for; matrix products, arithmetic and copies ran while one was open for 0% of the time, Pallas kernels for 7%

profile of v8, /device:TPU:1, one launch (start us, length us, event | category | flops | bytes accessed | tf_op | source)
XLA Modules:
  0.0 203.2 jit_solution(8380730113310350637)
XLA Ops:
  7.2 2.1 %prepare.1 = (bf16[128,2176]{1,0:T(8,128)(2,1)}, bf16[128,2176]{1,0:T(8,128)(2,1)}) custom-call(s32[8,128]{1,0:T(8,128)} %bitcast.65, f32[8,128]{1,0:T(8,128)} %bitcast.69, bf16[128,2048]{1,0:T(8,128)(2,1)} %tokens_hbm.1, bf16[128,2048]{1,0:T(8,128)(2,1)} %grads_hbm.1), custom_call_target="tpu_custom_call" | custom-call | flops 1048576 | bytes 2097152 | tf_op jit(solution)/shard_map/prepare/pallas_call | solution.py:97
  9.3 3.4 %collective-permute-start.2 = (bf16[128,2176]{1,0:T(8,128)(2,1)}, bf16[128,2176]{1,0:T(8,128)(2,1)S(1)}, u32[]{:S(2)}, u32[]{:S(2)}) collective-permute-start(bf16[128,2176]{1,0:T(8,128)(2,1)} %get-tuple-element.36.refs_0_), channel_id=1, source_target_pairs={{0,24},{1,25},{2,26},{3,27},{4,28},{5,29},{6,30},{7,31},{8,0},{9,1... | collective-permute-start | bytes 1671176 | tf_op jit(solution)/shard_map/ppermute | solution.py:477
  12.7 0.0 collective-permute-start
  12.7 2.7 %collective-permute-start.6 = (bf16[128,2176]{1,0:T(8,128)(2,1)}, bf16[128,2176]{1,0:T(8,128)(2,1)S(1)}, u32[]{:S(2)}, u32[]{:S(2)}) collective-permute-start(bf16[128,2176]{1,0:T(8,128)(2,1)} %get-tuple-element.42.refs_0_), channel_id=1, source_target_pairs={{0,6},{1,7},{2,0},{3,1},{4,2},{5,3},{6,4},{7,5},{8,14},{9,15},{10,... | collective-permute-start | bytes 1671176 | tf_op jit(solution)/shard_map/ppermute | solution.py:477
  15.4 0.0 collective-permute-start.4
  15.4 8.9 %collective-permute-done.2.refs_4_ = bf16[128,2176]{1,0:T(8,128)(2,1)S(1)} collective-permute-done((bf16[128,2176]{1,0:T(8,128)(2,1)}, bf16[128,2176]{1,0:T(8,128)(2,1)S(1)}, u32[]{:S(2)}, u32[]{:S(2)}) %collective-permute-start.2) | collective-permute-done | bytes 557088 | tf_op jit(solution)/shard_map/ppermute | solution.py:477
  24.3 3.4 %collective-permute-start.3 = (bf16[64,2176]{1,0:T(8,128)(2,1)S(1)}, bf16[64,2176]{1,0:T(8,128)(2,1)}, u32[]{:S(2)}, u32[]{:S(2)}) collective-permute-start(bf16[64,2176]{1,0:T(8,128)(2,1)S(1)} %slice.17), channel_id=1, source_target_pairs={{0,24},{1,25},{2,26},{3,27},{4,28},{5,29},{6,30},{7,31},{8,0},{9,1... | collective-permute-start | bytes 835592 | tf_op jit(solution)/shard_map/ppermute | solution.py:477
  27.7 0.0 collective-permute-done.refs_1_
  27.7 0.1 collective-permute-start.1
  27.8 0.0 collective-permute-done.6.refs_4_
  27.9 2.8 %collective-permute-start.7 = (bf16[64,2176]{1,0:T(8,128)(2,1)S(1)}, bf16[64,2176]{1,0:T(8,128)(2,1)}, u32[]{:S(2)}, u32[]{:S(2)}) collective-permute-start(bf16[64,2176]{1,0:T(8,128)(2,1)S(1)} %slice.19), channel_id=1, source_target_pairs={{0,6},{1,7},{2,0},{3,1},{4,2},{5,3},{6,4},{7,5},{8,14},{9,15},{10,... | collective-permute-start | bytes 835592 | tf_op jit(solution)/shard_map/ppermute | solution.py:477
  30.7 0.0 collective-permute-done.4.refs_1_
  30.7 0.1 collective-permute-start.5
  30.9 0.1 stack.239
  30.9 1.2 collective-permute-done.3.refs_3_
  32.1 3.3 %collective-permute-done.1.refs_2_ = bf16[64,2176]{1,0:T(8,128)(2,1)} collective-permute-done((bf16[64,2176]{1,0:T(8,128)(2,1)S(1)}, bf16[64,2176]{1,0:T(8,128)(2,1)}, u32[]{:S(2)}, u32[]{:S(2)}) %collective-permute-start.1) | collective-permute-done | bytes 278560 | tf_op jit(solution)/shard_map/ppermute | solution.py:477
  35.5 0.0 collective-permute-done.7.refs_3_
  35.5 2.7 %collective-permute-done.5.refs_2_ = bf16[64,2176]{1,0:T(8,128)(2,1)} collective-permute-done((bf16[64,2176]{1,0:T(8,128)(2,1)S(1)}, bf16[64,2176]{1,0:T(8,128)(2,1)}, u32[]{:S(2)}, u32[]{:S(2)}) %collective-permute-start.5) | collective-permute-done | bytes 278560 | tf_op jit(solution)/shard_map/ppermute | solution.py:477
  38.2 0.1 broadcast_in_dim.22.wanted_ref
  38.2 5.0 %dispatch.2 = bf16[8,144,2048]{2,1,0:T(8,128)(2,1)} custom-call(s32[8,128]{1,0:T(8,128)S(1)} %broadcast_in_dim.22.wanted_ref, s32[4]{0:T(128)S(1)} %iota_multiply_fusion.starts_ref, bf16[128,2176]{1,0:T(8,128)(2,1)} %get-tuple-element.36.refs_0_, bf16[128,2176]{1,0:T(8,128)(2,1)} %copy-done.6, bf16[64,2176]{1,0:T(8,128)(2,1)} %collective-permute-done.1.refs_2_, ...), custom_call_target="tpu_custom_call" | custom-call | flops 2415919104 | bytes 7340032 | tf_op jit(solution)/shard_map/dispatch/pallas_call | solution.py:182
  43.2 7.5 %all-to-all-start = ((bf16[8,144,2048]{2,1,0:T(8,128)(2,1)}), bf16[8,144,2048]{2,1,0:T(8,128)(2,1)}, u32[]{:S(2)}, u32[]{:S(2)}) async-start(bf16[8,144,2048]{2,1,0:T(8,128)(2,1)} %dispatch.2), calls=%async_computation | async-start | bytes 9437184 | tf_op jit(solution)/shard_map/all_to_all | solution.py:508
  50.8 0.1 stack.230
  50.9 0.1 broadcast_in_dim.10.wanted_ref
  50.9 5.2 %dispatch.3 = (bf16[144,2048]{1,0:T(8,128)(2,1)}, bf16[144,2048]{1,0:T(8,128)(2,1)}, bf16[144,2048]{1,0:T(8,128)(2,1)}, bf16[144,2048]{1,0:T(8,128)(2,1)}, bf16[...) custom-call(s32[8,128]{1,0:T(8,128)S(1)} %broadcast_in_dim.10.wanted_re, ...), custom_call_target="tpu_custom_call" | custom-call | flops 2415919104 | bytes 7340032 | tf_op jit(solution)/shard_map/dispatch/pallas_call | solution.py:182
  56.1 0.1 collective-permute-start.8
  56.2 2.7 %collective-permute-start.9 = (bf16[144,2048]{1,0:T(8,128)(2,1)}, bf16[144,2048]{1,0:T(8,128)(2,1)S(1)}, u32[]{:S(2)}, u32[]{:S(2)}) collective-permute-start(bf16[144,2048]{1,0:T(8,128)(2,1)} %get-tuple-element.49), channel_id=1, source_target_pairs={{0,24},{1,25},{2,26},{3,27},{4,28},{5,29},{6,30},{7,31},{8,0},{9,1... | collective-permute-start | bytes 1769480 | tf_op jit(solution)/shard_map/ppermute | solution.py:477
  58.9 1.1 collective-permute-start.10
  60.0 1.9 collective-permute-start.11
  61.9 1.1 collective-permute-start.12
  63.0 9.3 %collective-permute-done.8.refs_3_ = bf16[144,2048]{1,0:T(8,128)(2,1)S(1)} collective-permute-done((bf16[144,2048]{1,0:T(8,128)(2,1)}, bf16[144,2048]{1,0:T(8,128)(2,1)S(1)}, u32[]{:S(2)}, u32[]{:S(2)}) %collective-permute-start.8) | collective-permute-done | bytes 589856 | tf_op jit(solution)/shard_map/ppermute | solution.py:477
  72.3 14.3 %collective-permute-start.13 = (bf16[144,2048]{1,0:T(8,128)(2,1)}, bf16[144,2048]{1,0:T(8,128)(2,1)S(1)}, u32[]{:S(2)}, u32[]{:S(2)}) collective-permute-start(bf16[144,2048]{1,0:T(8,128)(2,1)} %get-tuple-element.53), channel_id=1, source_target_pairs={{0,17},{1,16},{2,19},{3,18},{4,21},{5,20},{6,23},{7,22},{8,25},{9,... | collective-permute-start | bytes 1769480 | tf_op jit(solution)/shard_map/ppermute | solution.py:477
  86.5 0.0 collective-permute-done.9.refs_4_
  86.5 0.0 collective-permute-start.14
  86.5 0.1 stack.221.refs_1_
  86.6 0.1 stack.212.refs_0_
  86.7 18.6 %all-to-all-done.refs_0_ = bf16[8,144,2048]{2,1,0:T(8,128)(2,1)} async-done(((bf16[8,144,2048]{2,1,0:T(8,128)(2,1)}), bf16[8,144,2048]{2,1,0:T(8,128)(2,1)}, u32[]{:S(2)}, u32[]{:S(2)}) %all-to-all-start) | async-done | bytes 4718624 | tf_op jit(solution)/shard_map/all_to_all | solution.py:508
  105.3 8.2 %forward.1 = (f32[1152,768]{1,0:T(8,128)S(1)}, bf16[384,1152]{1,0:T(8,128)(2,1)S(1)}, bf16[2048,768]{1,0:T(8,128)(2,1)S(1)}, bf16[1152,2048]{1,0:T(8,128)(2,1)S(1)}) custom-call(bf16[8,144,2048]{2,1,0:T(8,128)(2,1)} %all-to-all-done.refs_0_, bf16[2048,384]{1,0:T(8,128)(2,1)} %bitcast.70, bf16[2048,384]{1,0:T(8,128)(2,1)} %bitcast.71), custom_call_target="tpu_custom_call" | custom-call | flops 3623878656 | bytes 16777216 | tf_op jit(solution)/shard_map/forward/pallas_call | solution.py:248
  113.5 0.0 collective-permute-done.10.refs_5_
  113.5 0.0 collective-permute-done.11.refs_6_
  113.5 0.0 collective-permute-done.12.refs_7_
  113.5 0.0 collective-permute-done.13.refs_8_
  113.5 0.0 collective-permute-done.14.refs_9_
  113.6 16.5 %middle.1 = (bf16[8,2304,128]{2,1,0:T(8,128)(2,1)}, bf16[32,72,1024]{2,1,0:T(8,128)(2,1)}) custom-call(s32[32]{0:T(128)S(1)} %stack.212.refs_0_, s32[8]{0:T(128)S(1)} %stack.221.refs_1_, bf16[144,2048]{1,0:T(8,128)(2,1)S(1)} %copy-done.2, bf16[144,2048]{1,0:T(8,128)(2,1)S(1)} %collective-permute-done.8.refs_3_, ...), custom_call_target="tpu_custom_call" | custom-call | flops 10871635968 | bytes 29360128 | tf_op jit(solution)/shard_map/middle/pallas_call | solution.py:367
  130.1 0.0 reduce-scatter.2.cloned.1.call-update
  130.1 0.0 copy-start
  130.1 62.4 %all_to_all.10.ret_ref = bf16[32,72,1024]{2,1,0:T(8,128)(2,1)S(1)} all-to-all(bf16[32,72,1024]{2,1,0:T(8,128)(2,1)} %get-tuple-element.59), channel_id=1, replica_groups=mesh['dp'=8,'expert'=32] {'expert'}, dimensions={0} | all-to-all | bytes 9437184 | tf_op jit(solution)/shard_map/all_to_all | solution.py:515
  192.5 1.8 combine.1
  194.3 2.0 unpack.1
  (21 shorter events, 0.1 us)
Async XLA Ops:
  9.3 15.0 %collective-permute-start.2 = (bf16[128,2176]{1,0:T(8,128)(2,1)}, bf16[128,2176]{1,0:T(8,128)(2,1)S(1)}, u32[]{:S(2)}, u32[]{:S(2)}) collective-permute-start(bf16[128,2176]{1,0:T(8,128)(2,1)} %get-tuple-element.36.refs_0_), channel_id=1, source_target_pairs={{0,24},{1,25},{2,26},{3,27},{4,28},{5,29},{6,30},{7,31},{8,0},{9,1... | collective-permute-start | bytes 1671176 | tf_op jit(solution)/shard_map/ppermute | solution.py:477
  12.7 15.0 %collective-permute-start = (bf16[128,2176]{1,0:T(8,128)(2,1)}, bf16[128,2176]{1,0:T(8,128)(2,1)S(1)}, u32[]{:S(2)}, u32[]{:S(2)}) collective-permute-start(bf16[128,2176]{1,0:T(8,128)(2,1)} %get-tuple-element.36.refs_0_), channel_id=1, source_target_pairs={{0,8},{1,9},{2,10},{3,11},{4,12},{5,13},{6,14},{7,15},{8,16},{9,17... | collective-permute-start | bytes 1671176 | tf_op jit(solution)/shard_map/ppermute | solution.py:477
  12.7 15.1 %collective-permute-start.6 = (bf16[128,2176]{1,0:T(8,128)(2,1)}, bf16[128,2176]{1,0:T(8,128)(2,1)S(1)}, u32[]{:S(2)}, u32[]{:S(2)}) collective-permute-start(bf16[128,2176]{1,0:T(8,128)(2,1)} %get-tuple-element.42.refs_0_), channel_id=1, source_target_pairs={{0,6},{1,7},{2,0},{3,1},{4,2},{5,3},{6,4},{7,5},{8,14},{9,15},{10,... | collective-permute-start | bytes 1671176 | tf_op jit(solution)/shard_map/ppermute | solution.py:477
  15.4 15.3 %collective-permute-start.4 = (bf16[128,2176]{1,0:T(8,128)(2,1)}, bf16[128,2176]{1,0:T(8,128)(2,1)S(1)}, u32[]{:S(2)}, u32[]{:S(2)}) collective-permute-start(bf16[128,2176]{1,0:T(8,128)(2,1)} %get-tuple-element.42.refs_0_), channel_id=1, source_target_pairs={{0,2},{1,3},{2,4},{3,5},{4,6},{5,7},{6,0},{7,1},{8,10},{9,11},{10,... | collective-permute-start | bytes 1671176 | tf_op jit(solution)/shard_map/ppermute | solution.py:477
  24.3 13.9 %copy-start.5 = (bf16[128,2176]{1,0:T(8,128)(2,1)}, bf16[128,2176]{1,0:T(8,128)(2,1)S(1)}, u32[]{:S(2)}) copy-start(bf16[128,2176]{1,0:T(8,128)(2,1)S(1)} %collective-permute-done.2.refs_4_) | copy-start | bytes 1671172
  24.3 7.8 %collective-permute-start.3 = (bf16[64,2176]{1,0:T(8,128)(2,1)S(1)}, bf16[64,2176]{1,0:T(8,128)(2,1)}, u32[]{:S(2)}, u32[]{:S(2)}) collective-permute-start(bf16[64,2176]{1,0:T(8,128)(2,1)S(1)} %slice.17), channel_id=1, source_target_pairs={{0,24},{1,25},{2,26},{3,27},{4,28},{5,29},{6,30},{7,31},{8,0},{9,1... | collective-permute-start | bytes 835592 | tf_op jit(solution)/shard_map/ppermute | solution.py:477
  27.7 10.5 %copy-start.6 = (bf16[128,2176]{1,0:T(8,128)(2,1)}, bf16[128,2176]{1,0:T(8,128)(2,1)S(1)}, u32[]{:S(2)}) copy-start(bf16[128,2176]{1,0:T(8,128)(2,1)S(1)} %collective-permute-done.refs_1_) | copy-start | bytes 1671172
  27.7 7.7 %collective-permute-start.1 = (bf16[64,2176]{1,0:T(8,128)(2,1)S(1)}, bf16[64,2176]{1,0:T(8,128)(2,1)}, u32[]{:S(2)}, u32[]{:S(2)}) collective-permute-start(bf16[64,2176]{1,0:T(8,128)(2,1)S(1)} %slice.16), channel_id=1, source_target_pairs={{0,8},{1,9},{2,10},{3,11},{4,12},{5,13},{6,14},{7,15},{8,16},{9,17... | collective-permute-start | bytes 835592 | tf_op jit(solution)/shard_map/ppermute | solution.py:477
  27.8 15.4 %copy-start.3 = (bf16[128,2176]{1,0:T(8,128)(2,1)}, bf16[128,2176]{1,0:T(8,128)(2,1)S(1)}, u32[]{:S(2)}) copy-start(bf16[128,2176]{1,0:T(8,128)(2,1)S(1)} %collective-permute-done.6.refs_4_) | copy-start | bytes 1671172
  27.9 7.6 %collective-permute-start.7 = (bf16[64,2176]{1,0:T(8,128)(2,1)S(1)}, bf16[64,2176]{1,0:T(8,128)(2,1)}, u32[]{:S(2)}, u32[]{:S(2)}) collective-permute-start(bf16[64,2176]{1,0:T(8,128)(2,1)S(1)} %slice.19), channel_id=1, source_target_pairs={{0,6},{1,7},{2,0},{3,1},{4,2},{5,3},{6,4},{7,5},{8,14},{9,15},{10,... | collective-permute-start | bytes 835592 | tf_op jit(solution)/shard_map/ppermute | solution.py:477
  30.7 12.5 %copy-start.4 = (bf16[128,2176]{1,0:T(8,128)(2,1)}, bf16[128,2176]{1,0:T(8,128)(2,1)S(1)}, u32[]{:S(2)}) copy-start(bf16[128,2176]{1,0:T(8,128)(2,1)S(1)} %collective-permute-done.4.refs_1_) | copy-start | bytes 1671172
  30.7 7.4 %collective-permute-start.5 = (bf16[64,2176]{1,0:T(8,128)(2,1)S(1)}, bf16[64,2176]{1,0:T(8,128)(2,1)}, u32[]{:S(2)}, u32[]{:S(2)}) collective-permute-start(bf16[64,2176]{1,0:T(8,128)(2,1)S(1)} %slice.18), channel_id=1, source_target_pairs={{0,2},{1,3},{2,4},{3,5},{4,6},{5,7},{6,0},{7,1},{8,10},{9,11},{10,... | collective-permute-start | bytes 835592 | tf_op jit(solution)/shard_map/ppermute | solution.py:477
  43.2 62.1 %all-to-all-start = ((bf16[8,144,2048]{2,1,0:T(8,128)(2,1)}), bf16[8,144,2048]{2,1,0:T(8,128)(2,1)}, u32[]{:S(2)}, u32[]{:S(2)}) async-start(bf16[8,144,2048]{2,1,0:T(8,128)(2,1)} %dispatch.2), calls=%async_computation | async-start | bytes 9437184 | tf_op jit(solution)/shard_map/all_to_all | solution.py:508
  50.8 143.6 %reduce-scatter.2.cloned.1.call-start = ((), (), s32[]{:S(2)}) async-start(), calls=%async_computation.3 | async-start | bytes 5308416 | tf_op jit(solution)/shard_map/reduce_scatter | solution.py:514
  56.1 16.1 %collective-permute-start.8 = (bf16[144,2048]{1,0:T(8,128)(2,1)}, bf16[144,2048]{1,0:T(8,128)(2,1)S(1)}, u32[]{:S(2)}, u32[]{:S(2)}) collective-permute-start(bf16[144,2048]{1,0:T(8,128)(2,1)} %get-tuple-element.48), channel_id=1, source_target_pairs={{0,8},{1,9},{2,10},{3,11},{4,12},{5,13},{6,14},{7,15},{8,16},{9,17... | collective-permute-start | bytes 1769480 | tf_op jit(solution)/shard_map/ppermute | solution.py:477
  56.2 30.3 %collective-permute-start.9 = (bf16[144,2048]{1,0:T(8,128)(2,1)}, bf16[144,2048]{1,0:T(8,128)(2,1)S(1)}, u32[]{:S(2)}, u32[]{:S(2)}) collective-permute-start(bf16[144,2048]{1,0:T(8,128)(2,1)} %get-tuple-element.49), channel_id=1, source_target_pairs={{0,24},{1,25},{2,26},{3,27},{4,28},{5,29},{6,30},{7,31},{8,0},{9,1... | collective-permute-start | bytes 1769480 | tf_op jit(solution)/shard_map/ppermute | solution.py:477
  58.9 54.6 %collective-permute-start.10 = (bf16[144,2048]{1,0:T(8,128)(2,1)}, bf16[144,2048]{1,0:T(8,128)(2,1)S(1)}, u32[]{:S(2)}, u32[]{:S(2)}) collective-permute-start(bf16[144,2048]{1,0:T(8,128)(2,1)} %get-tuple-element.50), channel_id=1, source_target_pairs={{0,16},{1,17},{2,18},{3,19},{4,20},{5,21},{6,22},{7,23},{8,24},{9,... | collective-permute-start | bytes 1769480 | tf_op jit(solution)/shard_map/ppermute | solution.py:477
  60.0 53.5 %collective-permute-start.11 = (bf16[144,2048]{1,0:T(8,128)(2,1)}, bf16[144,2048]{1,0:T(8,128)(2,1)S(1)}, u32[]{:S(2)}, u32[]{:S(2)}) collective-permute-start(bf16[144,2048]{1,0:T(8,128)(2,1)} %get-tuple-element.51), channel_id=1, source_target_pairs={{0,9},{1,8},{2,11},{3,10},{4,13},{5,12},{6,15},{7,14},{8,17},{9,16... | collective-permute-start | bytes 1769480 | tf_op jit(solution)/shard_map/ppermute | solution.py:477
  61.9 51.6 %collective-permute-start.12 = (bf16[144,2048]{1,0:T(8,128)(2,1)}, bf16[144,2048]{1,0:T(8,128)(2,1)S(1)}, u32[]{:S(2)}, u32[]{:S(2)}) collective-permute-start(bf16[144,2048]{1,0:T(8,128)(2,1)} %get-tuple-element.52), channel_id=1, source_target_pairs={{0,25},{1,24},{2,27},{3,26},{4,29},{5,28},{6,31},{7,30},{8,1},{9,0... | collective-permute-start | bytes 1769480 | tf_op jit(solution)/shard_map/ppermute | solution.py:477
  72.3 41.3 %collective-permute-start.13 = (bf16[144,2048]{1,0:T(8,128)(2,1)}, bf16[144,2048]{1,0:T(8,128)(2,1)S(1)}, u32[]{:S(2)}, u32[]{:S(2)}) collective-permute-start(bf16[144,2048]{1,0:T(8,128)(2,1)} %get-tuple-element.53), channel_id=1, source_target_pairs={{0,17},{1,16},{2,19},{3,18},{4,21},{5,20},{6,23},{7,22},{8,25},{9,... | collective-permute-start | bytes 1769480 | tf_op jit(solution)/shard_map/ppermute | solution.py:477
  86.5 27.0 %collective-permute-start.14 = (bf16[144,2048]{1,0:T(8,128)(2,1)}, bf16[144,2048]{1,0:T(8,128)(2,1)}, u32[]{:S(2)}, u32[]{:S(2)}) collective-permute-start(bf16[144,2048]{1,0:T(8,128)(2,1)} %get-tuple-element.54), channel_id=1, source_target_pairs={{0,1},{1,0},{2,3},{3,2},{4,5},{5,4},{6,7},{7,6},{8,9},{9,8},{10,11... | collective-permute-start | bytes 1769480 | tf_op jit(solution)/shard_map/ppermute | solution.py:477
  105.3 8.2 %copy-start.1 = (bf16[1,384,2048]{2,1,0:T(8,128)(2,1)S(1)}, bf16[1,384,2048]{2,1,0:T(8,128)(2,1)}, u32[]{:S(2)}) copy-start(bf16[1,384,2048]{2,1,0:T(8,128)(2,1)} %param.13) | copy-start | bytes 4718596
  105.3 8.2 %copy-start.2 = (bf16[144,2048]{1,0:T(8,128)(2,1)S(1)}, bf16[144,2048]{1,0:T(8,128)(2,1)}, u32[]{:S(2)}) copy-start(bf16[144,2048]{1,0:T(8,128)(2,1)} %get-tuple-element.47.refs_2_) | copy-start | bytes 1769476
  130.1 62.4 %copy-start = (s32[128,8]{0,1:T(8,128)S(1)}, s32[128,8]{0,1:T(8,128)}, u32[]{:S(2)}) copy-start(s32[128,8]{0,1:T(8,128)} %param.10) | copy-start | bytes 12292
Sparse Core Ops, SparseCore 0:
  130.2 61.2 reduce-scatter.1
